TPU v7x, 32 devices: a whole 2x2x4 slice. The times are simulated.
32 devices in a mesh: expert: 16 (over z, x, core), hidden: 2 (over y).
Axes of the slice: x: 2, y: 2, z: 4, core: 2. Of those that a mesh axis runs over, the one named last changes fastest.
Arguments:
- swap_pairs: int32 [8, 2], replicated, may hold values from 0 to 15, as said below
- expert_ids: int32 [2048, 2], P('expert'), may hold values from 0 to 15, all different within a row; in each aligned block of 128 rows (0 to 127, 128 to 255, ...) at most 32 rows name the same one
- route_weights: float32 [2048, 2], P('expert'), may hold values from 0.05 to 0.6
- gate_up: bfloat16 [2048, 2, 2, 256], P('expert', None, None, 'hidden'), may hold values from -6 to 6
- grad_out: bfloat16 [2048, 3584], P('expert', 'hidden'), may hold values from -6 to 6
- down_weight: bfloat16 [16, 256, 3584], P('expert', 'hidden'), may hold values from -0.375 to 0.375
- first_moment: bfloat16 [16, 256, 3584], P('expert', 'hidden'), may hold values from -4 to 4
- second_moment: bfloat16 [16, 256, 3584], P('expert', 'hidden'), may hold values from 0.049804688 to 1
Outputs:
- combined: bfloat16 [2048, 3584], P('expert', 'hidden')
- grad_gate_up: bfloat16 [2048, 2, 2, 256], P('expert', None, None, 'hidden')
- adam_step: bfloat16 [16, 256, 3584], P('expert', 'hidden')
Inputs may be any that keep to these rules, and one draw needn't show every extreme that they name: `swap_pairs`: every place 0 .. 15 appears exactly once in the list. `expert_ids`: A row's 2 experts are distinct; in each aligned block of 128 rows (the rows of one device) no expert is named more than 32 times, a bound that some block reaches.
All inputs are finite; a program needn't handle non-finite values.
Results may differ from a plain program's by a relative error of at most 0.017.
Values may be sent and summed in bfloat16 or wider, within the bound.
No kernel may reach another device: no remote copies, remote signals or barrier semaphores. Data moves between devices by JAX's collectives and lax.ppermute only.
A program may use at most 128 MiB of HBM per device.

v0:
```python
import functools
import jax
import jax.numpy as jnp
from jax import lax
from jax.experimental import pallas as pl
from jax.experimental.pallas import tpu as pltpu
from jax.sharding import PartitionSpec as P

first_decay = 0.9
second_decay = 0.95
adam_epsilon = 1e-08


def partner_table(swap_pairs, places):
    column = jnp.arange(places, dtype=jnp.int32)
    left = swap_pairs[:, 0]
    right = swap_pairs[:, 1]
    moved = jnp.where(left[:, None] == column[None, :], right[:, None] - column[None, :], 0)
    moved = moved + jnp.where(right[:, None] == column[None, :], left[:, None] - column[None, :], 0)
    return column + jnp.sum(moved, axis=0)


def relocate_state(weight_here, first_here, second_here, partner):
    places = partner.shape[0]
    shape_here = weight_here.shape
    spread = (
        lax.all_to_all(
            weight_here.reshape(places, -1), "expert", split_axis=0, concat_axis=0, tiled=True
        ),
        lax.all_to_all(
            first_here.reshape(places, -1), "expert", split_axis=0, concat_axis=0, tiled=True
        ),
        lax.all_to_all(
            second_here.reshape(places, -1), "expert", split_axis=0, concat_axis=0, tiled=True
        ),
    )
    ordered = tuple((jnp.take(member, partner, axis=0) for member in spread))
    collected = (
        lax.all_to_all(ordered[0], "expert", split_axis=0, concat_axis=0, tiled=True),
        lax.all_to_all(ordered[1], "expert", split_axis=0, concat_axis=0, tiled=True),
        lax.all_to_all(ordered[2], "expert", split_axis=0, concat_axis=0, tiled=True),
    )
    return tuple((member.reshape(shape_here) for member in collected))


def slot_numbers(destination, places, capacity):
    column = jnp.arange(places, dtype=jnp.int32)
    one_hot = (destination[:, None] == column[None, :]).astype(jnp.int32)
    before = jnp.cumsum(one_hot, axis=0) - one_hot
    earlier_count = jnp.sum(before * one_hot, axis=1)
    return destination * capacity + earlier_count


def general_local(
    swap_pairs,
    expert_ids,
    route_weights,
    gate_up,
    grad_out,
    down_weight,
    first_moment,
    second_moment,
):
    places = lax.axis_size("expert")
    tok_count, top_count = expert_ids.shape
    hid_dev = down_weight.shape[1]
    capacity = 2 * tok_count * top_count // places
    total_slots = places * capacity
    choice_count = tok_count * top_count
    partner = partner_table(swap_pairs, places)
    weight_here = down_weight[0]
    first_here = first_moment[0]
    second_here = second_moment[0]
    flat_ids = expert_ids.reshape(-1)
    column = jnp.arange(places, dtype=jnp.int32)
    weight_here, first_here, second_here = relocate_state(
        weight_here, first_here, second_here, partner
    )
    destination = jnp.sum(
        jnp.where(flat_ids[:, None] == column[None, :], partner[None, :], 0), axis=1
    )
    slot_index = slot_numbers(destination, places, capacity)
    choice_acts = gate_up.reshape(choice_count, 2 * hid_dev)
    scaled = (route_weights[:, :, None] * grad_out[:, None, :].astype(jnp.float32)).astype(
        jnp.bfloat16
    )
    scaled = scaled.reshape(choice_count, grad_out.shape[1])
    send_acts = jnp.zeros((total_slots, 2 * hid_dev), jnp.bfloat16).at[slot_index].set(choice_acts)
    send_grads = (
        jnp.zeros((total_slots, grad_out.shape[1]), jnp.bfloat16).at[slot_index].set(scaled)
    )
    recv_acts, recv_grads = (
        lax.all_to_all(
            send_acts.reshape(places, capacity, 2 * hid_dev),
            "expert",
            split_axis=0,
            concat_axis=0,
            tiled=True,
        ),
        lax.all_to_all(
            send_grads.reshape(places, capacity, grad_out.shape[1]),
            "expert",
            split_axis=0,
            concat_axis=0,
            tiled=True,
        ),
    )
    recv_acts = recv_acts.reshape(total_slots, 2 * hid_dev)
    recv_grads = recv_grads.reshape(total_slots, grad_out.shape[1])
    gate_pre = recv_acts[:, :hid_dev].astype(jnp.float32)
    up_pre = recv_acts[:, hid_dev:].astype(jnp.float32)
    sigmoid_gate = jax.nn.sigmoid(gate_pre)
    silu_gate = gate_pre * sigmoid_gate
    hidden = (silu_gate * up_pre).astype(jnp.bfloat16)
    partial_value = jnp.dot(hidden, weight_here, preferred_element_type=jnp.float32)
    summed = lax.psum_scatter(
        partial_value.astype(jnp.bfloat16), "hidden", scatter_dimension=1, tiled=True
    ).astype(jnp.float32)
    returned = lax.all_to_all(
        summed.reshape(places, capacity, summed.shape[1]).astype(jnp.bfloat16),
        "expert",
        split_axis=0,
        concat_axis=0,
        tiled=True,
    ).astype(jnp.float32)
    per_choice = jnp.take(returned.reshape(total_slots, summed.shape[1]), slot_index, axis=0)
    per_choice = per_choice.reshape(tok_count, top_count, summed.shape[1])
    combined = jnp.einsum("tk,tkd->td", route_weights, per_choice).astype(jnp.bfloat16)
    portion = lax.all_gather(recv_grads, "hidden", axis=1, tiled=True)
    grad_hidden = lax.dot_general(
        portion, weight_here, (((1,), (1,)), ((), ())), preferred_element_type=jnp.float32
    )
    product_block = lax.dot_general(
        hidden, portion, (((0,), (0,)), ((), ())), preferred_element_type=jnp.float32
    )
    grad_weight = product_block
    grad_hidden, grad_weight = (grad_hidden, grad_weight)
    grad_gate = grad_hidden * up_pre * sigmoid_gate * (1.0 + gate_pre * (1.0 - sigmoid_gate))
    grad_up = grad_hidden * silu_gate
    grad_rows = jnp.concatenate([grad_gate, grad_up], axis=1).astype(jnp.bfloat16)
    returned_grads = lax.all_to_all(
        grad_rows.reshape(places, capacity, 2 * hid_dev),
        "expert",
        split_axis=0,
        concat_axis=0,
        tiled=True,
    )
    grad_gate_up = jnp.take(returned_grads.reshape(total_slots, 2 * hid_dev), slot_index, axis=0)
    grad_gate_up = grad_gate_up.reshape(tok_count, top_count, 2, hid_dev)
    first_new = first_decay * first_here.astype(jnp.float32) + (1.0 - first_decay) * grad_weight
    second_new = (
        second_decay * second_here.astype(jnp.float32)
        + (1.0 - second_decay) * grad_weight * grad_weight
    )
    update = (first_new / (jnp.sqrt(second_new) + adam_epsilon)).astype(jnp.bfloat16)
    return (combined, grad_gate_up, update[None])


bf16 = jnp.bfloat16
f32 = jnp.float32
KERNEL_PARAMS = pltpu.CompilerParams(vmem_limit_bytes=40 * 1024 * 1024)


def whole_call(body, out_shape, name):
    return pl.pallas_call(body, out_shape=out_shape, name=name, compiler_params=KERNEL_PARAMS)


def level_and_side(half):
    return lax.axis_index("expert") // half, lax.axis_index("hidden")


def columns_at(ref, index, wide):
    return ref[:, pl.ds(pl.multiple_of(index * wide, wide), wide)]


def same_index(size):
    first = lax.broadcasted_iota(jnp.int32, (size, size), 0)
    second = lax.broadcasted_iota(jnp.int32, (size, size), 1)
    return first == second


def prepare_body(acts_ref, ids_ref, weights_ref, hidden_ref, far_ref):
    tok = acts_ref.shape[0]
    units = acts_ref.shape[1] // 4
    for choice in range(2):
        at = 2 * choice * units
        gate = acts_ref[:, at : at + units].astype(f32)
        up = acts_ref[:, at + units : at + 2 * units].astype(f32)
        value = (gate * jax.nn.sigmoid(gate) * up).astype(bf16)
        hidden_ref[choice * tok : (choice + 1) * tok, :] = value
        far_ref[choice * tok : (choice + 1) * tok, :] = value
    weights = weights_ref[...]
    high = weights.astype(bf16)
    middle = (weights - high.astype(f32)).astype(bf16)
    low = (weights - high.astype(f32) - middle.astype(f32)).astype(bf16)
    unit = same_index(tok).astype(f32).astype(bf16)
    pieces = [
        lax.dot_general(piece, unit, (((0,), (0,)), ((), ())), preferred_element_type=f32)
        for piece in (ids_ref[...].astype(f32).astype(bf16), high, middle, low)
    ]
    blank = jnp.zeros((16 - 8, tok), f32)
    far_ref[2 * tok : 2 * tok + 16, :] = jnp.concatenate(pieces + [blank], axis=0).astype(bf16)


def split_body(*refs):
    out_ref = refs[-1]
    side = lax.axis_index("hidden")
    for k, ref in enumerate(refs[:-1]):
        out_ref[k] = columns_at(ref, 1 - side, ref.shape[1] // 2)


def read_meta(ref):
    tok = ref.shape[1]
    meta = ref[2 * tok : 2 * tok + 16, :].astype(f32)
    ids = jnp.concatenate([meta[0:1, :], meta[1:2, :]], axis=1)
    weights = [
        meta[2 + k : 3 + k, :] + meta[4 + k : 5 + k, :] + meta[6 + k : 7 + k, :] for k in range(2)
    ]
    return ids, weights


def slot_choice(bin_of, bins, cap):
    count = bin_of.shape[1]
    column = lax.broadcasted_iota(jnp.int32, (bins, count), 0).astype(f32)
    one_hot = (bin_of == column).astype(f32)
    first = lax.broadcasted_iota(jnp.int32, (count, count), 0)
    second = lax.broadcasted_iota(jnp.int32, (count, count), 1)
    earlier = (first < second).astype(f32).astype(bf16)
    rank = jnp.dot(one_hot.astype(bf16), earlier, preferred_element_type=f32)
    slot = jnp.sum(one_hot * (rank + column * cap + 1.0), axis=0, keepdims=True) - 1.0
    return slot == lax.broadcasted_iota(jnp.int32, (bins * cap, count), 0).astype(f32)


def pack_body(half, acts_ref, beside_ref, *refs):
    out_ref = refs[-1]
    bins, cap, _ = out_ref.shape
    units = beside_ref.shape[1]
    grads = jnp.concatenate([ref[...] for ref in refs[:-1]], axis=0)
    tok, wide = grads.shape
    level, _ = level_and_side(half)
    ids, weights = read_meta(acts_ref)
    chosen = slot_choice(ids - (half * level).astype(f32), bins, cap)
    weights = jnp.concatenate(weights, axis=1)
    factor = jnp.sum(jnp.where(chosen, weights, 0.0), axis=1, keepdims=True)
    one_hot = chosen.astype(f32)
    by_token = (one_hot[:, :tok] + one_hot[:, tok:]).astype(bf16)
    rows = jnp.dot(by_token, grads, preferred_element_type=f32)
    out_ref[:, :, 0:wide] = (rows * factor).astype(bf16).reshape(bins, cap, wide)
    for side, ref in enumerate((acts_ref, beside_ref)):
        at = wide + side * units
        acts = jnp.dot(
            one_hot.astype(bf16), ref[0 : 2 * tok, :], preferred_element_type=f32
        )
        out_ref[:, :, at : at + units] = acts.astype(bf16).reshape(bins, cap, units)


def rows_of(ref, start, size):
    sources, cap, _ = ref.shape
    return ref[:, :, start : start + size].reshape(sources * cap, size)


def forward_body(recv_ref, far_ref, weight_ref, beside_ref, out_ref):
    sources, _, cap, wide = out_ref.shape
    units = weight_ref.shape[0]
    weights = (columns_at(weight_ref, lax.axis_index("hidden"), wide), beside_ref[0])
    for block, ref in enumerate((recv_ref, far_ref)):
        total = None
        for side, weight in enumerate(weights):
            acts = rows_of(ref, wide + side * units, units)
            part = jnp.dot(acts, weight, preferred_element_type=f32)
            total = part if total is None else total + part
        out_ref[:, block] = total.astype(bf16).reshape(sources, cap, wide)


def grad_hidden_body(recv_ref, far_ref, weight_ref, beside_ref, keep_ref, send_ref):
    _, sources, cap, units = send_ref.shape
    wide = beside_ref.shape[2]
    own = columns_at(weight_ref, lax.axis_index("hidden"), wide)
    for block, ref in enumerate((recv_ref, far_ref)):
        scaled = rows_of(ref, 0, wide)
        for weight, out_ref in ((own, keep_ref), (beside_ref[0], send_ref)):
            part = lax.dot_general(
                scaled, weight, (((1,), (1,)), ((), ())), preferred_element_type=f32
            )
            out_ref[block] = part.astype(out_ref.dtype).reshape(sources, cap, units)


def add_sides_body(keep_ref, got_ref, own_ref, far_ref):
    own_ref[...] = (keep_ref[0] + got_ref[0].astype(f32)).astype(bf16)
    far_ref[...] = (keep_ref[1] + got_ref[1].astype(f32)).astype(bf16)


def update_body(half, recv_ref, far_ref, first_ref, second_ref, *refs):
    keep_ref, send_ref = refs[-2:]
    _, units, wide = refs[0].shape
    level, here = level_and_side(half)
    narrow = wide // 2
    for side in range(2):
        for part, out_ref in ((level, keep_ref), (1 - level, send_ref)):
            columns = pl.ds(pl.multiple_of(part * narrow, narrow), narrow)
            if side == 0:
                moments = [
                    columns_at(ref, 2 * here + part, narrow) for ref in (first_ref, second_ref)
                ]
            else:
                moments = [ref[0, :, columns] for ref in refs[:-2]]
            grad = None
            for ref in (recv_ref, far_ref):
                sources, cap, _ = ref.shape
                more = lax.dot_general(
                    rows_of(ref, wide + side * units, units),
                    ref[:, :, columns].reshape(sources * cap, narrow),
                    (((0,), (0,)), ((), ())),
                    preferred_element_type=f32,
                )
                grad = more if grad is None else grad + more
            first = first_decay * moments[0].astype(f32) + (1.0 - first_decay) * grad
            second = second_decay * moments[1].astype(f32)
            second = second + (1.0 - second_decay) * grad * grad
            out_ref[side] = (first / (jnp.sqrt(second) + adam_epsilon)).astype(bf16)


def stack_body(step_ref, far_step_ref, rows_ref, far_rows_ref, out_ref):
    sources = out_ref.shape[0]
    _, units, narrow = step_ref.shape
    cap = rows_ref.shape[1]
    each = units // sources
    for expert, (steps, rows) in enumerate(((step_ref, rows_ref), (far_step_ref, far_rows_ref))):
        for side in range(2):
            at = (2 * expert + side) * each
            out_ref[:, at : at + each, 0:narrow] = steps[side].reshape(sources, each, narrow)
        out_ref[:, expert * cap : (expert + 1) * cap, narrow:] = rows[...]


def combine_body(half, acts_ref, far_acts_ref, back_ref, own_ref, far_ref):
    bins, _, cap, wide = back_ref.shape
    tok = own_ref.shape[0]
    level, _ = level_and_side(half)
    diagonal = same_index(tok)
    for block, (ref, out_ref) in enumerate(((acts_ref, own_ref), (far_acts_ref, far_ref))):
        ids, weights = read_meta(ref)
        chosen = slot_choice(ids - (half * level).astype(f32), bins, cap)
        chosen = chosen.astype(f32).astype(bf16)
        rows = back_ref[:, block].reshape(bins * cap, wide)
        total = None
        for choice in range(2):
            picked = lax.dot_general(
                chosen[:, choice * tok : (choice + 1) * tok],
                rows,
                (((0,), (0,)), ((), ())),
                preferred_element_type=f32,
            )
            upright = jnp.sum(
                jnp.where(diagonal, weights[choice], 0.0), axis=1, keepdims=True
            )
            part = upright * picked
            total = part if total is None else total + part
        out_ref[...] = total.astype(out_ref.dtype)


def add_halves_body(own_ref, far_ref, out_ref):
    out_ref[...] = (own_ref[...] + far_ref[...].astype(f32)).astype(bf16)


def gate_grads_body(half, far_acts_ref, acts_ref, recv_ref, out_ref):
    sources, rows, total_wide = recv_ref.shape
    tok = acts_ref.shape[0]
    units = acts_ref.shape[1] // 4
    level, _ = level_and_side(half)
    ids, _ = read_meta(far_acts_ref)
    upper = (ids >= half).astype(f32)
    bin_of = (ids - half * upper) * 2 + jnp.abs(upper - level.astype(f32))
    chosen = slot_choice(bin_of, 2 * sources, rows // 2).astype(f32).astype(bf16)
    table = recv_ref[:, :, total_wide - units :].reshape(sources * rows, units)
    for choice in range(2):
        at = 2 * choice * units
        gate = acts_ref[:, at : at + units].astype(f32)
        up = acts_ref[:, at + units : at + 2 * units].astype(f32)
        grad = lax.dot_general(
            chosen[:, choice * tok : (choice + 1) * tok],
            table,
            (((0,), (0,)), ((), ())),
            preferred_element_type=f32,
        )
        sigmoid = jax.nn.sigmoid(gate)
        out_ref[:, at : at + units] = (
            grad * up * sigmoid * (1.0 + gate * (1.0 - sigmoid))
        ).astype(bf16)
        out_ref[:, at + units : at + 2 * units] = (grad * (gate * sigmoid)).astype(bf16)


def route_steps_body(source_ref, line_ref, recv_ref, out_ref):
    count, each, wide = out_ref.shape
    for k in range(count):
        line = pl.multiple_of(line_ref[k] * each, each)
        out_ref[k] = recv_ref[source_ref[k], pl.ds(line, each), 0:wide]


def place_steps_body(recv_ref, out_ref):
    halves, sources, sides, each, wide = recv_ref.shape
    for half in range(halves):
        for source in range(sources):
            for side in range(sides):
                at = (side * halves + half) * wide
                out_ref[source * each : (source + 1) * each, at : at + wide] = recv_ref[
                    half, source, side
                ]


def after(x, *others):
    return lax.optimization_barrier((x, *others))[0]


def mirrored_local(
    swap_pairs,
    expert_ids,
    route_weights,
    gate_up,
    grad_out,
    down_weight,
    first_moment,
    second_moment,
):
    places = lax.axis_size("expert")
    half = places // 2
    level, side = level_and_side(half)
    tok, top = expert_ids.shape
    units = down_weight.shape[1]
    wide = grad_out.shape[1]
    narrow = wide // 2
    cap = 2 * tok * top // places
    each = units // half
    across = [(k, (k + half) % places) for k in range(places)]
    beside = [(0, 1), (1, 0)]
    diagonal = [
        (2 * k + a, 2 * ((k + half) % places) + 1 - a) for k in range(places) for a in range(2)
    ]
    groups = [list(range(half)), list(range(half, places))]

    def mirror(x):
        return lax.ppermute(x, "expert", across)

    def neighbour(x):
        return lax.ppermute(x, "hidden", beside)

    def exchange(x):
        return lax.all_to_all(
            x, "expert", split_axis=0, concat_axis=0, tiled=True, axis_index_groups=groups
        )

    def shaped(*shape, dtype=bf16):
        return jax.ShapeDtypeStruct(shape, dtype)

    grads_far = [mirror(grad_out[: tok // 2]), mirror(grad_out[tok // 2 :])]
    acts = gate_up.reshape(tok, 4 * units)
    hidden, noted = whole_call(
        prepare_body, (shaped(top * tok, units), shaped(top * tok + 16, units)), "prepare"
    )(acts, expert_ids, route_weights)
    noted_far = mirror(noted)
    hidden_beside = neighbour(hidden)
    hidden_diagonal = lax.ppermute(hidden, ("expert", "hidden"), diagonal)

    state = (down_weight[0], first_moment[0], second_moment[0])
    split = whole_call(split_body, shaped(1, units, wide), "split_state")
    weight_beside = neighbour(split(state[0]))
    first_beside = neighbour(split(after(state[1], hidden)))
    second_beside = neighbour(split(after(state[2], hidden)))

    row = wide + 2 * units
    pack = functools.partial(
        whole_call, functools.partial(pack_body, half), shaped(half, cap, row)
    )
    packed = pack("pack_own")(noted, hidden_beside, grad_out)
    recv = exchange(after(packed, grads_far[0], weight_beside))
    packed_far = pack("pack_far")(noted_far, hidden_diagonal, *grads_far)
    recv_far = exchange(after(packed_far, recv, first_beside))
    recv_far = after(recv_far, second_beside)

    outputs = whole_call(forward_body, shaped(half, 2, cap, wide), "forward")(
        recv, recv_far, state[0], weight_beside
    )
    back = exchange(outputs.reshape(half, 2 * cap, wide)).reshape(half, 2, cap, wide)

    grad_keep, grad_send = whole_call(
        grad_hidden_body,
        (shaped(2, half, cap, units, dtype=f32), shaped(2, half, cap, units)),
        "grad_hidden",
    )(recv, recv_far, state[0], weight_beside)
    step, step_send = whole_call(
        functools.partial(update_body, half),
        (shaped(2, units, narrow), shaped(2, units, narrow)),
        "update",
    )(recv, recv_far, *state[1:], first_beside, second_beside)
    step_far = mirror(step_send)
    rows_own, rows_send = whole_call(
        add_sides_body, (shaped(half, cap, units), shaped(half, cap, units)), "add_sides"
    )(grad_keep, neighbour(grad_send))
    rows_far = mirror(rows_send)
    stacked = whole_call(stack_body, shaped(half, 2 * cap, narrow + units), "stack_steps")(
        step, step_far, rows_own, rows_far
    )
    combined_own, combined_send = whole_call(
        functools.partial(combine_body, half),
        (shaped(tok, wide, dtype=f32), shaped(tok, wide)),
        "combine",
    )(noted, noted_far, back)
    combined_far = mirror(combined_send)
    combined = whole_call(add_halves_body, shaped(tok, wide), "add_halves")(
        combined_own, combined_far
    )

    spread = exchange(after(stacked, back))

    partner = partner_table(swap_pairs, places)
    from_source = jnp.repeat(partner % half, 2)
    sides = jnp.tile(jnp.arange(2, dtype=jnp.int32), places)
    from_line = jnp.repeat((partner // half) ^ level, 2) * 2 + (sides ^ side)
    smem = pl.BlockSpec(memory_space=pltpu.SMEM)
    vmem = pl.BlockSpec(memory_space=pltpu.VMEM)
    routed = pl.pallas_call(
        route_steps_body,
        in_specs=[smem, smem, vmem],
        out_specs=vmem,
        out_shape=shaped(2 * places, each, narrow),
        name="route_steps",
        compiler_params=KERNEL_PARAMS,
    )(from_source.astype(jnp.int32), from_line.astype(jnp.int32), spread)
    placed = lax.all_to_all(
        after(routed, combined_far), ("expert", "hidden"), split_axis=0, concat_axis=0, tiled=True
    )

    grad_gate_up = whole_call(
        functools.partial(gate_grads_body, half), shaped(tok, 4 * units), "gate_grads"
    )(noted, acts, spread).reshape(gate_up.shape)
    adam_step = whole_call(place_steps_body, shaped(units, 2 * wide), "place_steps")(
        placed.reshape(2, half, 2, each, narrow)
    )
    return combined, grad_gate_up, adam_step[None]


def chosen_local(places, sides, *arrays):
    tok, top = arrays[1].shape
    units = arrays[5].shape[1]
    wide = arrays[4].shape[1]
    cap = 2 * tok * top // places
    fits = sides == 2 and top == 2 and places % 4 == 0 and places <= 256
    fits = fits and places * cap == 2 * tok * top and cap % 16 == 0
    fits = fits and wide % 256 == 0 and units == tok and tok % 128 == 0
    fits = fits and units % (8 * places) == 0 and 2 * cap == 4 * (units // (places // 2))
    return mirrored_local(*arrays) if fits else general_local(*arrays)


def solution(mesh):
    placed = (
        P(),
        P("expert", None),
        P("expert", None),
        P("expert", None, None, "hidden"),
        P("expert", "hidden"),
        P("expert", "hidden", None),
        P("expert", "hidden", None),
        P("expert", "hidden", None),
    )
    return jax.shard_map(
        functools.partial(chosen_local, mesh.shape["expert"], mesh.shape["hidden"]),
        mesh=mesh,
        in_specs=placed,
        out_specs=(
            P("expert", "hidden"),
            P("expert", None, None, "hidden"),
            P("expert", "hidden", None),
        ),
        check_vma=False,
    )
```

profile of v0, /device:TPU:0, one launch (start us, length us, event | category | flops | bytes accessed | tf_op | source)
XLA Modules:
  0.0 168.8 jit_solution(8283139504095418376)
XLA Ops:
  0.7 1.2 copy-done
  1.9 3.0 %collective-permute-start.3 = (bf16[1,128,1792]{2,1,0:T(8,128)(2,1)S(1)}, bf16[1,128,1792]{2,1,0:T(8,128)(2,1)S(1)}, u32[]{:S(2)}, u32[]{:S(2)}) collective-permute-start(bf16[1,128,1792]{2,1,0:T(8,128)(2,1)S(1)} %split_state.3), channel_id=1, source_target_pairs={{0,1},{1,0},{2,3},{3,2},{4,5},{5,4},{6,7},{7,6},{8,9},{9,8},{10,11... | collective-permute-start | bytes 1376264 | tf_op jit(solution)/shard_map/ppermute | solution.py:444
  6.0 2.7 %collective-permute-start.2 = (bf16[64,1792]{1,0:T(8,128)(2,1)S(1)}, bf16[64,1792]{1,0:T(8,128)(2,1)S(1)}, u32[]{:S(2)}, u32[]{:S(2)}) collective-permute-start(bf16[64,1792]{1,0:T(8,128)(2,1)S(1)} %get-tuple-element.38), channel_id=1, source_target_pairs={{0,16},{2,18},{4,20},{6,22},{8,24},{10,26},{12,28},{14,30},{16,0},... | collective-permute-start | bytes 688136 | tf_op jit(solution)/shard_map/ppermute | solution.py:441
  9.7 7.1 %collective-permute-done.1.beside_ref = bf16[256,128]{1,0:T(8,128)(2,1)S(1)} collective-permute-done((bf16[256,128]{1,0:T(8,128)(2,1)S(1)}, bf16[256,128]{1,0:T(8,128)(2,1)S(1)}, u32[]{:S(2)}, u32[]{:S(2)}) %collective-permute-start.1) | collective-permute-done | bytes 65568 | tf_op jit(solution)/shard_map/ppermute | solution.py:444
  16.8 1.6 pack_own.1
  18.9 3.6 %all-to-all-start = ((bf16[8,32,2048]{2,1,0:T(8,128)(2,1)}), bf16[8,32,2048]{2,1,0:T(8,128)(2,1)S(1)}, u32[]{:S(2)}, u32[]{:S(2)}) async-start(bf16[8,32,2048]{2,1,0:T(8,128)(2,1)} %pack_own.1), calls=%async_computation | async-start | bytes 2097152 | tf_op jit(solution)/shard_map/all_to_all | solution.py:447
  22.6 1.6 collective-permute-start.6
  24.2 2.6 %collective-permute-start.5 = (bf16[64,1792]{1,0:T(8,128)(2,1)S(1)}, bf16[64,1792]{1,0:T(8,128)(2,1)S(1)}, u32[]{:S(2)}, u32[]{:S(2)}) collective-permute-start(bf16[64,1792]{1,0:T(8,128)(2,1)S(1)} %get-tuple-element.37), channel_id=1, source_target_pairs={{0,16},{2,18},{4,20},{6,22},{8,24},{10,26},{12,28},{14,30},{16,0},... | collective-permute-start | bytes 688136 | tf_op jit(solution)/shard_map/ppermute | solution.py:441
  27.1 2.6 %collective-permute-start.4 = (bf16[256,128]{1,0:T(8,128)(2,1)S(1)}, bf16[256,128]{1,0:T(8,128)(2,1)S(1)}, u32[]{:S(2)}, u32[]{:S(2)}) collective-permute-start(bf16[256,128]{1,0:T(8,128)(2,1)S(1)} %get-tuple-element.21), channel_id=1, source_target_pairs={{0,17},{1,16},{2,19},{3,18},{4,21},{5,20},{6,23},{7,22},{8,25},{9,... | collective-permute-start | bytes 196616 | tf_op jit(solution)/shard_map/ppermute | solution.py:461
  29.7 13.0 %collective-permute-done.4.beside_ref = bf16[256,128]{1,0:T(8,128)(2,1)S(1)} collective-permute-done((bf16[256,128]{1,0:T(8,128)(2,1)S(1)}, bf16[256,128]{1,0:T(8,128)(2,1)S(1)}, u32[]{:S(2)}, u32[]{:S(2)}) %collective-permute-start.4) | collective-permute-done | bytes 65568 | tf_op jit(solution)/shard_map/ppermute | solution.py:461
  46.2 7.8 %all-to-all-start.1 = ((bf16[8,32,2048]{2,1,0:T(8,128)(2,1)}), bf16[8,32,2048]{2,1,0:T(8,128)(2,1)S(1)}, u32[]{:S(2)}, u32[]{:S(2)}) async-start(bf16[8,32,2048]{2,1,0:T(8,128)(2,1)} %copy-done.3), calls=%async_computation.1 | async-start | bytes 2097152 | tf_op jit(solution)/shard_map/all_to_all | solution.py:447
  53.9 1.2 copy-done.6
  55.8 12.3 %collective-permute-done.7.refs_1_ = bf16[1,128,1792]{2,1,0:T(8,128)(2,1)S(1)} collective-permute-done((bf16[1,128,1792]{2,1,0:T(8,128)(2,1)S(1)}, bf16[1,128,1792]{2,1,0:T(8,128)(2,1)S(1)}, u32[]{:S(2)}, u32[]{:S(2)}) %collective-permute-start.7) | collective-permute-done | bytes 458784 | tf_op jit(solution)/shard_map/ppermute | solution.py:444
  68.9 1.1 forward.1
  70.0 1.2 copy-done.2
  71.2 4.3 %all-to-all-start.2 = ((bf16[8,64,1792]{2,1,0:T(8,128)(2,1)}), bf16[8,64,1792]{2,1,0:T(8,128)(2,1)}, u32[]{:S(2)}, u32[]{:S(2)}) async-start(bf16[8,64,1792]{2,1,0:T(8,128)(2,1)} %bitcast.14), calls=%async_computation.2 | async-start | bytes 3670016 | tf_op jit(solution)/shard_map/all_to_all | solution.py:447
  75.6 1.2 copy-done.5
  76.8 1.2 copy-done.7
  80.0 1.7 %update.1 = (bf16[2,128,896]{2,1,0:T(8,128)(2,1)S(1)}, bf16[2,128,896]{2,1,0:T(8,128)(2,1)S(1)}) custom-call(bf16[8,32,2048]{2,1,0:T(8,128)(2,1)S(1)} %all-to-all-done.recv_ref, bf16[8,32,2048]{2,1,0:T(8,128)(2,1)S(1)} %all-to-all-done.1.far_ref, bf16[128,3584]{1,0:T(8,128)(2,1)S(1)} %bitcast.16, bf16[128,3584]{1,0:T(8,128)(2,1)S(1)} %bitcast.18, ...), custom_call_target="tpu_custom_call" | custom-call | tf_op jit(solution)/shard_map/update/pallas_call | solution.py:489
  81.8 1.1 grad_hidden.1
  83.6 5.1 %collective-permute-done.10.got_ref = bf16[2,8,32,128]{3,2,1,0:T(8,128)(2,1)S(1)} collective-permute-done((bf16[2,8,32,128]{3,2,1,0:T(8,128)(2,1)S(1)}, bf16[2,8,32,128]{3,2,1,0:T(8,128)(2,1)S(1)}, u32[]{:S(2)}, u32[]{:S(2)}) %collective-permute-start.10) | collective-permute-done | bytes 131104 | tf_op jit(solution)/shard_map/ppermute | solution.py:444
  88.8 2.7 %collective-permute-start.11 = (bf16[8,32,128]{2,1,0:T(8,128)(2,1)S(1)}, bf16[8,32,128]{2,1,0:T(8,128)(2,1)S(1)}, u32[]{:S(2)}, u32[]{:S(2)}) collective-permute-start(bf16[8,32,128]{2,1,0:T(8,128)(2,1)S(1)} %get-tuple-element.34), channel_id=1, source_target_pairs={{0,16},{2,18},{4,20},{6,22},{8,24},{10,26},{12,28},{14,30},{16,0},... | collective-permute-start | bytes 196616 | tf_op jit(solution)/shard_map/ppermute | solution.py:441
  91.5 16.0 %collective-permute-done.11.far_rows_ref = bf16[8,32,128]{2,1,0:T(8,128)(2,1)S(1)} collective-permute-done((bf16[8,32,128]{2,1,0:T(8,128)(2,1)S(1)}, bf16[8,32,128]{2,1,0:T(8,128)(2,1)S(1)}, u32[]{:S(2)}, u32[]{:S(2)}) %collective-permute-start.11) | collective-permute-done | bytes 65568 | tf_op jit(solution)/shard_map/ppermute | solution.py:441
  107.5 1.1 stack_steps.1
  108.6 1.1 all-to-all-done.2
  109.7 3.6 %all-to-all-start.3 = ((bf16[8,64,1024]{2,1,0:T(8,128)(2,1)}), bf16[8,64,1024]{2,1,0:T(8,128)(2,1)S(1)}, u32[]{:S(2)}, u32[]{:S(2)}) async-start(bf16[8,64,1024]{2,1,0:T(8,128)(2,1)} %stack_steps.1), calls=%async_computation.3 | async-start | bytes 2097152 | tf_op jit(solution)/shard_map/all_to_all | solution.py:447
  113.3 2.7 %combine.1 = (f32[128,1792]{1,0:T(8,128)S(1)}, bf16[128,1792]{1,0:T(8,128)(2,1)S(1)}) custom-call(bf16[272,128]{1,0:T(8,128)(2,1)S(1)} %get-tuple-element.20.acts_ref.far_acts_ref, bf16[272,128]{1,0:T(8,128)(2,1)S(1)} %copy-done.16, bf16[8,2,32,1792]{3,2,1,0:T(8,128)(2,1)} %bitcast.4.back_ref), custom_call_target="tpu_custom_call" | custom-call | tf_op jit(solution)/shard_map/combine/pallas_call | solution.py:502
  116.0 2.4 %collective-permute-start.8 = (bf16[128,1792]{1,0:T(8,128)(2,1)S(1)}, bf16[128,1792]{1,0:T(8,128)(2,1)S(1)}, u32[]{:S(2)}, u32[]{:S(2)}) collective-permute-start(bf16[128,1792]{1,0:T(8,128)(2,1)S(1)} %get-tuple-element.28), channel_id=1, source_target_pairs={{0,16},{2,18},{4,20},{6,22},{8,24},{10,26},{12,28},{14,30},{16,0},... | collective-permute-start | bytes 1376264 | tf_op jit(solution)/shard_map/ppermute | solution.py:441
  118.8 18.4 %all-to-all-done.3.recv_ref = bf16[8,64,1024]{2,1,0:T(8,128)(2,1)S(1)} async-done(((bf16[8,64,1024]{2,1,0:T(8,128)(2,1)}), bf16[8,64,1024]{2,1,0:T(8,128)(2,1)S(1)}, u32[]{:S(2)}, u32[]{:S(2)}) %all-to-all-start.3) | async-done | bytes 1048608 | tf_op jit(solution)/shard_map/all_to_all | solution.py:447
  137.1 1.5 route_steps.1
  139.6 4.7 %all-to-all-start.4 = ((bf16[32,16,896]{2,1,0:T(8,128)(2,1)}), bf16[32,16,896]{2,1,0:T(8,128)(2,1)S(1)}, u32[]{:S(2)}, u32[]{:S(2)}) async-start(bf16[32,16,896]{2,1,0:T(8,128)(2,1)} %route_steps.1), calls=%async_computation.4 | async-start | bytes 1835008 | tf_op jit(solution)/shard_map/all_to_all | solution.py:528
  146.4 21.4 %all-to-all-done.4 = bf16[32,16,896]{2,1,0:T(8,128)(2,1)S(1)} async-done(((bf16[32,16,896]{2,1,0:T(8,128)(2,1)}), bf16[32,16,896]{2,1,0:T(8,128)(2,1)S(1)}, u32[]{:S(2)}, u32[]{:S(2)}) %all-to-all-start.4) | async-done | bytes 917536 | tf_op jit(solution)/shard_map/all_to_all | solution.py:528
  (76 shorter events, 15.1 us)
Async XLA Ops:
  0.6 8.1 %copy-start.20 = (s32[128,2]{0,1:T(2,128)S(1)}, s32[128,2]{0,1:T(2,128)}, u32[]{:S(2)}) copy-start(s32[128,2]{0,1:T(2,128)} %param.9) | copy-start | bytes 3076
  0.6 1.2 copy-start
  1.8 6.8 %copy-start.19 = (bf16[128,2,2,128]{3,2,1,0:T(2,128)(2,1)S(1)}, bf16[128,2,2,128]{3,2,1,0:T(2,128)(2,1)}, u32[]{:S(2)}) copy-start(bf16[128,2,2,128]{3,2,1,0:T(2,128)(2,1)} %param.11) | copy-start | bytes 393220
  1.8 7.0 %copy-start.21 = (f32[128,2]{0,1:T(2,128)S(1)}, f32[128,2]{0,1:T(2,128)}, u32[]{:S(2)}) copy-start(f32[128,2]{0,1:T(2,128)} %param.10) | copy-start | bytes 3076
  1.8 15.0 %copy-start.8 = (bf16[128,1792]{1,0:T(8,128)(2,1)S(1)}, bf16[128,1792]{1,0:T(8,128)(2,1)}, u32[]{:S(2)}) copy-start(bf16[128,1792]{1,0:T(8,128)(2,1)} %refs_0_.1) | copy-start | bytes 1376260
  1.9 17.1 %collective-permute-start.3 = (bf16[1,128,1792]{2,1,0:T(8,128)(2,1)S(1)}, bf16[1,128,1792]{2,1,0:T(8,128)(2,1)S(1)}, u32[]{:S(2)}, u32[]{:S(2)}) collective-permute-start(bf16[1,128,1792]{2,1,0:T(8,128)(2,1)S(1)} %split_state.3), channel_id=1, source_target_pairs={{0,1},{1,0},{2,3},{3,2},{4,5},{5,4},{6,7},{7,6},{8,9},{9,8},{10,11... | collective-permute-start | bytes 1376264 | tf_op jit(solution)/shard_map/ppermute | solution.py:444
  6.0 12.9 %collective-permute-start.2 = (bf16[64,1792]{1,0:T(8,128)(2,1)S(1)}, bf16[64,1792]{1,0:T(8,128)(2,1)S(1)}, u32[]{:S(2)}, u32[]{:S(2)}) collective-permute-start(bf16[64,1792]{1,0:T(8,128)(2,1)S(1)} %get-tuple-element.38), channel_id=1, source_target_pairs={{0,16},{2,18},{4,20},{6,22},{8,24},{10,26},{12,28},{14,30},{16,0},... | collective-permute-start | bytes 688136 | tf_op jit(solution)/shard_map/ppermute | solution.py:441
  8.7 10.2 %copy-start.9 = (bf16[128,512]{1,0:T(8,128)(2,1)}, bf16[128,512]{1,0:T(8,128)(2,1)S(1)}, u32[]{:S(2)}) copy-start(bf16[128,512]{1,0:T(8,128)(2,1)S(1)} %reshape.30.acts_ref) | copy-start | bytes 393220
  9.1 7.7 %collective-permute-start.1 = (bf16[256,128]{1,0:T(8,128)(2,1)S(1)}, bf16[256,128]{1,0:T(8,128)(2,1)S(1)}, u32[]{:S(2)}, u32[]{:S(2)}) collective-permute-start(bf16[256,128]{1,0:T(8,128)(2,1)S(1)} %get-tuple-element.21), channel_id=1, source_target_pairs={{0,1},{1,0},{2,3},{3,2},{4,5},{5,4},{6,7},{7,6},{8,9},{9,8},{10,11... | collective-permute-start | bytes 196616 | tf_op jit(solution)/shard_map/ppermute | solution.py:444
  16.8 5.7 %copy-start.4 = (bf16[1,128,3584]{2,1,0:T(8,128)(2,1)S(1)}, bf16[1,128,3584]{2,1,0:T(8,128)(2,1)}, u32[]{:S(2)}) copy-start(bf16[1,128,3584]{2,1,0:T(8,128)(2,1)} %param.14) | copy-start | bytes 2752516
  18.9 3.6 %copy-start.17 = (bf16[64,1792]{1,0:T(8,128)(2,1)}, bf16[64,1792]{1,0:T(8,128)(2,1)S(1)}, u32[]{:S(2)}) copy-start(bf16[64,1792]{1,0:T(8,128)(2,1)S(1)} %collective-permute-done.2.refs_0_) | copy-start | bytes 688132
  18.9 27.2 %all-to-all-start = ((bf16[8,32,2048]{2,1,0:T(8,128)(2,1)}), bf16[8,32,2048]{2,1,0:T(8,128)(2,1)S(1)}, u32[]{:S(2)}, u32[]{:S(2)}) async-start(bf16[8,32,2048]{2,1,0:T(8,128)(2,1)} %pack_own.1), calls=%async_computation | async-start | bytes 2097152 | tf_op jit(solution)/shard_map/all_to_all | solution.py:447
  22.6 22.8 %collective-permute-start.6 = (bf16[1,128,1792]{2,1,0:T(8,128)(2,1)S(1)}, bf16[1,128,1792]{2,1,0:T(8,128)(2,1)S(1)}, u32[]{:S(2)}, u32[]{:S(2)}) collective-permute-start(bf16[1,128,1792]{2,1,0:T(8,128)(2,1)S(1)} %split_state.4), channel_id=1, source_target_pairs={{0,1},{1,0},{2,3},{3,2},{4,5},{5,4},{6,7},{7,6},{8,9},{9,8},{10,11... | collective-permute-start | bytes 1376264 | tf_op jit(solution)/shard_map/ppermute | solution.py:444
  24.2 18.6 %collective-permute-start.5 = (bf16[64,1792]{1,0:T(8,128)(2,1)S(1)}, bf16[64,1792]{1,0:T(8,128)(2,1)S(1)}, u32[]{:S(2)}, u32[]{:S(2)}) collective-permute-start(bf16[64,1792]{1,0:T(8,128)(2,1)S(1)} %get-tuple-element.37), channel_id=1, source_target_pairs={{0,16},{2,18},{4,20},{6,22},{8,24},{10,26},{12,28},{14,30},{16,0},... | collective-permute-start | bytes 688136 | tf_op jit(solution)/shard_map/ppermute | solution.py:441
  26.7 16.0 %collective-permute-start = (bf16[272,128]{1,0:T(8,128)(2,1)S(1)}, bf16[272,128]{1,0:T(8,128)(2,1)S(1)}, u32[]{:S(2)}, u32[]{:S(2)}) collective-permute-start(bf16[272,128]{1,0:T(8,128)(2,1)S(1)} %get-tuple-element.20.acts_ref.far_acts_ref), channel_id=1, source_target_pairs={{0,16},{2,18},{4,20},{6,22},{8,24},{10,26},{12,28},{14,30},{16,0},... | collective-permute-start | bytes 208904 | tf_op jit(solution)/shard_map/ppermute | solution.py:441
  27.1 15.7 %collective-permute-start.4 = (bf16[256,128]{1,0:T(8,128)(2,1)S(1)}, bf16[256,128]{1,0:T(8,128)(2,1)S(1)}, u32[]{:S(2)}, u32[]{:S(2)}) collective-permute-start(bf16[256,128]{1,0:T(8,128)(2,1)S(1)} %get-tuple-element.21), channel_id=1, source_target_pairs={{0,17},{1,16},{2,19},{3,18},{4,21},{5,20},{6,23},{7,22},{8,25},{9,... | collective-permute-start | bytes 196616 | tf_op jit(solution)/shard_map/ppermute | solution.py:461
  42.8 3.4 %copy-start.15 = (bf16[272,128]{1,0:T(8,128)(2,1)}, bf16[272,128]{1,0:T(8,128)(2,1)S(1)}, u32[]{:S(2)}) copy-start(bf16[272,128]{1,0:T(8,128)(2,1)S(1)} %collective-permute-done.acts_ref.far_acts_ref) | copy-start | bytes 208900
  45.4 23.5 %copy-start.1 = (bf16[1,128,3584]{2,1,0:T(8,128)(2,1)S(1)}, bf16[1,128,3584]{2,1,0:T(8,128)(2,1)}, u32[]{:S(2)}) copy-start(bf16[1,128,3584]{2,1,0:T(8,128)(2,1)} %param.13) | copy-start | bytes 2752516
  46.2 22.7 %all-to-all-start.1 = ((bf16[8,32,2048]{2,1,0:T(8,128)(2,1)}), bf16[8,32,2048]{2,1,0:T(8,128)(2,1)S(1)}, u32[]{:S(2)}, u32[]{:S(2)}) async-start(bf16[8,32,2048]{2,1,0:T(8,128)(2,1)} %copy-done.3), calls=%async_computation.1 | async-start | bytes 2097152 | tf_op jit(solution)/shard_map/all_to_all | solution.py:447
  55.1 13.0 %collective-permute-start.7 = (bf16[1,128,1792]{2,1,0:T(8,128)(2,1)S(1)}, bf16[1,128,1792]{2,1,0:T(8,128)(2,1)S(1)}, u32[]{:S(2)}, u32[]{:S(2)}) collective-permute-start(bf16[1,128,1792]{2,1,0:T(8,128)(2,1)S(1)} %split_state.5), channel_id=1, source_target_pairs={{0,1},{1,0},{2,3},{3,2},{4,5},{5,4},{6,7},{7,6},{8,9},{9,8},{10,11... | collective-permute-start | bytes 1376264 | tf_op jit(solution)/shard_map/ppermute | solution.py:444
  70.0 1.2 copy-start.2
  71.2 38.5 %all-to-all-start.2 = ((bf16[8,64,1792]{2,1,0:T(8,128)(2,1)}), bf16[8,64,1792]{2,1,0:T(8,128)(2,1)}, u32[]{:S(2)}, u32[]{:S(2)}) async-start(bf16[8,64,1792]{2,1,0:T(8,128)(2,1)} %bitcast.14), calls=%async_computation.2 | async-start | bytes 3670016 | tf_op jit(solution)/shard_map/all_to_all | solution.py:447
  75.6 1.2 copy-start.5
  81.7 25.8 %collective-permute-start.9 = (bf16[2,128,896]{2,1,0:T(8,128)(2,1)S(1)}, bf16[2,128,896]{2,1,0:T(8,128)(2,1)S(1)}, u32[]{:S(2)}, u32[]{:S(2)}) collective-permute-start(bf16[2,128,896]{2,1,0:T(8,128)(2,1)S(1)} %get-tuple-element.30), channel_id=1, source_target_pairs={{0,16},{2,18},{4,20},{6,22},{8,24},{10,26},{12,28},{14,30},{16,0},... | collective-permute-start | bytes 1376264 | tf_op jit(solution)/shard_map/ppermute | solution.py:441
  82.9 5.8 %collective-permute-start.10 = (bf16[2,8,32,128]{3,2,1,0:T(8,128)(2,1)S(1)}, bf16[2,8,32,128]{3,2,1,0:T(8,128)(2,1)S(1)}, u32[]{:S(2)}, u32[]{:S(2)}) collective-permute-start(bf16[2,8,32,128]{3,2,1,0:T(8,128)(2,1)S(1)} %get-tuple-element.32), channel_id=1, source_target_pairs={{0,1},{1,0},{2,3},{3,2},{4,5},{5,4},{6,7},{7,6},{8,9},{9,8},{10,11... | collective-permute-start | bytes 393224 | tf_op jit(solution)/shard_map/ppermute | solution.py:444
  88.8 18.7 %collective-permute-start.11 = (bf16[8,32,128]{2,1,0:T(8,128)(2,1)S(1)}, bf16[8,32,128]{2,1,0:T(8,128)(2,1)S(1)}, u32[]{:S(2)}, u32[]{:S(2)}) collective-permute-start(bf16[8,32,128]{2,1,0:T(8,128)(2,1)S(1)} %get-tuple-element.34), channel_id=1, source_target_pairs={{0,16},{2,18},{4,20},{6,22},{8,24},{10,26},{12,28},{14,30},{16,0},... | collective-permute-start | bytes 196616 | tf_op jit(solution)/shard_map/ppermute | solution.py:441
  107.5 5.8 %copy-start.22 = (s32[8,2]{0,1:T(2,128)S(1)}, s32[8,2]{0,1:T(2,128)}, u32[]{:S(2)}) copy-start(s32[8,2]{0,1:T(2,128)} %param.8) | copy-start | bytes 196
  107.5 5.8 %copy-start.16 = (bf16[272,128]{1,0:T(8,128)(2,1)S(1)}, bf16[272,128]{1,0:T(8,128)(2,1)}, u32[]{:S(2)}) copy-start(bf16[272,128]{1,0:T(8,128)(2,1)} %copy-done.15) | copy-start | bytes 208900
  109.7 27.4 %all-to-all-start.3 = ((bf16[8,64,1024]{2,1,0:T(8,128)(2,1)}), bf16[8,64,1024]{2,1,0:T(8,128)(2,1)S(1)}, u32[]{:S(2)}, u32[]{:S(2)}) async-start(bf16[8,64,1024]{2,1,0:T(8,128)(2,1)} %stack_steps.1), calls=%async_computation.3 | async-start | bytes 2097152 | tf_op jit(solution)/shard_map/all_to_all | solution.py:447
  116.0 23.7 %collective-permute-start.8 = (bf16[128,1792]{1,0:T(8,128)(2,1)S(1)}, bf16[128,1792]{1,0:T(8,128)(2,1)S(1)}, u32[]{:S(2)}, u32[]{:S(2)}) collective-permute-start(bf16[128,1792]{1,0:T(8,128)(2,1)S(1)} %get-tuple-element.28), channel_id=1, source_target_pairs={{0,16},{2,18},{4,20},{6,22},{8,24},{10,26},{12,28},{14,30},{16,0},... | collective-permute-start | bytes 1376264 | tf_op jit(solution)/shard_map/ppermute | solution.py:441
  138.7 6.5 %copy-start.10 = (bf16[128,512]{1,0:T(8,128)(2,1)S(1)}, bf16[128,512]{1,0:T(8,128)(2,1)}, u32[]{:S(2)}) copy-start(bf16[128,512]{1,0:T(8,128)(2,1)} %copy-done.9) | copy-start | bytes 393220
  139.6 28.2 %all-to-all-start.4 = ((bf16[32,16,896]{2,1,0:T(8,128)(2,1)}), bf16[32,16,896]{2,1,0:T(8,128)(2,1)S(1)}, u32[]{:S(2)}, u32[]{:S(2)}) async-start(bf16[32,16,896]{2,1,0:T(8,128)(2,1)} %route_steps.1), calls=%async_computation.4 | async-start | bytes 1835008 | tf_op jit(solution)/shard_map/all_to_all | solution.py:528
  (8 other events, 7.9 us)
where the time goes:
time: 170 us; the launch traced here: 169 us
  waiting for transfers between devices  96 us (56%)
  starting transfers between devices  43.9 us (26%)
  Pallas kernels  14.1 us (8%)
  local copies, waits for them, and re-layouts  13.8 us (8%)
    ppermute x5, waiting for transfers between devices, neighbour(): return lax.ppermute(x, 'hidden', beside)  24.6 us
    all_to_all x1, waiting for transfers between devices, mirrored_local(): lax.all_to_all(after(routed, combined_far), ('expert', 'hidden'), split_a...  21.4 us
    all_to_all x4, waiting for transfers between devices, exchange(): lax.all_to_all(x, 'expert', split_axis=0, concat_axis=0, tiled=True, axis...  19.5 us
    all_to_all x4, starting transfers between devices, exchange(): lax.all_to_all(x, 'expert', split_axis=0, concat_axis=0, tiled=True, axis...  19.2 us
    ppermute x6, waiting for transfers between devices, mirror(): return lax.ppermute(x, 'expert', across)  17.4 us
    ppermute x1, waiting for transfers between devices, mirrored_local(): hidden_diagonal = lax.ppermute(hidden, ('expert', 'hidden'), diagonal)  13 us
    unnamed x48, local copies, waits for them, and re-layouts  11.7 us
    ppermute x6, starting transfers between devices, mirror(): return lax.ppermute(x, 'expert', across)  10.7 us
  transfers between devices with their start and end apart: 17, of which 10 were waited for; matrix products, arithmetic and copies ran while one was open for 1% of the time, Pallas kernels for 7%

commit v1 on v0

--- a/solution.py
+++ b/solution.py
@@ -158,11 +158,15 @@
 
 bf16 = jnp.bfloat16
 f32 = jnp.float32
+HEAVY = 10_000_000_000
 KERNEL_PARAMS = pltpu.CompilerParams(vmem_limit_bytes=40 * 1024 * 1024)
 
 
-def whole_call(body, out_shape, name):
-    return pl.pallas_call(body, out_shape=out_shape, name=name, compiler_params=KERNEL_PARAMS)
+def whole_call(body, out_shape, name, moved=None):
+    cost = None if moved is None else pl.CostEstimate(flops=100 * moved, bytes_accessed=moved, transcendentals=0)
+    return pl.pallas_call(
+        body, out_shape=out_shape, name=name, compiler_params=KERNEL_PARAMS, cost_estimate=cost
+    )
 
 
 def level_and_side(half):
@@ -259,129 +263,163 @@
     return ref[:, :, start : start + size].reshape(sources * cap, size)
 
 
-def forward_body(recv_ref, far_ref, weight_ref, beside_ref, out_ref):
-    sources, _, cap, wide = out_ref.shape
+def place_in_half(half):
+    return lax.rem(lax.axis_index("expert"), half)
+
+
+def forward_body(half, block, recv_ref, weight_ref, beside_ref, *out_refs):
+    cap, wide = out_refs[0].shape[-2:]
     units = weight_ref.shape[0]
-    weights = (columns_at(weight_ref, lax.axis_index("hidden"), wide), beside_ref[0])
-    for block, ref in enumerate((recv_ref, far_ref)):
-        total = None
-        for side, weight in enumerate(weights):
-            acts = rows_of(ref, wide + side * units, units)
-            part = jnp.dot(acts, weight, preferred_element_type=f32)
-            total = part if total is None else total + part
-        out_ref[:, block] = total.astype(bf16).reshape(sources, cap, wide)
-
-
-def grad_hidden_body(recv_ref, far_ref, weight_ref, beside_ref, keep_ref, send_ref):
-    _, sources, cap, units = send_ref.shape
-    wide = beside_ref.shape[2]
-    own = columns_at(weight_ref, lax.axis_index("hidden"), wide)
-    for block, ref in enumerate((recv_ref, far_ref)):
-        scaled = rows_of(ref, 0, wide)
-        for weight, out_ref in ((own, keep_ref), (beside_ref[0], send_ref)):
-            part = lax.dot_general(
-                scaled, weight, (((1,), (1,)), ((), ())), preferred_element_type=f32
-            )
-            out_ref[block] = part.astype(out_ref.dtype).reshape(sources, cap, units)
-
-
-def add_sides_body(keep_ref, got_ref, own_ref, far_ref):
-    own_ref[...] = (keep_ref[0] + got_ref[0].astype(f32)).astype(bf16)
-    far_ref[...] = (keep_ref[1] + got_ref[1].astype(f32)).astype(bf16)
-
-
-def update_body(half, recv_ref, far_ref, first_ref, second_ref, *refs):
-    keep_ref, send_ref = refs[-2:]
-    _, units, wide = refs[0].shape
+    me = place_in_half(half)
+    acts = jnp.concatenate([recv_ref[me ^ r, :, wide:] for r in range(half)], axis=0)
+    total = jnp.dot(
+        acts[:, :units],
+        columns_at(weight_ref, lax.axis_index("hidden"), wide),
+        preferred_element_type=f32,
+    )
+    total = total + jnp.dot(acts[:, units:], beside_ref[0], preferred_element_type=f32)
+    total = total.astype(bf16).reshape(half // 2, 2, cap, wide)
+    if block == 1:
+        for distance, ref in enumerate(out_refs):
+            ref[...] = total[distance]
+    else:
+        for core, ref in enumerate(out_refs):
+            ref[...] = total[:, core]
+
+
+def join_cores_body(keep_ref, got_ref, *out_refs):
+    for distance, ref in enumerate(out_refs):
+        ref[0] = keep_ref[distance]
+        ref[1] = got_ref[distance]
+
+
+def other_core_body(*refs):
+    out_ref = refs[-1]
+    for distance, ref in enumerate(refs[:-1]):
+        out_ref[distance] = ref[1]
+
+
+def update_body(
+    half,
+    recv_ref,
+    far_ref,
+    weight_ref,
+    first_ref,
+    second_ref,
+    weight_beside,
+    first_beside,
+    second_beside,
+    out_ref,
+):
+    _, units, wide = first_beside.shape
     level, here = level_and_side(half)
+    groups = out_ref.shape[0]
     narrow = wide // 2
-    for side in range(2):
-        for part, out_ref in ((level, keep_ref), (1 - level, send_ref)):
-            columns = pl.ds(pl.multiple_of(part * narrow, narrow), narrow)
+    each = units // groups
+    acts = jnp.concatenate([rows_of(ref, wide, 2 * units) for ref in (recv_ref, far_ref)], axis=0)
+    scaled = jnp.concatenate([rows_of(ref, 0, wide) for ref in (recv_ref, far_ref)], axis=0)
+    for part in range(2):
+        grads = lax.dot_general(
+            acts,
+            scaled[:, part * narrow : (part + 1) * narrow],
+            (((0,), (0,)), ((), ())),
+            preferred_element_type=f32,
+        )
+        for side in range(2):
             if side == 0:
                 moments = [
                     columns_at(ref, 2 * here + part, narrow) for ref in (first_ref, second_ref)
                 ]
             else:
-                moments = [ref[0, :, columns] for ref in refs[:-2]]
-            grad = None
-            for ref in (recv_ref, far_ref):
-                sources, cap, _ = ref.shape
-                more = lax.dot_general(
-                    rows_of(ref, wide + side * units, units),
-                    ref[:, :, columns].reshape(sources * cap, narrow),
-                    (((0,), (0,)), ((), ())),
-                    preferred_element_type=f32,
-                )
-                grad = more if grad is None else grad + more
+                moments = [
+                    ref[0, :, part * narrow : (part + 1) * narrow]
+                    for ref in (first_beside, second_beside)
+                ]
+            grad = grads[side * units : (side + 1) * units]
             first = first_decay * moments[0].astype(f32) + (1.0 - first_decay) * grad
             second = second_decay * moments[1].astype(f32)
             second = second + (1.0 - second_decay) * grad * grad
-            out_ref[side] = (first / (jnp.sqrt(second) + adam_epsilon)).astype(bf16)
-
-
-def stack_body(step_ref, far_step_ref, rows_ref, far_rows_ref, out_ref):
-    sources = out_ref.shape[0]
-    _, units, narrow = step_ref.shape
-    cap = rows_ref.shape[1]
-    each = units // sources
-    for expert, (steps, rows) in enumerate(((step_ref, rows_ref), (far_step_ref, far_rows_ref))):
-        for side in range(2):
-            at = (2 * expert + side) * each
-            out_ref[:, at : at + each, 0:narrow] = steps[side].reshape(sources, each, narrow)
-        out_ref[:, expert * cap : (expert + 1) * cap, narrow:] = rows[...]
-
-
-def combine_body(half, acts_ref, far_acts_ref, back_ref, own_ref, far_ref):
-    bins, _, cap, wide = back_ref.shape
-    tok = own_ref.shape[0]
+            step = (first / (jnp.sqrt(second) + adam_epsilon)).astype(bf16)
+            out_ref[:, part, side * each : (side + 1) * each, 0:narrow] = step.reshape(
+                groups, each, narrow
+            )
+    own = columns_at(weight_ref, here, wide)
+    for part, weight in enumerate((own, weight_beside[0])):
+        rows = lax.dot_general(
+            scaled, weight, (((1,), (1,)), ((), ())), preferred_element_type=f32
+        ).astype(bf16)
+        rows = rows.reshape(2, half // 2, 2, -1, units)
+        at = narrow + part * units
+        for block, place in enumerate((level, 1 - level)):
+            lines = pl.ds(place * (half // 2), half // 2)
+            for odd in range(2):
+                out_ref[lines, odd, :, at : at + units] = rows[block, :, odd]
+
+
+def combine_far_body(half, acts_ref, *refs):
+    near_refs, other_ref, out_ref = refs[:-2], refs[-2], refs[-1]
+    pieces = []
+    for distance, ref in enumerate(near_refs):
+        pieces += [ref[0], other_ref[distance]]
+    out_ref[...] = combined(half, acts_ref, pieces, out_ref.shape[0]).astype(bf16)
+
+
+def combine_own_body(half, acts_ref, far_ref, *refs):
+    out_ref = refs[-1]
+    pieces = [ref[core] for ref in refs[:-1] for core in range(2)]
+    total = combined(half, acts_ref, pieces, out_ref.shape[0])
+    out_ref[...] = (total + far_ref[...].astype(f32)).astype(bf16)
+
+
+def combined(half, acts_ref, pieces, tok):
+    cap = pieces[0].shape[0]
     level, _ = level_and_side(half)
     diagonal = same_index(tok)
-    for block, (ref, out_ref) in enumerate(((acts_ref, own_ref), (far_acts_ref, far_ref))):
-        ids, weights = read_meta(ref)
-        chosen = slot_choice(ids - (half * level).astype(f32), bins, cap)
-        chosen = chosen.astype(f32).astype(bf16)
-        rows = back_ref[:, block].reshape(bins * cap, wide)
-        total = None
-        for choice in range(2):
-            picked = lax.dot_general(
-                chosen[:, choice * tok : (choice + 1) * tok],
-                rows,
-                (((0,), (0,)), ((), ())),
-                preferred_element_type=f32,
-            )
-            upright = jnp.sum(
-                jnp.where(diagonal, weights[choice], 0.0), axis=1, keepdims=True
-            )
-            part = upright * picked
-            total = part if total is None else total + part
-        out_ref[...] = total.astype(out_ref.dtype)
-
-
-def add_halves_body(own_ref, far_ref, out_ref):
-    out_ref[...] = (own_ref[...] + far_ref[...].astype(f32)).astype(bf16)
-
-
-def gate_grads_body(half, far_acts_ref, acts_ref, recv_ref, out_ref):
-    sources, rows, total_wide = recv_ref.shape
-    tok = acts_ref.shape[0]
-    units = acts_ref.shape[1] // 4
-    level, _ = level_and_side(half)
-    ids, _ = read_meta(far_acts_ref)
-    upper = (ids >= half).astype(f32)
-    bin_of = (ids - half * upper) * 2 + jnp.abs(upper - level.astype(f32))
-    chosen = slot_choice(bin_of, 2 * sources, rows // 2).astype(f32).astype(bf16)
-    table = recv_ref[:, :, total_wide - units :].reshape(sources * rows, units)
+    ids, weights = read_meta(acts_ref)
+    ids = ids.astype(jnp.int32) - half * level
+    inside = (ids >= 0) & (ids < half)
+    bin_of = jnp.where(inside, ids ^ place_in_half(half), -1).astype(f32)
+    chosen = slot_choice(bin_of, half, cap).astype(f32).astype(bf16)
+    rows = jnp.concatenate(pieces, axis=0)
+    total = None
     for choice in range(2):
-        at = 2 * choice * units
-        gate = acts_ref[:, at : at + units].astype(f32)
-        up = acts_ref[:, at + units : at + 2 * units].astype(f32)
-        grad = lax.dot_general(
+        picked = lax.dot_general(
             chosen[:, choice * tok : (choice + 1) * tok],
-            table,
+            rows,
             (((0,), (0,)), ((), ())),
             preferred_element_type=f32,
         )
+        upright = jnp.sum(jnp.where(diagonal, weights[choice], 0.0), axis=1, keepdims=True)
+        part = upright * picked
+        total = part if total is None else total + part
+    return total
+
+
+def pick_grads_body(meta_ref, recv_ref, own_ref, send_ref):
+    places, rows, total_wide = recv_ref.shape
+    units = own_ref.shape[1]
+    ids, _ = read_meta(meta_ref)
+    chosen = slot_choice(ids, places, rows).astype(f32).astype(bf16)
+    for part, out_ref in enumerate((own_ref, send_ref)):
+        at = total_wide - (2 - part) * units
+        picked = lax.dot_general(
+            chosen,
+            recv_ref[:, :, at : at + units].reshape(places * rows, units),
+            (((0,), (0,)), ((), ())),
+            preferred_element_type=f32,
+        )
+        out_ref[...] = picked.astype(out_ref.dtype)
+
+
+def gate_grads_body(acts_ref, own_ref, got_ref, out_ref):
+    tok = acts_ref.shape[0]
+    units = own_ref.shape[1]
+    for choice in range(2):
+        at = 2 * choice * units
+        lines = slice(choice * tok, (choice + 1) * tok)
+        gate = acts_ref[:, at : at + units].astype(f32)
+        up = acts_ref[:, at + units : at + 2 * units].astype(f32)
+        grad = own_ref[lines, :] + got_ref[lines, :].astype(f32)
         sigmoid = jax.nn.sigmoid(gate)
         out_ref[:, at : at + units] = (
             grad * up * sigmoid * (1.0 + gate * (1.0 - sigmoid))
@@ -397,13 +435,13 @@
 
 
 def place_steps_body(recv_ref, out_ref):
-    halves, sources, sides, each, wide = recv_ref.shape
-    for half in range(halves):
-        for source in range(sources):
+    groups, parts, sides, each, wide = recv_ref.shape
+    for group in range(groups):
+        for part in range(parts):
             for side in range(sides):
-                at = (side * halves + half) * wide
-                out_ref[source * each : (source + 1) * each, at : at + wide] = recv_ref[
-                    half, source, side
+                at = (side * parts + part) * wide
+                out_ref[group * each : (group + 1) * each, at : at + wide] = recv_ref[
+                    group, part, side
                 ]
 
 
@@ -451,7 +489,7 @@
     def shaped(*shape, dtype=bf16):
         return jax.ShapeDtypeStruct(shape, dtype)
 
-    grads_far = [mirror(grad_out[: tok // 2]), mirror(grad_out[tok // 2 :])]
+    grads_far = [mirror(grad_out)]
     acts = gate_up.reshape(tok, 4 * units)
     hidden, noted = whole_call(
         prepare_body, (shaped(top * tok, units), shaped(top * tok + 16, units)), "prepare"
@@ -471,50 +509,58 @@
         whole_call, functools.partial(pack_body, half), shaped(half, cap, row)
     )
     packed = pack("pack_own")(noted, hidden_beside, grad_out)
-    recv = exchange(after(packed, grads_far[0], weight_beside))
-    packed_far = pack("pack_far")(noted_far, hidden_diagonal, *grads_far)
-    recv_far = exchange(after(packed_far, recv, first_beside))
-    recv_far = after(recv_far, second_beside)
-
-    outputs = whole_call(forward_body, shaped(half, 2, cap, wide), "forward")(
-        recv, recv_far, state[0], weight_beside
-    )
-    back = exchange(outputs.reshape(half, 2 * cap, wide)).reshape(half, 2, cap, wide)
-
-    grad_keep, grad_send = whole_call(
-        grad_hidden_body,
-        (shaped(2, half, cap, units, dtype=f32), shaped(2, half, cap, units)),
-        "grad_hidden",
-    )(recv, recv_far, state[0], weight_beside)
-    step, step_send = whole_call(
+    recv = exchange(packed)
+
+    packed_far = pack("pack_far", moved=HEAVY)(noted_far, hidden_diagonal, *grads_far)
+    recv, packed_far, weight_beside, first_beside = lax.optimization_barrier(
+        (recv, packed_far, weight_beside, first_beside)
+    )
+    recv_far = exchange(packed_far)
+    recv_far, second_beside = lax.optimization_barrier((recv_far, second_beside))
+
+    def forward(rows, block, shape, name):
+        return whole_call(functools.partial(forward_body, half, block), shape, name)(
+            rows, state[0], weight_beside
+        )
+
+    def at_distance(x, distance):
+        return lax.ppermute(x, "expert", [(k, k ^ distance) for k in range(places)])
+
+    def by_chip(outputs):
+        return [outputs[0]] + [at_distance(outputs[k], 2 * k) for k in range(1, half // 2)]
+
+    pairs = (shaped(2, cap, wide),) * (half // 2)
+    cores = (shaped(half // 2, cap, wide),) * 2
+
+    outputs_far = forward(recv_far, 1, pairs, "forward_far")
+    steps = whole_call(
         functools.partial(update_body, half),
-        (shaped(2, units, narrow), shaped(2, units, narrow)),
+        shaped(half, 2, 2 * each, narrow + 2 * units),
         "update",
-    )(recv, recv_far, *state[1:], first_beside, second_beside)
-    step_far = mirror(step_send)
-    rows_own, rows_send = whole_call(
-        add_sides_body, (shaped(half, cap, units), shaped(half, cap, units)), "add_sides"
-    )(grad_keep, neighbour(grad_send))
-    rows_far = mirror(rows_send)
-    stacked = whole_call(stack_body, shaped(half, 2 * cap, narrow + units), "stack_steps")(
-        step, step_far, rows_own, rows_far
-    )
-    combined_own, combined_send = whole_call(
-        functools.partial(combine_body, half),
-        (shaped(tok, wide, dtype=f32), shaped(tok, wide)),
-        "combine",
-    )(noted, noted_far, back)
+    )(recv, after(recv_far, outputs_far), *state, weight_beside, first_beside, second_beside)
+    spread = lax.all_to_all(
+        steps.reshape(places, 2 * each, narrow + 2 * units),
+        "expert",
+        split_axis=0,
+        concat_axis=0,
+        tiled=True,
+    )
+
+    near_far = by_chip(outputs_far)
+    near_far, steps = lax.optimization_barrier((near_far, steps))
+    crossing = whole_call(other_core_body, cores[0], "other_core_far")(*near_far)
+    combined_send = whole_call(
+        functools.partial(combine_far_body, half), shaped(tok, wide), "combine_far", HEAVY
+    )(noted_far, *near_far, at_distance(crossing, 1))
     combined_far = mirror(combined_send)
-    combined = whole_call(add_halves_body, shaped(tok, wide), "add_halves")(
-        combined_own, combined_far
-    )
-
-    spread = exchange(after(stacked, back))
+    keep_core, send_core = forward(after(recv, combined_send), 0, cores, "forward_own")
+    joined = whole_call(join_cores_body, pairs, "join_cores")(
+        keep_core, at_distance(send_core, 1)
+    )
+    near = by_chip(joined)
 
     partner = partner_table(swap_pairs, places)
-    from_source = jnp.repeat(partner % half, 2)
     sides = jnp.tile(jnp.arange(2, dtype=jnp.int32), places)
-    from_line = jnp.repeat((partner // half) ^ level, 2) * 2 + (sides ^ side)
     smem = pl.BlockSpec(memory_space=pltpu.SMEM)
     vmem = pl.BlockSpec(memory_space=pltpu.VMEM)
     routed = pl.pallas_call(
@@ -524,16 +570,27 @@
         out_shape=shaped(2 * places, each, narrow),
         name="route_steps",
         compiler_params=KERNEL_PARAMS,
-    )(from_source.astype(jnp.int32), from_line.astype(jnp.int32), spread)
+    )(jnp.repeat(partner, 2).astype(jnp.int32), (sides ^ side).astype(jnp.int32), spread)
     placed = lax.all_to_all(
-        after(routed, combined_far), ("expert", "hidden"), split_axis=0, concat_axis=0, tiled=True
-    )
-
-    grad_gate_up = whole_call(
-        functools.partial(gate_grads_body, half), shaped(tok, 4 * units), "gate_grads"
-    )(noted, acts, spread).reshape(gate_up.shape)
+        after(routed, combined_send), ("expert", "hidden"), split_axis=0, concat_axis=0, tiled=True
+    )
+
+    rows_own, rows_send = whole_call(
+        pick_grads_body,
+        (shaped(top * tok, units, dtype=f32), shaped(top * tok, units)),
+        "pick_grads",
+        HEAVY,
+    )(noted, spread)
+    grad_gate_up = whole_call(gate_grads_body, shaped(tok, 4 * units), "gate_grads")(
+        acts, rows_own, neighbour(rows_send)
+    ).reshape(gate_up.shape)
+
+    near, combined_far = lax.optimization_barrier((near, combined_far, rows_own))[:2]
+    combined = whole_call(
+        functools.partial(combine_own_body, half), shaped(tok, wide), "combine_own"
+    )(noted, combined_far, *near)
     adam_step = whole_call(place_steps_body, shaped(units, 2 * wide), "place_steps")(
-        placed.reshape(2, half, 2, each, narrow)
+        placed.reshape(half, 2, 2, each, narrow)
     )
     return combined, grad_gate_up, adam_step[None]
 
@@ -546,7 +603,8 @@
     fits = sides == 2 and top == 2 and places % 4 == 0 and places <= 256
     fits = fits and places * cap == 2 * tok * top and cap % 16 == 0
     fits = fits and wide % 256 == 0 and units == tok and tok % 128 == 0
-    fits = fits and units % (8 * places) == 0 and 2 * cap == 4 * (units // (places // 2))
+    fits = fits and places & (places - 1) == 0 and (units // (places // 2)) % 16 == 0
+    fits = fits and cap == 2 * (units // (places // 2))
     return mirrored_local(*arrays) if fits else general_local(*arrays)
 
 

time: 170 us -> 153 us (0.900)
  waiting for transfers between devices: 96 us -> 75.3 us
  Pallas kernels: 14.1 us -> 24.2 us
  local copies, waits for them, and re-layouts: 13.8 us -> 6.31 us
  starting transfers between devices: 43.9 us -> 45.8 us
    ppermute x6 -> x3, waiting for transfers between devices: 17.4 us -> 0.24 us  [mirror(): return lax.ppermute(x, 'expert', across)]
    all_to_all x1 -> x2, waiting for transfers between devices: 21.4 us -> 38.3 us  [the longest x1 23.4 us: mirrored_local(): lax.all_to_all(steps.reshape(places, 2 * each, narrow + 2 * units), 'expe...]
    all_to_all x4 -> x2, waiting for transfers between devices: 19.5 us -> 7.25 us  [exchange(): lax.all_to_all(x, 'expert', split_axis=0, concat_axis=0, tiled=True, axis...]
    all_to_all x4 -> x2, starting transfers between devices: 19.2 us -> 7.8 us  [exchange(): lax.all_to_all(x, 'expert', split_axis=0, concat_axis=0, tiled=True, axis...]
    ppermute x5, waiting for transfers between devices: 24.6 us -> 15.2 us  [neighbour(): return lax.ppermute(x, 'hidden', beside)]
    all_to_all x1 -> x2, starting transfers between devices: 4.72 us -> 13.8 us  [the longest x1 8.49 us: mirrored_local(): lax.all_to_all(after(routed, combined_send), ('expert', 'hidden'), split_...]
    ppermute x0 -> x8, starting transfers between devices: none -> 7.54 us  [at_distance(): return lax.ppermute(x, 'expert', [(k, k ^ distance) for k in range(places)])]
    unnamed x48 -> x42, local copies, waits for them, and re-layouts: 11.7 us -> 4.41 us
  transfers between devices with their start and end apart: 17 -> 21, of which waited for: 10 -> 11; matrix products, arithmetic and copies ran while one was open for 1% -> 2% of each run, Pallas kernels for 7% -> 13%
where the time goes in v1:
time: 153 us
  waiting for transfers between devices  75.3 us (49%)
  starting transfers between devices  45.8 us (30%)
  Pallas kernels  24.2 us (16%)
  local copies, waits for them, and re-layouts  6.31 us (4%)
    all_to_all x1, waiting for transfers between devices, mirrored_local(): lax.all_to_all(steps.reshape(places, 2 * each, narrow + 2 * units), 'expe...  23.4 us
    ppermute x5, waiting for transfers between devices, neighbour(): return lax.ppermute(x, 'hidden', beside)  15.2 us
    all_to_all x1, waiting for transfers between devices, mirrored_local(): lax.all_to_all(after(routed, combined_send), ('expert', 'hidden'), split_...  14.8 us
    ppermute x1, waiting for transfers between devices, mirrored_local(): hidden_diagonal = lax.ppermute(hidden, ('expert', 'hidden'), diagonal)  9.63 us
    all_to_all x1, starting transfers between devices, mirrored_local(): lax.all_to_all(after(routed, combined_send), ('expert', 'hidden'), split_...  8.49 us
    all_to_all x2, starting transfers between devices, exchange(): lax.all_to_all(x, 'expert', split_axis=0, concat_axis=0, tiled=True, axis...  7.8 us
    ppermute x8, starting transfers between devices, at_distance(): return lax.ppermute(x, 'expert', [(k, k ^ distance) for k in range(places)])  7.54 us
    all_to_all x2, waiting for transfers between devices, exchange(): lax.all_to_all(x, 'expert', split_axis=0, concat_axis=0, tiled=True, axis...  7.25 us
  transfers between devices with their start and end apart: 21, of which 11 were waited for; matrix products, arithmetic and copies ran while one was open for 2% of the time, Pallas kernels for 13%

profile of v1, /device:TPU:0, one launch (start us, length us, event | category | flops | bytes accessed | tf_op | source)
XLA Modules:
  0.0 152.5 jit_solution(16497306728626886684)
XLA Ops:
  0.6 4.1 %collective-permute-start.3 = (bf16[128,1792]{1,0:T(8,128)(2,1)}, bf16[128,1792]{1,0:T(8,128)(2,1)S(1)}, u32[]{:S(2)}, u32[]{:S(2)}) collective-permute-start(bf16[128,1792]{1,0:T(8,128)(2,1)} %refs_0_.1), channel_id=1, source_target_pairs={{0,16},{2,18},{4,20},{6,22},{8,24},{10,26},{12,28},{14,30},{16,0},... | collective-permute-start | bytes 1376264 | tf_op jit(solution)/shard_map/ppermute | solution.py:479
  7.6 1.8 %collective-permute-start = (bf16[256,128]{1,0:T(8,128)(2,1)S(1)}, bf16[256,128]{1,0:T(8,128)(2,1)S(1)}, u32[]{:S(2)}, u32[]{:S(2)}) collective-permute-start(bf16[256,128]{1,0:T(8,128)(2,1)S(1)} %get-tuple-element.38), channel_id=1, source_target_pairs={{0,1},{1,0},{2,3},{3,2},{4,5},{5,4},{6,7},{7,6},{8,9},{9,8},{10,11... | collective-permute-start | bytes 196616 | tf_op jit(solution)/shard_map/ppermute | solution.py:482
  9.4 2.5 %collective-permute-start.2 = (bf16[256,128]{1,0:T(8,128)(2,1)S(1)}, bf16[256,128]{1,0:T(8,128)(2,1)S(1)}, u32[]{:S(2)}, u32[]{:S(2)}) collective-permute-start(bf16[256,128]{1,0:T(8,128)(2,1)S(1)} %get-tuple-element.38), channel_id=1, source_target_pairs={{0,17},{1,16},{2,19},{3,18},{4,21},{5,20},{6,23},{7,22},{8,25},{9,... | collective-permute-start | bytes 196616 | tf_op jit(solution)/shard_map/ppermute | solution.py:499
  13.9 1.5 collective-permute-start.5
  16.8 1.7 %pack_own.1 = bf16[8,32,2048]{2,1,0:T(8,128)(2,1)} custom-call(bf16[272,128]{1,0:T(8,128)(2,1)S(1)} %get-tuple-element.37.acts_ref.meta_ref, bf16[256,128]{1,0:T(8,128)(2,1)S(1)} %collective-permute-done.beside_ref, bf16[128,1792]{1,0:T(8,128)(2,1)S(1)} %copy-done.8), custom_call_target="tpu_custom_call" | custom-call | tf_op jit(solution)/shard_map/pack_own/pallas_call | solution.py:511
  18.4 4.2 %all-to-all-start = ((bf16[8,32,2048]{2,1,0:T(8,128)(2,1)}), bf16[8,32,2048]{2,1,0:T(8,128)(2,1)}, u32[]{:S(2)}, u32[]{:S(2)}) async-start(bf16[8,32,2048]{2,1,0:T(8,128)(2,1)} %pack_own.1), calls=%async_computation | async-start | bytes 2097152 | tf_op jit(solution)/shard_map/all_to_all | solution.py:485
  22.7 9.6 %collective-permute-done.2.beside_ref = bf16[256,128]{1,0:T(8,128)(2,1)S(1)} collective-permute-done((bf16[256,128]{1,0:T(8,128)(2,1)S(1)}, bf16[256,128]{1,0:T(8,128)(2,1)S(1)}, u32[]{:S(2)}, u32[]{:S(2)}) %collective-permute-start.2) | collective-permute-done | bytes 65568 | tf_op jit(solution)/shard_map/ppermute | solution.py:499
  34.0 2.6 %collective-permute-done.4.beside_ref.weight_beside = bf16[1,128,1792]{2,1,0:T(8,128)(2,1)} collective-permute-done((bf16[1,128,1792]{2,1,0:T(8,128)(2,1)}, bf16[1,128,1792]{2,1,0:T(8,128)(2,1)}, u32[]{:S(2)}, u32[]{:S(2)}) %collective-permute-start.4) | collective-permute-done | bytes 458784 | tf_op jit(solution)/shard_map/ppermute | solution.py:482
  36.6 5.8 %all-to-all-done.recv_ref = bf16[8,32,2048]{2,1,0:T(8,128)(2,1)} async-done(((bf16[8,32,2048]{2,1,0:T(8,128)(2,1)}), bf16[8,32,2048]{2,1,0:T(8,128)(2,1)}, u32[]{:S(2)}, u32[]{:S(2)}) %all-to-all-start) | async-done | bytes 1048608 | tf_op jit(solution)/shard_map/all_to_all | solution.py:485
  42.4 3.6 %all-to-all-start.1 = ((bf16[8,32,2048]{2,1,0:T(8,128)(2,1)}), bf16[8,32,2048]{2,1,0:T(8,128)(2,1)S(1)}, u32[]{:S(2)}, u32[]{:S(2)}) async-start(bf16[8,32,2048]{2,1,0:T(8,128)(2,1)} %copy-done.7), calls=%async_computation.1 | async-start | bytes 2097152 | tf_op jit(solution)/shard_map/all_to_all | solution.py:485
  46.1 1.7 %collective-permute-start.6 = (bf16[1,128,1792]{2,1,0:T(8,128)(2,1)S(1)}, bf16[1,128,1792]{2,1,0:T(8,128)(2,1)S(1)}, u32[]{:S(2)}, u32[]{:S(2)}) collective-permute-start(bf16[1,128,1792]{2,1,0:T(8,128)(2,1)S(1)} %split_state.5), channel_id=1, source_target_pairs={{0,1},{1,0},{2,3},{3,2},{4,5},{5,4},{6,7},{7,6},{8,9},{9,8},{10,11... | collective-permute-start | bytes 1376264 | tf_op jit(solution)/shard_map/ppermute | solution.py:482
  47.7 11.2 %collective-permute-done.6.second_beside = bf16[1,128,1792]{2,1,0:T(8,128)(2,1)S(1)} collective-permute-done((bf16[1,128,1792]{2,1,0:T(8,128)(2,1)S(1)}, bf16[1,128,1792]{2,1,0:T(8,128)(2,1)S(1)}, u32[]{:S(2)}, u32[]{:S(2)}) %collective-permute-start.6) | collective-permute-done | bytes 458784 | tf_op jit(solution)/shard_map/ppermute | solution.py:482
  58.9 1.4 all-to-all-done.1.recv_ref.far_ref
  60.4 1.7 %forward_far.1 = (bf16[2,32,1792]{2,1,0:T(8,128)(2,1)S(1)}, bf16[2,32,1792]{2,1,0:T(8,128)(2,1)S(1)}, bf16[2,32,1792]{2,1,0:T(8,128)(2,1)S(1)}, bf16[2,32,1792]{2,1,0:T(8,128)(2,1)S(1)}) custom-call(bf16[8,32,2048]{2,1,0:T(8,128)(2,1)S(1)} %all-to-all-done.1.recv_ref.far_ref, bf16[128,3584]{1,0:T(8,128)(2,1)S(1)} %bitcast.11, ...), custom_call_target="tpu_custom_call" | custom-call | tf_op jit(solution)/shard_map/forward_far/pallas_call | solution.py:522
  62.1 1.5 %collective-permute-start.7 = (bf16[2,32,1792]{2,1,0:T(8,128)(2,1)S(1)}, bf16[2,32,1792]{2,1,0:T(8,128)(2,1)S(1)}, u32[]{:S(2)}, u32[]{:S(2)}) collective-permute-start(bf16[2,32,1792]{2,1,0:T(8,128)(2,1)S(1)} %get-tuple-element.46), channel_id=1, source_target_pairs={{0,4},{2,6},{4,0},{6,2},{8,12},{10,14},{12,8},{14,10},{16,20},{18,... | collective-permute-start | bytes 688136 | tf_op jit(solution)/shard_map/ppermute | solution.py:527
  64.2 1.5 collective-permute-start.9
  65.7 5.0 %update.1 = bf16[8,2,32,1152]{3,2,1,0:T(8,128)(2,1)} custom-call(bf16[8,32,2048]{2,1,0:T(8,128)(2,1)} %all-to-all-done.recv_ref, bf16[8,32,2048]{2,1,0:T(8,128)(2,1)S(1)} %all-to-all-done.1.recv_ref.far_ref, bf16[128,3584]{1,0:T(8,128)(2,1)S(1)} %bitcast.12, bf16[128,3584]{1,0:T(8,128)(2,1)S(1)} %bitcast.15, bf16[128,3584]{1,0:T(8,128)(2,1)S(1)} %bitcast.17, ...), custom_call_target="tpu_custom_call" | custom-call | tf_op jit(solution)/shard_map/update/pallas_call | solution.py:536
  70.7 1.5 collective-permute-done.8.refs_2_
  72.2 3.2 %collective-permute-done.9.refs_3_ = bf16[2,32,1792]{2,1,0:T(8,128)(2,1)S(1)} collective-permute-done((bf16[2,32,1792]{2,1,0:T(8,128)(2,1)S(1)}, bf16[2,32,1792]{2,1,0:T(8,128)(2,1)S(1)}, u32[]{:S(2)}, u32[]{:S(2)}) %collective-permute-start.9) | collective-permute-done | bytes 229408 | tf_op jit(solution)/shard_map/ppermute | solution.py:527
  76.2 5.3 %all-to-all-start.2 = ((bf16[16,32,1152]{2,1,0:T(8,128)(2,1)}), bf16[16,32,1152]{2,1,0:T(8,128)(2,1)}, u32[]{:S(2)}, u32[]{:S(2)}) async-start(bf16[16,32,1152]{2,1,0:T(8,128)(2,1)} %bitcast.3), calls=%async_computation.2 | async-start | bytes 2359296 | tf_op jit(solution)/shard_map/all_to_all | solution.py:541
  82.9 2.0 %forward_own.1 = (bf16[4,32,1792]{2,1,0:T(8,128)(2,1)S(1)}, bf16[4,32,1792]{2,1,0:T(8,128)(2,1)S(1)}) custom-call(bf16[8,32,2048]{2,1,0:T(8,128)(2,1)} %all-to-all-done.recv_ref, bf16[128,3584]{1,0:T(8,128)(2,1)S(1)} %bitcast.13, bf16[1,128,1792]{2,1,0:T(8,128)(2,1)} %collective-permute-done.4.beside_ref.weight_beside), custom_call_target="tpu_custom_call" | custom-call | tf_op jit(solution)/shard_map/forward_own/pallas_call | solution.py:522
  85.7 2.6 %collective-permute-start.15 = (bf16[128,1792]{1,0:T(8,128)(2,1)}, bf16[128,1792]{1,0:T(8,128)(2,1)}, u32[]{:S(2)}, u32[]{:S(2)}) collective-permute-start(bf16[128,1792]{1,0:T(8,128)(2,1)} %combine_far.1), channel_id=1, source_target_pairs={{0,16},{2,18},{4,20},{6,22},{8,24},{10,26},{12,28},{14,30},{16,0},... | collective-permute-start | bytes 1376264 | tf_op jit(solution)/shard_map/ppermute | solution.py:479
  89.2 1.5 collective-permute-start.12
  90.7 1.5 collective-permute-start.13
  92.7 23.4 %all-to-all-done.2.recv_ref = bf16[16,32,1152]{2,1,0:T(8,128)(2,1)} async-done(((bf16[16,32,1152]{2,1,0:T(8,128)(2,1)}), bf16[16,32,1152]{2,1,0:T(8,128)(2,1)}, u32[]{:S(2)}, u32[]{:S(2)}) %all-to-all-start.2) | async-done | bytes 1179680 | tf_op jit(solution)/shard_map/all_to_all | solution.py:541
  116.1 2.3 %route_steps.1 = bf16[32,16,896]{2,1,0:T(8,128)(2,1)} custom-call(s32[32]{0:T(128)S(1)} %reshape.26.source_ref, s32[32]{0:T(128)S(1)} %xor.10.line_ref, bf16[16,32,1152]{2,1,0:T(8,128)(2,1)} %all-to-all-done.2.recv_ref), custom_call_target="tpu_custom_call" | custom-call | tf_op jit(solution)/shard_map/route_steps/pallas_call | solution.py:566
  118.5 8.5 %all-to-all-start.3 = ((bf16[32,16,896]{2,1,0:T(8,128)(2,1)}), bf16[32,16,896]{2,1,0:T(8,128)(2,1)}, u32[]{:S(2)}, u32[]{:S(2)}) async-start(bf16[32,16,896]{2,1,0:T(8,128)(2,1)} %route_steps.1), calls=%async_computation.3 | async-start | bytes 1835008 | tf_op jit(solution)/shard_map/all_to_all | solution.py:574
  127.0 1.8 %pick_grads.1 = (f32[256,128]{1,0:T(8,128)S(1)}, bf16[256,128]{1,0:T(8,128)(2,1)S(1)}) custom-call(bf16[272,128]{1,0:T(8,128)(2,1)S(1)} %copy-done.10, bf16[16,32,1152]{2,1,0:T(8,128)(2,1)} %all-to-all-done.2.recv_ref), custom_call_target="tpu_custom_call" | custom-call | flops 999999995904 | bytes 10000000000 | tf_op jit(solution)/shard_map/pick_grads/pallas_call | solution.py:578
  128.8 1.8 %collective-permute-start.16 = (bf16[256,128]{1,0:T(8,128)(2,1)S(1)}, bf16[256,128]{1,0:T(8,128)(2,1)S(1)}, u32[]{:S(2)}, u32[]{:S(2)}) collective-permute-start(bf16[256,128]{1,0:T(8,128)(2,1)S(1)} %get-tuple-element.69), channel_id=1, source_target_pairs={{0,1},{1,0},{2,3},{3,2},{4,5},{5,4},{6,7},{7,6},{8,9},{9,8},{10,11... | collective-permute-start | bytes 196616 | tf_op jit(solution)/shard_map/ppermute | solution.py:482
  130.8 2.7 %combine_own.1 = bf16[128,1792]{1,0:T(8,128)(2,1)} custom-call(bf16[272,128]{1,0:T(8,128)(2,1)S(1)} %copy-done.10, bf16[128,1792]{1,0:T(8,128)(2,1)} %collective-permute-done.15.far_ref, bf16[2,32,1792]{2,1,0:T(8,128)(2,1)S(1)} %get-tuple-element.65.refs_0_, bf16[2,32,1792]{2,1,0:T(8,128)(2,1)} %collective-permute-done.12.refs_1_, ...), custom_call_target="tpu_custom_call" | custom-call | tf_op jit(solution)/shard_map/combine_own/pallas_call | solution.py:589
  135.6 14.8 %all-to-all-done.3 = bf16[32,16,896]{2,1,0:T(8,128)(2,1)} async-done(((bf16[32,16,896]{2,1,0:T(8,128)(2,1)}), bf16[32,16,896]{2,1,0:T(8,128)(2,1)}, u32[]{:S(2)}, u32[]{:S(2)}) %all-to-all-start.3) | async-done | bytes 917536 | tf_op jit(solution)/shard_map/all_to_all | solution.py:574
  150.4 2.2 %place_steps.1 = bf16[128,3584]{1,0:T(8,128)(2,1)} custom-call(bf16[8,2,2,16,896]{4,3,2,1,0:T(8,128)(2,1)} %bitcast.6.recv_ref), custom_call_target="tpu_custom_call" | custom-call | tf_op jit(solution)/shard_map/place_steps/pallas_call | solution.py:592
  (78 shorter events, 15.1 us)
Async XLA Ops:
  0.6 14.8 %copy-start = (bf16[1,128,3584]{2,1,0:T(8,128)(2,1)S(1)}, bf16[1,128,3584]{2,1,0:T(8,128)(2,1)}, u32[]{:S(2)}) copy-start(bf16[1,128,3584]{2,1,0:T(8,128)(2,1)} %param.13) | copy-start | bytes 2752516
  0.6 31.7 %collective-permute-start.3 = (bf16[128,1792]{1,0:T(8,128)(2,1)}, bf16[128,1792]{1,0:T(8,128)(2,1)S(1)}, u32[]{:S(2)}, u32[]{:S(2)}) collective-permute-start(bf16[128,1792]{1,0:T(8,128)(2,1)} %refs_0_.1), channel_id=1, source_target_pairs={{0,16},{2,18},{4,20},{6,22},{8,24},{10,26},{12,28},{14,30},{16,0},... | collective-permute-start | bytes 1376264 | tf_op jit(solution)/shard_map/ppermute | solution.py:479
  5.7 10.5 %copy-start.5 = (bf16[128,512]{1,0:T(8,128)(2,1)}, bf16[128,512]{1,0:T(8,128)(2,1)S(1)}, u32[]{:S(2)}) copy-start(bf16[128,512]{1,0:T(8,128)(2,1)S(1)} %reshape.23.acts_ref) | copy-start | bytes 393220
  7.5 9.3 %copy-start.9 = (bf16[272,128]{1,0:T(8,128)(2,1)}, bf16[272,128]{1,0:T(8,128)(2,1)S(1)}, u32[]{:S(2)}) copy-start(bf16[272,128]{1,0:T(8,128)(2,1)S(1)} %get-tuple-element.37.acts_ref.meta_ref) | copy-start | bytes 208900
  7.5 24.8 %collective-permute-start.1 = (bf16[272,128]{1,0:T(8,128)(2,1)S(1)}, bf16[272,128]{1,0:T(8,128)(2,1)S(1)}, u32[]{:S(2)}, u32[]{:S(2)}) collective-permute-start(bf16[272,128]{1,0:T(8,128)(2,1)S(1)} %get-tuple-element.37.acts_ref.meta_ref), channel_id=1, source_target_pairs={{0,16},{2,18},{4,20},{6,22},{8,24},{10,26},{12,28},{14,30},{16,0},... | collective-permute-start | bytes 208904 | tf_op jit(solution)/shard_map/ppermute | solution.py:479
  7.6 8.6 %collective-permute-start = (bf16[256,128]{1,0:T(8,128)(2,1)S(1)}, bf16[256,128]{1,0:T(8,128)(2,1)S(1)}, u32[]{:S(2)}, u32[]{:S(2)}) collective-permute-start(bf16[256,128]{1,0:T(8,128)(2,1)S(1)} %get-tuple-element.38), channel_id=1, source_target_pairs={{0,1},{1,0},{2,3},{3,2},{4,5},{5,4},{6,7},{7,6},{8,9},{9,8},{10,11... | collective-permute-start | bytes 196616 | tf_op jit(solution)/shard_map/ppermute | solution.py:482
  9.4 22.9 %collective-permute-start.2 = (bf16[256,128]{1,0:T(8,128)(2,1)S(1)}, bf16[256,128]{1,0:T(8,128)(2,1)S(1)}, u32[]{:S(2)}, u32[]{:S(2)}) collective-permute-start(bf16[256,128]{1,0:T(8,128)(2,1)S(1)} %get-tuple-element.38), channel_id=1, source_target_pairs={{0,17},{1,16},{2,19},{3,18},{4,21},{5,20},{6,23},{7,22},{8,25},{9,... | collective-permute-start | bytes 196616 | tf_op jit(solution)/shard_map/ppermute | solution.py:499
  13.9 20.0 %collective-permute-start.5 = (bf16[1,128,1792]{2,1,0:T(8,128)(2,1)}, bf16[1,128,1792]{2,1,0:T(8,128)(2,1)}, u32[]{:S(2)}, u32[]{:S(2)}) collective-permute-start(bf16[1,128,1792]{2,1,0:T(8,128)(2,1)} %split_state.4), channel_id=1, source_target_pairs={{0,1},{1,0},{2,3},{3,2},{4,5},{5,4},{6,7},{7,6},{8,9},{9,8},{10,11... | collective-permute-start | bytes 1376264 | tf_op jit(solution)/shard_map/ppermute | solution.py:482
  16.3 20.4 %collective-permute-start.4 = (bf16[1,128,1792]{2,1,0:T(8,128)(2,1)}, bf16[1,128,1792]{2,1,0:T(8,128)(2,1)}, u32[]{:S(2)}, u32[]{:S(2)}) collective-permute-start(bf16[1,128,1792]{2,1,0:T(8,128)(2,1)} %split_state.3), channel_id=1, source_target_pairs={{0,1},{1,0},{2,3},{3,2},{4,5},{5,4},{6,7},{7,6},{8,9},{9,8},{10,11... | collective-permute-start | bytes 1376264 | tf_op jit(solution)/shard_map/ppermute | solution.py:482
  18.4 24.0 %all-to-all-start = ((bf16[8,32,2048]{2,1,0:T(8,128)(2,1)}), bf16[8,32,2048]{2,1,0:T(8,128)(2,1)}, u32[]{:S(2)}, u32[]{:S(2)}) async-start(bf16[8,32,2048]{2,1,0:T(8,128)(2,1)} %pack_own.1), calls=%async_computation | async-start | bytes 2097152 | tf_op jit(solution)/shard_map/all_to_all | solution.py:485
  34.0 12.0 %copy-start.3 = (bf16[1,128,3584]{2,1,0:T(8,128)(2,1)S(1)}, bf16[1,128,3584]{2,1,0:T(8,128)(2,1)}, u32[]{:S(2)}) copy-start(bf16[1,128,3584]{2,1,0:T(8,128)(2,1)} %param.15) | copy-start | bytes 2752516
  42.4 17.9 %all-to-all-start.1 = ((bf16[8,32,2048]{2,1,0:T(8,128)(2,1)}), bf16[8,32,2048]{2,1,0:T(8,128)(2,1)S(1)}, u32[]{:S(2)}, u32[]{:S(2)}) async-start(bf16[8,32,2048]{2,1,0:T(8,128)(2,1)} %copy-done.7), calls=%async_computation.1 | async-start | bytes 2097152 | tf_op jit(solution)/shard_map/all_to_all | solution.py:485
  46.1 19.6 %copy-start.2 = (bf16[1,128,3584]{2,1,0:T(8,128)(2,1)S(1)}, bf16[1,128,3584]{2,1,0:T(8,128)(2,1)}, u32[]{:S(2)}) copy-start(bf16[1,128,3584]{2,1,0:T(8,128)(2,1)} %param.14) | copy-start | bytes 2752516
  46.1 12.9 %collective-permute-start.6 = (bf16[1,128,1792]{2,1,0:T(8,128)(2,1)S(1)}, bf16[1,128,1792]{2,1,0:T(8,128)(2,1)S(1)}, u32[]{:S(2)}, u32[]{:S(2)}) collective-permute-start(bf16[1,128,1792]{2,1,0:T(8,128)(2,1)S(1)} %split_state.5), channel_id=1, source_target_pairs={{0,1},{1,0},{2,3},{3,2},{4,5},{5,4},{6,7},{7,6},{8,9},{9,8},{10,11... | collective-permute-start | bytes 1376264 | tf_op jit(solution)/shard_map/ppermute | solution.py:482
  62.1 13.3 %copy-start.11 = (bf16[2,32,1792]{2,1,0:T(8,128)(2,1)}, bf16[2,32,1792]{2,1,0:T(8,128)(2,1)S(1)}, u32[]{:S(2)}) copy-start(bf16[2,32,1792]{2,1,0:T(8,128)(2,1)S(1)} %get-tuple-element.52.refs_0_) | copy-start | bytes 688132
  62.1 8.6 %collective-permute-start.7 = (bf16[2,32,1792]{2,1,0:T(8,128)(2,1)S(1)}, bf16[2,32,1792]{2,1,0:T(8,128)(2,1)S(1)}, u32[]{:S(2)}, u32[]{:S(2)}) collective-permute-start(bf16[2,32,1792]{2,1,0:T(8,128)(2,1)S(1)} %get-tuple-element.46), channel_id=1, source_target_pairs={{0,4},{2,6},{4,0},{6,2},{8,12},{10,14},{12,8},{14,10},{16,20},{18,... | collective-permute-start | bytes 688136 | tf_op jit(solution)/shard_map/ppermute | solution.py:527
  63.7 8.5 %collective-permute-start.8 = (bf16[2,32,1792]{2,1,0:T(8,128)(2,1)S(1)}, bf16[2,32,1792]{2,1,0:T(8,128)(2,1)S(1)}, u32[]{:S(2)}, u32[]{:S(2)}) collective-permute-start(bf16[2,32,1792]{2,1,0:T(8,128)(2,1)S(1)} %get-tuple-element.47), channel_id=1, source_target_pairs={{0,8},{2,10},{4,12},{6,14},{8,0},{10,2},{12,4},{14,6},{16,24},{18,... | collective-permute-start | bytes 688136 | tf_op jit(solution)/shard_map/ppermute | solution.py:527
  64.2 11.2 %collective-permute-start.9 = (bf16[2,32,1792]{2,1,0:T(8,128)(2,1)S(1)}, bf16[2,32,1792]{2,1,0:T(8,128)(2,1)S(1)}, u32[]{:S(2)}, u32[]{:S(2)}) collective-permute-start(bf16[2,32,1792]{2,1,0:T(8,128)(2,1)S(1)} %get-tuple-element.48), channel_id=1, source_target_pairs={{0,12},{2,14},{4,8},{6,10},{8,4},{10,6},{12,0},{14,2},{16,28},{18,... | collective-permute-start | bytes 688136 | tf_op jit(solution)/shard_map/ppermute | solution.py:527
  75.5 6.0 %collective-permute-start.10 = (bf16[4,32,1792]{2,1,0:T(8,128)(2,1)S(1)}, bf16[4,32,1792]{2,1,0:T(8,128)(2,1)S(1)}, u32[]{:S(2)}, u32[]{:S(2)}) collective-permute-start(bf16[4,32,1792]{2,1,0:T(8,128)(2,1)S(1)} %other_core_far.1), channel_id=1, source_target_pairs={{0,2},{2,0},{4,6},{6,4},{8,10},{10,8},{12,14},{14,12},{16,18},{18,... | collective-permute-start | bytes 1376264 | tf_op jit(solution)/shard_map/ppermute | solution.py:527
  76.1 5.3 %copy-start.14 = (bf16[2,32,1792]{2,1,0:T(8,128)(2,1)S(1)}, bf16[2,32,1792]{2,1,0:T(8,128)(2,1)}, u32[]{:S(2)}) copy-start(bf16[2,32,1792]{2,1,0:T(8,128)(2,1)} %copy-done.13) | copy-start | bytes 688132
  76.1 5.3 %copy-start.16 = (bf16[2,32,1792]{2,1,0:T(8,128)(2,1)S(1)}, bf16[2,32,1792]{2,1,0:T(8,128)(2,1)}, u32[]{:S(2)}) copy-start(bf16[2,32,1792]{2,1,0:T(8,128)(2,1)} %copy-done.15) | copy-start | bytes 688132
  76.2 5.3 %copy-start.18 = (bf16[2,32,1792]{2,1,0:T(8,128)(2,1)S(1)}, bf16[2,32,1792]{2,1,0:T(8,128)(2,1)}, u32[]{:S(2)}) copy-start(bf16[2,32,1792]{2,1,0:T(8,128)(2,1)} %copy-done.17) | copy-start | bytes 688132
  76.2 40.0 %all-to-all-start.2 = ((bf16[16,32,1152]{2,1,0:T(8,128)(2,1)}), bf16[16,32,1152]{2,1,0:T(8,128)(2,1)}, u32[]{:S(2)}, u32[]{:S(2)}) async-start(bf16[16,32,1152]{2,1,0:T(8,128)(2,1)} %bitcast.3), calls=%async_computation.2 | async-start | bytes 2359296 | tf_op jit(solution)/shard_map/all_to_all | solution.py:541
  84.9 3.4 %collective-permute-start.11 = (bf16[4,32,1792]{2,1,0:T(8,128)(2,1)S(1)}, bf16[4,32,1792]{2,1,0:T(8,128)(2,1)S(1)}, u32[]{:S(2)}, u32[]{:S(2)}) collective-permute-start(bf16[4,32,1792]{2,1,0:T(8,128)(2,1)S(1)} %get-tuple-element.58), channel_id=1, source_target_pairs={{0,2},{2,0},{4,6},{6,4},{8,10},{10,8},{12,14},{14,12},{16,18},{18,... | collective-permute-start | bytes 1376264 | tf_op jit(solution)/shard_map/ppermute | solution.py:527
  85.7 45.1 %collective-permute-start.15 = (bf16[128,1792]{1,0:T(8,128)(2,1)}, bf16[128,1792]{1,0:T(8,128)(2,1)}, u32[]{:S(2)}, u32[]{:S(2)}) collective-permute-start(bf16[128,1792]{1,0:T(8,128)(2,1)} %combine_far.1), channel_id=1, source_target_pairs={{0,16},{2,18},{4,20},{6,22},{8,24},{10,26},{12,28},{14,30},{16,0},... | collective-permute-start | bytes 1376264 | tf_op jit(solution)/shard_map/ppermute | solution.py:479
  89.2 41.6 %collective-permute-start.12 = (bf16[2,32,1792]{2,1,0:T(8,128)(2,1)}, bf16[2,32,1792]{2,1,0:T(8,128)(2,1)}, u32[]{:S(2)}, u32[]{:S(2)}) collective-permute-start(bf16[2,32,1792]{2,1,0:T(8,128)(2,1)} %get-tuple-element.60), channel_id=1, source_target_pairs={{0,4},{2,6},{4,0},{6,2},{8,12},{10,14},{12,8},{14,10},{16,20},{18,... | collective-permute-start | bytes 688136 | tf_op jit(solution)/shard_map/ppermute | solution.py:527
  90.7 40.1 %collective-permute-start.13 = (bf16[2,32,1792]{2,1,0:T(8,128)(2,1)}, bf16[2,32,1792]{2,1,0:T(8,128)(2,1)}, u32[]{:S(2)}, u32[]{:S(2)}) collective-permute-start(bf16[2,32,1792]{2,1,0:T(8,128)(2,1)} %get-tuple-element.61), channel_id=1, source_target_pairs={{0,8},{2,10},{4,12},{6,14},{8,0},{10,2},{12,4},{14,6},{16,24},{18,... | collective-permute-start | bytes 688136 | tf_op jit(solution)/shard_map/ppermute | solution.py:527
  92.1 38.6 %collective-permute-start.14 = (bf16[2,32,1792]{2,1,0:T(8,128)(2,1)}, bf16[2,32,1792]{2,1,0:T(8,128)(2,1)}, u32[]{:S(2)}, u32[]{:S(2)}) collective-permute-start(bf16[2,32,1792]{2,1,0:T(8,128)(2,1)} %get-tuple-element.62), channel_id=1, source_target_pairs={{0,12},{2,14},{4,8},{6,10},{8,4},{10,6},{12,0},{14,2},{16,28},{18,... | collective-permute-start | bytes 688136 | tf_op jit(solution)/shard_map/ppermute | solution.py:527
  118.5 8.5 %copy-start.10 = (bf16[272,128]{1,0:T(8,128)(2,1)S(1)}, bf16[272,128]{1,0:T(8,128)(2,1)}, u32[]{:S(2)}) copy-start(bf16[272,128]{1,0:T(8,128)(2,1)} %copy-done.9) | copy-start | bytes 208900
  118.5 31.9 %all-to-all-start.3 = ((bf16[32,16,896]{2,1,0:T(8,128)(2,1)}), bf16[32,16,896]{2,1,0:T(8,128)(2,1)}, u32[]{:S(2)}, u32[]{:S(2)}) async-start(bf16[32,16,896]{2,1,0:T(8,128)(2,1)} %route_steps.1), calls=%async_computation.3 | async-start | bytes 1835008 | tf_op jit(solution)/shard_map/all_to_all | solution.py:574
  128.7 6.0 %copy-start.6 = (bf16[128,512]{1,0:T(8,128)(2,1)S(1)}, bf16[128,512]{1,0:T(8,128)(2,1)}, u32[]{:S(2)}) copy-start(bf16[128,512]{1,0:T(8,128)(2,1)} %copy-done.5) | copy-start | bytes 393220
  128.8 6.0 %collective-permute-start.16 = (bf16[256,128]{1,0:T(8,128)(2,1)S(1)}, bf16[256,128]{1,0:T(8,128)(2,1)S(1)}, u32[]{:S(2)}, u32[]{:S(2)}) collective-permute-start(bf16[256,128]{1,0:T(8,128)(2,1)S(1)} %get-tuple-element.69), channel_id=1, source_target_pairs={{0,1},{1,0},{2,3},{3,2},{4,5},{5,4},{6,7},{7,6},{8,9},{9,8},{10,11... | collective-permute-start | bytes 196616 | tf_op jit(solution)/shard_map/ppermute | solution.py:482
  (9 other events, 27.7 us)

commit v2 on v1

--- a/solution.py
+++ b/solution.py
@@ -183,7 +183,7 @@
     return first == second
 
 
-def prepare_body(acts_ref, ids_ref, weights_ref, hidden_ref, far_ref):
+def prepare_body(acts_ref, choices_ref, hidden_ref, far_ref):
     tok = acts_ref.shape[0]
     units = acts_ref.shape[1] // 4
     for choice in range(2):
@@ -193,14 +193,14 @@
         value = (gate * jax.nn.sigmoid(gate) * up).astype(bf16)
         hidden_ref[choice * tok : (choice + 1) * tok, :] = value
         far_ref[choice * tok : (choice + 1) * tok, :] = value
-    weights = weights_ref[...]
+    ids, weights = choices_ref[:, 0:2], choices_ref[:, 2:4]
     high = weights.astype(bf16)
     middle = (weights - high.astype(f32)).astype(bf16)
     low = (weights - high.astype(f32) - middle.astype(f32)).astype(bf16)
     unit = same_index(tok).astype(f32).astype(bf16)
     pieces = [
         lax.dot_general(piece, unit, (((0,), (0,)), ((), ())), preferred_element_type=f32)
-        for piece in (ids_ref[...].astype(f32).astype(bf16), high, middle, low)
+        for piece in (ids.astype(bf16), high, middle, low)
     ]
     blank = jnp.zeros((16 - 8, tok), f32)
     far_ref[2 * tok : 2 * tok + 16, :] = jnp.concatenate(pieces + [blank], axis=0).astype(bf16)
@@ -339,7 +339,8 @@
             first = first_decay * moments[0].astype(f32) + (1.0 - first_decay) * grad
             second = second_decay * moments[1].astype(f32)
             second = second + (1.0 - second_decay) * grad * grad
-            step = (first / (jnp.sqrt(second) + adam_epsilon)).astype(bf16)
+            root = second * lax.rsqrt(second) + adam_epsilon
+            step = (first * pl.reciprocal(root, approx=True)).astype(bf16)
             out_ref[:, part, side * each : (side + 1) * each, 0:narrow] = step.reshape(
                 groups, each, narrow
             )
@@ -493,7 +494,7 @@
     acts = gate_up.reshape(tok, 4 * units)
     hidden, noted = whole_call(
         prepare_body, (shaped(top * tok, units), shaped(top * tok + 16, units)), "prepare"
-    )(acts, expert_ids, route_weights)
+    )(acts, jnp.concatenate([expert_ids.astype(f32), route_weights], axis=1))
     noted_far = mirror(noted)
     hidden_beside = neighbour(hidden)
     hidden_diagonal = lax.ppermute(hidden, ("expert", "hidden"), diagonal)
@@ -550,7 +551,7 @@
     near_far, steps = lax.optimization_barrier((near_far, steps))
     crossing = whole_call(other_core_body, cores[0], "other_core_far")(*near_far)
     combined_send = whole_call(
-        functools.partial(combine_far_body, half), shaped(tok, wide), "combine_far", HEAVY
+        functools.partial(combine_far_body, half), shaped(tok, wide), "combine_far", 105_000_000
     )(noted_far, *near_far, at_distance(crossing, 1))
     combined_far = mirror(combined_send)
     keep_core, send_core = forward(after(recv, combined_send), 0, cores, "forward_own")

time: 153 us -> 149 us (0.974)
  waiting for transfers between devices: 75.3 us -> 70 us
    all_to_all x1, waiting for transfers between devices: 23.4 us -> 19 us  [mirrored_local(): lax.all_to_all(steps.reshape(places, 2 * each, narrow + 2 * units), 'expe...]
    ppermute x8, waiting for transfers between devices: 4.74 us -> 1.72 us  [at_distance(): return lax.ppermute(x, 'expert', [(k, k ^ distance) for k in range(places)])]
    ppermute x3, waiting for transfers between devices: 0.24 us -> 2.71 us  [mirror(): return lax.ppermute(x, 'expert', across)]
    unnamed x42 -> x28, local copies, waits for them, and re-layouts: 4.41 us -> 2.88 us
  transfers between devices with their start and end apart: 21 -> 21, of which waited for: 11 -> 10; matrix products, arithmetic and copies ran while one was open for 2% -> 2% of each run, Pallas kernels for 13% -> 14%
where the time goes in v2:
time: 149 us; the launch traced here: 148 us
  waiting for transfers between devices  70 us (47%)
  starting transfers between devices  46 us (31%)
  Pallas kernels  24.9 us (17%)
  local copies, waits for them, and re-layouts  4.9 us (3%)
  other arithmetic  1.49 us (1%)
    all_to_all x1, waiting for transfers between devices, mirrored_local(): lax.all_to_all(steps.reshape(places, 2 * each, narrow + 2 * units), 'expe...  19 us
    all_to_all x1, waiting for transfers between devices, mirrored_local(): lax.all_to_all(after(routed, combined_send), ('expert', 'hidden'), split_...  15.7 us
    ppermute x5, waiting for transfers between devices, neighbour(): return lax.ppermute(x, 'hidden', beside)  13.9 us
    ppermute x1, waiting for transfers between devices, mirrored_local(): hidden_diagonal = lax.ppermute(hidden, ('expert', 'hidden'), diagonal)  9.69 us
    all_to_all x1, starting transfers between devices, mirrored_local(): lax.all_to_all(after(routed, combined_send), ('expert', 'hidden'), split_...  8.51 us
    all_to_all x2, starting transfers between devices, exchange(): lax.all_to_all(x, 'expert', split_axis=0, concat_axis=0, tiled=True, axis...  7.78 us
    ppermute x8, starting transfers between devices, at_distance(): return lax.ppermute(x, 'expert', [(k, k ^ distance) for k in range(places)])  7.64 us
    all_to_all x2, waiting for transfers between devices, exchange(): lax.all_to_all(x, 'expert', split_axis=0, concat_axis=0, tiled=True, axis...  7.28 us
  transfers between devices with their start and end apart: 21, of which 10 were waited for; matrix products, arithmetic and copies ran while one was open for 2% of the time, Pallas kernels for 14%

profile of v2, /device:TPU:0, one launch (start us, length us, event | category | flops | bytes accessed | tf_op | source)
XLA Modules:
  0.0 148.1 jit_solution(4125709269219683569)
XLA Ops:
  0.6 4.1 %collective-permute-start.3 = (bf16[128,1792]{1,0:T(8,128)(2,1)}, bf16[128,1792]{1,0:T(8,128)(2,1)S(1)}, u32[]{:S(2)}, u32[]{:S(2)}) collective-permute-start(bf16[128,1792]{1,0:T(8,128)(2,1)} %refs_0_.1), channel_id=1, source_target_pairs={{0,16},{2,18},{4,20},{6,22},{8,24},{10,26},{12,28},{14,30},{16,0},... | collective-permute-start | bytes 1376264 | tf_op jit(solution)/shard_map/ppermute | solution.py:480
  7.6 1.8 %collective-permute-start = (bf16[256,128]{1,0:T(8,128)(2,1)S(1)}, bf16[256,128]{1,0:T(8,128)(2,1)S(1)}, u32[]{:S(2)}, u32[]{:S(2)}) collective-permute-start(bf16[256,128]{1,0:T(8,128)(2,1)S(1)} %get-tuple-element.38), channel_id=1, source_target_pairs={{0,1},{1,0},{2,3},{3,2},{4,5},{5,4},{6,7},{7,6},{8,9},{9,8},{10,11... | collective-permute-start | bytes 196616 | tf_op jit(solution)/shard_map/ppermute | solution.py:483
  9.4 2.5 %collective-permute-start.2 = (bf16[256,128]{1,0:T(8,128)(2,1)S(1)}, bf16[256,128]{1,0:T(8,128)(2,1)S(1)}, u32[]{:S(2)}, u32[]{:S(2)}) collective-permute-start(bf16[256,128]{1,0:T(8,128)(2,1)S(1)} %get-tuple-element.38), channel_id=1, source_target_pairs={{0,17},{1,16},{2,19},{3,18},{4,21},{5,20},{6,23},{7,22},{8,25},{9,... | collective-permute-start | bytes 196616 | tf_op jit(solution)/shard_map/ppermute | solution.py:500
  13.9 1.5 %collective-permute-start.5 = (bf16[1,128,1792]{2,1,0:T(8,128)(2,1)}, bf16[1,128,1792]{2,1,0:T(8,128)(2,1)}, u32[]{:S(2)}, u32[]{:S(2)}) collective-permute-start(bf16[1,128,1792]{2,1,0:T(8,128)(2,1)} %split_state.4), channel_id=1, source_target_pairs={{0,1},{1,0},{2,3},{3,2},{4,5},{5,4},{6,7},{7,6},{8,9},{9,8},{10,11... | collective-permute-start | bytes 1376264 | tf_op jit(solution)/shard_map/ppermute | solution.py:483
  16.7 1.6 %pack_own.1 = bf16[8,32,2048]{2,1,0:T(8,128)(2,1)} custom-call(bf16[272,128]{1,0:T(8,128)(2,1)S(1)} %get-tuple-element.37.acts_ref.meta_ref, bf16[256,128]{1,0:T(8,128)(2,1)S(1)} %collective-permute-done.beside_ref, bf16[128,1792]{1,0:T(8,128)(2,1)S(1)} %copy-done.8), custom_call_target="tpu_custom_call" | custom-call | tf_op jit(solution)/shard_map/pack_own/pallas_call | solution.py:512
  18.4 4.2 %all-to-all-start = ((bf16[8,32,2048]{2,1,0:T(8,128)(2,1)}), bf16[8,32,2048]{2,1,0:T(8,128)(2,1)}, u32[]{:S(2)}, u32[]{:S(2)}) async-start(bf16[8,32,2048]{2,1,0:T(8,128)(2,1)} %pack_own.1), calls=%async_computation | async-start | bytes 2097152 | tf_op jit(solution)/shard_map/all_to_all | solution.py:486
  22.6 9.7 %collective-permute-done.2.beside_ref = bf16[256,128]{1,0:T(8,128)(2,1)S(1)} collective-permute-done((bf16[256,128]{1,0:T(8,128)(2,1)S(1)}, bf16[256,128]{1,0:T(8,128)(2,1)S(1)}, u32[]{:S(2)}, u32[]{:S(2)}) %collective-permute-start.2) | collective-permute-done | bytes 65568 | tf_op jit(solution)/shard_map/ppermute | solution.py:500
  34.0 2.6 %collective-permute-done.4.beside_ref.weight_beside = bf16[1,128,1792]{2,1,0:T(8,128)(2,1)} collective-permute-done((bf16[1,128,1792]{2,1,0:T(8,128)(2,1)}, bf16[1,128,1792]{2,1,0:T(8,128)(2,1)}, u32[]{:S(2)}, u32[]{:S(2)}) %collective-permute-start.4) | collective-permute-done | bytes 458784 | tf_op jit(solution)/shard_map/ppermute | solution.py:483
  36.6 5.8 %all-to-all-done.recv_ref = bf16[8,32,2048]{2,1,0:T(8,128)(2,1)} async-done(((bf16[8,32,2048]{2,1,0:T(8,128)(2,1)}), bf16[8,32,2048]{2,1,0:T(8,128)(2,1)}, u32[]{:S(2)}, u32[]{:S(2)}) %all-to-all-start) | async-done | bytes 1048608 | tf_op jit(solution)/shard_map/all_to_all | solution.py:486
  42.4 3.6 %all-to-all-start.1 = ((bf16[8,32,2048]{2,1,0:T(8,128)(2,1)}), bf16[8,32,2048]{2,1,0:T(8,128)(2,1)S(1)}, u32[]{:S(2)}, u32[]{:S(2)}) async-start(bf16[8,32,2048]{2,1,0:T(8,128)(2,1)} %copy-done.7), calls=%async_computation.1 | async-start | bytes 2097152 | tf_op jit(solution)/shard_map/all_to_all | solution.py:486
  46.1 1.7 %collective-permute-start.6 = (bf16[1,128,1792]{2,1,0:T(8,128)(2,1)S(1)}, bf16[1,128,1792]{2,1,0:T(8,128)(2,1)S(1)}, u32[]{:S(2)}, u32[]{:S(2)}) collective-permute-start(bf16[1,128,1792]{2,1,0:T(8,128)(2,1)S(1)} %split_state.5), channel_id=1, source_target_pairs={{0,1},{1,0},{2,3},{3,2},{4,5},{5,4},{6,7},{7,6},{8,9},{9,8},{10,11... | collective-permute-start | bytes 1376264 | tf_op jit(solution)/shard_map/ppermute | solution.py:483
  47.7 11.2 %collective-permute-done.6.second_beside = bf16[1,128,1792]{2,1,0:T(8,128)(2,1)S(1)} collective-permute-done((bf16[1,128,1792]{2,1,0:T(8,128)(2,1)S(1)}, bf16[1,128,1792]{2,1,0:T(8,128)(2,1)S(1)}, u32[]{:S(2)}, u32[]{:S(2)}) %collective-permute-start.6) | collective-permute-done | bytes 458784 | tf_op jit(solution)/shard_map/ppermute | solution.py:483
  58.9 1.4 all-to-all-done.1.recv_ref.far_ref
  60.4 2.5 %forward_far.1 = (bf16[2,32,1792]{2,1,0:T(8,128)(2,1)S(1)}, bf16[2,32,1792]{2,1,0:T(8,128)(2,1)}, bf16[2,32,1792]{2,1,0:T(8,128)(2,1)}, bf16[2,32,1792]{2,1,0:T(8,128)(2,1)}) custom-call(bf16[8,32,2048]{2,1,0:T(8,128)(2,1)S(1)} %all-to-all-done.1.recv_ref.far_ref, bf16[128,3584]{1,0:T(8,128)(2,1)S(1)} %bitcast.11, ...), custom_call_target="tpu_custom_call" | custom-call | tf_op jit(solution)/shard_map/forward_far/pallas_call | solution.py:523
  63.6 1.5 collective-permute-start.7
  65.6 1.5 collective-permute-start.9
  67.1 4.6 %update.1 = bf16[8,2,32,1152]{3,2,1,0:T(8,128)(2,1)} custom-call(bf16[8,32,2048]{2,1,0:T(8,128)(2,1)} %all-to-all-done.recv_ref, bf16[8,32,2048]{2,1,0:T(8,128)(2,1)S(1)} %all-to-all-done.1.recv_ref.far_ref, bf16[128,3584]{1,0:T(8,128)(2,1)S(1)} %bitcast.12, bf16[128,3584]{1,0:T(8,128)(2,1)S(1)} %bitcast.15, bf16[128,3584]{1,0:T(8,128)(2,1)S(1)} %bitcast.17, ...), custom_call_target="tpu_custom_call" | custom-call | tf_op jit(solution)/shard_map/update/pallas_call | solution.py:537
  71.7 5.2 %all-to-all-start.2 = ((bf16[16,32,1152]{2,1,0:T(8,128)(2,1)}), bf16[16,32,1152]{2,1,0:T(8,128)(2,1)S(1)}, u32[]{:S(2)}, u32[]{:S(2)}) async-start(bf16[16,32,1152]{2,1,0:T(8,128)(2,1)} %bitcast.3), calls=%async_computation.2 | async-start | bytes 2359296 | tf_op jit(solution)/shard_map/all_to_all | solution.py:542
  78.7 1.5 %collective-permute-done.10.refs_4_ = bf16[4,32,1792]{2,1,0:T(8,128)(2,1)S(1)} collective-permute-done((bf16[4,32,1792]{2,1,0:T(8,128)(2,1)S(1)}, bf16[4,32,1792]{2,1,0:T(8,128)(2,1)S(1)}, u32[]{:S(2)}, u32[]{:S(2)}) %collective-permute-start.10) | collective-permute-done | bytes 458784 | tf_op jit(solution)/shard_map/ppermute | solution.py:528
  80.2 2.5 %combine_far.1 = bf16[128,1792]{1,0:T(8,128)(2,1)} custom-call(bf16[272,128]{1,0:T(8,128)(2,1)S(1)} %collective-permute-done.1.acts_ref, bf16[2,32,1792]{2,1,0:T(8,128)(2,1)S(1)} %copy-done.12, bf16[2,32,1792]{2,1,0:T(8,128)(2,1)} %collective-permute-done.7.refs_1_, bf16[2,32,1792]{2,1,0:T(8,128)(2,1)} %collective-permute-done.8.refs_2_, ...), custom_call_target="tpu_custom_call" | custom-call | flops 10499999744 | bytes 105000000 | tf_op jit(solution)/shard_map/combine_far/pallas_call | solution.py:553
  82.8 2.0 %forward_own.1 = (bf16[4,32,1792]{2,1,0:T(8,128)(2,1)S(1)}, bf16[4,32,1792]{2,1,0:T(8,128)(2,1)S(1)}) custom-call(bf16[8,32,2048]{2,1,0:T(8,128)(2,1)} %all-to-all-done.recv_ref, bf16[128,3584]{1,0:T(8,128)(2,1)S(1)} %bitcast.13, bf16[1,128,1792]{2,1,0:T(8,128)(2,1)} %collective-permute-done.4.beside_ref.weight_beside), custom_call_target="tpu_custom_call" | custom-call | tf_op jit(solution)/shard_map/forward_own/pallas_call | solution.py:523
  85.5 2.8 %collective-permute-start.15 = (bf16[128,1792]{1,0:T(8,128)(2,1)}, bf16[128,1792]{1,0:T(8,128)(2,1)}, u32[]{:S(2)}, u32[]{:S(2)}) collective-permute-start(bf16[128,1792]{1,0:T(8,128)(2,1)} %combine_far.1), channel_id=1, source_target_pairs={{0,16},{2,18},{4,20},{6,22},{8,24},{10,26},{12,28},{14,30},{16,0},... | collective-permute-start | bytes 1376264 | tf_op jit(solution)/shard_map/ppermute | solution.py:480
  89.2 1.5 collective-permute-start.12
  90.6 1.3 collective-permute-start.13
  92.6 19.0 %all-to-all-done.2.recv_ref = bf16[16,32,1152]{2,1,0:T(8,128)(2,1)S(1)} async-done(((bf16[16,32,1152]{2,1,0:T(8,128)(2,1)}), bf16[16,32,1152]{2,1,0:T(8,128)(2,1)S(1)}, u32[]{:S(2)}, u32[]{:S(2)}) %all-to-all-start.2) | async-done | bytes 1179680 | tf_op jit(solution)/shard_map/all_to_all | solution.py:542
  111.6 1.6 %route_steps.1 = bf16[32,16,896]{2,1,0:T(8,128)(2,1)} custom-call(s32[32]{0:T(128)S(1)} %reshape.26.source_ref, s32[32]{0:T(128)S(1)} %xor.10.line_ref, bf16[16,32,1152]{2,1,0:T(8,128)(2,1)S(1)} %all-to-all-done.2.recv_ref), custom_call_target="tpu_custom_call" | custom-call | tf_op jit(solution)/shard_map/route_steps/pallas_call | solution.py:567
  113.2 8.5 %all-to-all-start.3 = ((bf16[32,16,896]{2,1,0:T(8,128)(2,1)}), bf16[32,16,896]{2,1,0:T(8,128)(2,1)}, u32[]{:S(2)}, u32[]{:S(2)}) async-start(bf16[32,16,896]{2,1,0:T(8,128)(2,1)} %route_steps.1), calls=%async_computation.3 | async-start | bytes 1835008 | tf_op jit(solution)/shard_map/all_to_all | solution.py:575
  122.2 1.8 %collective-permute-start.16 = (bf16[256,128]{1,0:T(8,128)(2,1)S(1)}, bf16[256,128]{1,0:T(8,128)(2,1)S(1)}, u32[]{:S(2)}, u32[]{:S(2)}) collective-permute-start(bf16[256,128]{1,0:T(8,128)(2,1)S(1)} %get-tuple-element.69), channel_id=1, source_target_pairs={{0,1},{1,0},{2,3},{3,2},{4,5},{5,4},{6,7},{7,6},{8,9},{9,8},{10,11... | collective-permute-start | bytes 196616 | tf_op jit(solution)/shard_map/ppermute | solution.py:483
  124.0 2.7 %collective-permute-done.15.far_ref = bf16[128,1792]{1,0:T(8,128)(2,1)} collective-permute-done((bf16[128,1792]{1,0:T(8,128)(2,1)}, bf16[128,1792]{1,0:T(8,128)(2,1)}, u32[]{:S(2)}, u32[]{:S(2)}) %collective-permute-start.15) | collective-permute-done | bytes 458784 | tf_op jit(solution)/shard_map/ppermute | solution.py:480
  126.7 2.7 %combine_own.1 = bf16[128,1792]{1,0:T(8,128)(2,1)} custom-call(bf16[272,128]{1,0:T(8,128)(2,1)S(1)} %copy-done.10, bf16[128,1792]{1,0:T(8,128)(2,1)} %collective-permute-done.15.far_ref, bf16[2,32,1792]{2,1,0:T(8,128)(2,1)S(1)} %get-tuple-element.65.refs_0_, bf16[2,32,1792]{2,1,0:T(8,128)(2,1)} %collective-permute-done.12.refs_1_, ...), custom_call_target="tpu_custom_call" | custom-call | tf_op jit(solution)/shard_map/combine_own/pallas_call | solution.py:590
  130.2 15.7 %all-to-all-done.3 = bf16[32,16,896]{2,1,0:T(8,128)(2,1)} async-done(((bf16[32,16,896]{2,1,0:T(8,128)(2,1)}), bf16[32,16,896]{2,1,0:T(8,128)(2,1)}, u32[]{:S(2)}, u32[]{:S(2)}) %all-to-all-start.3) | async-done | bytes 917536 | tf_op jit(solution)/shard_map/all_to_all | solution.py:575
  145.9 2.2 %place_steps.1 = bf16[128,3584]{1,0:T(8,128)(2,1)} custom-call(bf16[8,2,2,16,896]{4,3,2,1,0:T(8,128)(2,1)} %bitcast.6.recv_ref), custom_call_target="tpu_custom_call" | custom-call | tf_op jit(solution)/shard_map/place_steps/pallas_call | solution.py:593
  (67 shorter events, 14.3 us)
Async XLA Ops:
  0.6 14.8 %copy-start = (bf16[1,128,3584]{2,1,0:T(8,128)(2,1)S(1)}, bf16[1,128,3584]{2,1,0:T(8,128)(2,1)}, u32[]{:S(2)}) copy-start(bf16[1,128,3584]{2,1,0:T(8,128)(2,1)} %param.13) | copy-start | bytes 2752516
  0.6 31.7 %collective-permute-start.3 = (bf16[128,1792]{1,0:T(8,128)(2,1)}, bf16[128,1792]{1,0:T(8,128)(2,1)S(1)}, u32[]{:S(2)}, u32[]{:S(2)}) collective-permute-start(bf16[128,1792]{1,0:T(8,128)(2,1)} %refs_0_.1), channel_id=1, source_target_pairs={{0,16},{2,18},{4,20},{6,22},{8,24},{10,26},{12,28},{14,30},{16,0},... | collective-permute-start | bytes 1376264 | tf_op jit(solution)/shard_map/ppermute | solution.py:480
  5.7 10.5 %copy-start.5 = (bf16[128,512]{1,0:T(8,128)(2,1)}, bf16[128,512]{1,0:T(8,128)(2,1)S(1)}, u32[]{:S(2)}) copy-start(bf16[128,512]{1,0:T(8,128)(2,1)S(1)} %reshape.23.acts_ref) | copy-start | bytes 393220
  7.4 9.3 %copy-start.9 = (bf16[272,128]{1,0:T(8,128)(2,1)}, bf16[272,128]{1,0:T(8,128)(2,1)S(1)}, u32[]{:S(2)}) copy-start(bf16[272,128]{1,0:T(8,128)(2,1)S(1)} %get-tuple-element.37.acts_ref.meta_ref) | copy-start | bytes 208900
  7.5 24.8 %collective-permute-start.1 = (bf16[272,128]{1,0:T(8,128)(2,1)S(1)}, bf16[272,128]{1,0:T(8,128)(2,1)S(1)}, u32[]{:S(2)}, u32[]{:S(2)}) collective-permute-start(bf16[272,128]{1,0:T(8,128)(2,1)S(1)} %get-tuple-element.37.acts_ref.meta_ref), channel_id=1, source_target_pairs={{0,16},{2,18},{4,20},{6,22},{8,24},{10,26},{12,28},{14,30},{16,0},... | collective-permute-start | bytes 208904 | tf_op jit(solution)/shard_map/ppermute | solution.py:480
  7.6 8.6 %collective-permute-start = (bf16[256,128]{1,0:T(8,128)(2,1)S(1)}, bf16[256,128]{1,0:T(8,128)(2,1)S(1)}, u32[]{:S(2)}, u32[]{:S(2)}) collective-permute-start(bf16[256,128]{1,0:T(8,128)(2,1)S(1)} %get-tuple-element.38), channel_id=1, source_target_pairs={{0,1},{1,0},{2,3},{3,2},{4,5},{5,4},{6,7},{7,6},{8,9},{9,8},{10,11... | collective-permute-start | bytes 196616 | tf_op jit(solution)/shard_map/ppermute | solution.py:483
  9.4 22.9 %collective-permute-start.2 = (bf16[256,128]{1,0:T(8,128)(2,1)S(1)}, bf16[256,128]{1,0:T(8,128)(2,1)S(1)}, u32[]{:S(2)}, u32[]{:S(2)}) collective-permute-start(bf16[256,128]{1,0:T(8,128)(2,1)S(1)} %get-tuple-element.38), channel_id=1, source_target_pairs={{0,17},{1,16},{2,19},{3,18},{4,21},{5,20},{6,23},{7,22},{8,25},{9,... | collective-permute-start | bytes 196616 | tf_op jit(solution)/shard_map/ppermute | solution.py:500
  13.1 3.6 %copy-start.8 = (bf16[128,1792]{1,0:T(8,128)(2,1)S(1)}, bf16[128,1792]{1,0:T(8,128)(2,1)}, u32[]{:S(2)}) copy-start(bf16[128,1792]{1,0:T(8,128)(2,1)} %refs_0_.1) | copy-start | bytes 1376260
  13.9 20.1 %collective-permute-start.5 = (bf16[1,128,1792]{2,1,0:T(8,128)(2,1)}, bf16[1,128,1792]{2,1,0:T(8,128)(2,1)}, u32[]{:S(2)}, u32[]{:S(2)}) collective-permute-start(bf16[1,128,1792]{2,1,0:T(8,128)(2,1)} %split_state.4), channel_id=1, source_target_pairs={{0,1},{1,0},{2,3},{3,2},{4,5},{5,4},{6,7},{7,6},{8,9},{9,8},{10,11... | collective-permute-start | bytes 1376264 | tf_op jit(solution)/shard_map/ppermute | solution.py:483
  16.2 20.4 %collective-permute-start.4 = (bf16[1,128,1792]{2,1,0:T(8,128)(2,1)}, bf16[1,128,1792]{2,1,0:T(8,128)(2,1)}, u32[]{:S(2)}, u32[]{:S(2)}) collective-permute-start(bf16[1,128,1792]{2,1,0:T(8,128)(2,1)} %split_state.3), channel_id=1, source_target_pairs={{0,1},{1,0},{2,3},{3,2},{4,5},{5,4},{6,7},{7,6},{8,9},{9,8},{10,11... | collective-permute-start | bytes 1376264 | tf_op jit(solution)/shard_map/ppermute | solution.py:483
  18.4 24.1 %all-to-all-start = ((bf16[8,32,2048]{2,1,0:T(8,128)(2,1)}), bf16[8,32,2048]{2,1,0:T(8,128)(2,1)}, u32[]{:S(2)}, u32[]{:S(2)}) async-start(bf16[8,32,2048]{2,1,0:T(8,128)(2,1)} %pack_own.1), calls=%async_computation | async-start | bytes 2097152 | tf_op jit(solution)/shard_map/all_to_all | solution.py:486
  34.0 12.1 %copy-start.3 = (bf16[1,128,3584]{2,1,0:T(8,128)(2,1)S(1)}, bf16[1,128,3584]{2,1,0:T(8,128)(2,1)}, u32[]{:S(2)}) copy-start(bf16[1,128,3584]{2,1,0:T(8,128)(2,1)} %param.15) | copy-start | bytes 2752516
  42.4 17.9 %all-to-all-start.1 = ((bf16[8,32,2048]{2,1,0:T(8,128)(2,1)}), bf16[8,32,2048]{2,1,0:T(8,128)(2,1)S(1)}, u32[]{:S(2)}, u32[]{:S(2)}) async-start(bf16[8,32,2048]{2,1,0:T(8,128)(2,1)} %copy-done.7), calls=%async_computation.1 | async-start | bytes 2097152 | tf_op jit(solution)/shard_map/all_to_all | solution.py:486
  46.1 21.0 %copy-start.2 = (bf16[1,128,3584]{2,1,0:T(8,128)(2,1)S(1)}, bf16[1,128,3584]{2,1,0:T(8,128)(2,1)}, u32[]{:S(2)}) copy-start(bf16[1,128,3584]{2,1,0:T(8,128)(2,1)} %param.14) | copy-start | bytes 2752516
  46.1 12.9 %collective-permute-start.6 = (bf16[1,128,1792]{2,1,0:T(8,128)(2,1)S(1)}, bf16[1,128,1792]{2,1,0:T(8,128)(2,1)S(1)}, u32[]{:S(2)}, u32[]{:S(2)}) collective-permute-start(bf16[1,128,1792]{2,1,0:T(8,128)(2,1)S(1)} %split_state.5), channel_id=1, source_target_pairs={{0,1},{1,0},{2,3},{3,2},{4,5},{5,4},{6,7},{7,6},{8,9},{9,8},{10,11... | collective-permute-start | bytes 1376264 | tf_op jit(solution)/shard_map/ppermute | solution.py:483
  60.4 6.7 %copy-start.4 = (bf16[1,128,3584]{2,1,0:T(8,128)(2,1)S(1)}, bf16[1,128,3584]{2,1,0:T(8,128)(2,1)}, u32[]{:S(2)}) copy-start(bf16[1,128,3584]{2,1,0:T(8,128)(2,1)} %param.15) | copy-start | bytes 2752516
  63.6 13.4 %collective-permute-start.7 = (bf16[2,32,1792]{2,1,0:T(8,128)(2,1)}, bf16[2,32,1792]{2,1,0:T(8,128)(2,1)}, u32[]{:S(2)}, u32[]{:S(2)}) collective-permute-start(bf16[2,32,1792]{2,1,0:T(8,128)(2,1)} %get-tuple-element.46), channel_id=1, source_target_pairs={{0,4},{2,6},{4,0},{6,2},{8,12},{10,14},{12,8},{14,10},{16,20},{18,... | collective-permute-start | bytes 688136 | tf_op jit(solution)/shard_map/ppermute | solution.py:528
  65.1 11.9 %collective-permute-start.8 = (bf16[2,32,1792]{2,1,0:T(8,128)(2,1)}, bf16[2,32,1792]{2,1,0:T(8,128)(2,1)}, u32[]{:S(2)}, u32[]{:S(2)}) collective-permute-start(bf16[2,32,1792]{2,1,0:T(8,128)(2,1)} %get-tuple-element.47), channel_id=1, source_target_pairs={{0,8},{2,10},{4,12},{6,14},{8,0},{10,2},{12,4},{14,6},{16,24},{18,... | collective-permute-start | bytes 688136 | tf_op jit(solution)/shard_map/ppermute | solution.py:528
  65.6 11.5 %collective-permute-start.9 = (bf16[2,32,1792]{2,1,0:T(8,128)(2,1)}, bf16[2,32,1792]{2,1,0:T(8,128)(2,1)}, u32[]{:S(2)}, u32[]{:S(2)}) collective-permute-start(bf16[2,32,1792]{2,1,0:T(8,128)(2,1)} %get-tuple-element.48), channel_id=1, source_target_pairs={{0,12},{2,14},{4,8},{6,10},{8,4},{10,6},{12,0},{14,2},{16,28},{18,... | collective-permute-start | bytes 688136 | tf_op jit(solution)/shard_map/ppermute | solution.py:528
  71.7 5.4 %copy-start.12 = (bf16[2,32,1792]{2,1,0:T(8,128)(2,1)S(1)}, bf16[2,32,1792]{2,1,0:T(8,128)(2,1)}, u32[]{:S(2)}) copy-start(bf16[2,32,1792]{2,1,0:T(8,128)(2,1)} %copy-done.11) | copy-start | bytes 688132
  71.7 39.9 %all-to-all-start.2 = ((bf16[16,32,1152]{2,1,0:T(8,128)(2,1)}), bf16[16,32,1152]{2,1,0:T(8,128)(2,1)S(1)}, u32[]{:S(2)}, u32[]{:S(2)}) async-start(bf16[16,32,1152]{2,1,0:T(8,128)(2,1)} %bitcast.3), calls=%async_computation.2 | async-start | bytes 2359296 | tf_op jit(solution)/shard_map/all_to_all | solution.py:542
  78.4 1.9 %collective-permute-start.10 = (bf16[4,32,1792]{2,1,0:T(8,128)(2,1)S(1)}, bf16[4,32,1792]{2,1,0:T(8,128)(2,1)S(1)}, u32[]{:S(2)}, u32[]{:S(2)}) collective-permute-start(bf16[4,32,1792]{2,1,0:T(8,128)(2,1)S(1)} %other_core_far.1), channel_id=1, source_target_pairs={{0,2},{2,0},{4,6},{6,4},{8,10},{10,8},{12,14},{14,12},{16,18},{18,... | collective-permute-start | bytes 1376264 | tf_op jit(solution)/shard_map/ppermute | solution.py:528
  82.8 2.3 %copy-start.13 = (s32[8,2]{0,1:T(2,128)S(1)}, s32[8,2]{0,1:T(2,128)}, u32[]{:S(2)}) copy-start(s32[8,2]{0,1:T(2,128)} %param.8) | copy-start | bytes 196
  84.8 3.5 %collective-permute-start.11 = (bf16[4,32,1792]{2,1,0:T(8,128)(2,1)S(1)}, bf16[4,32,1792]{2,1,0:T(8,128)(2,1)S(1)}, u32[]{:S(2)}, u32[]{:S(2)}) collective-permute-start(bf16[4,32,1792]{2,1,0:T(8,128)(2,1)S(1)} %get-tuple-element.58), channel_id=1, source_target_pairs={{0,2},{2,0},{4,6},{6,4},{8,10},{10,8},{12,14},{14,12},{16,18},{18,... | collective-permute-start | bytes 1376264 | tf_op jit(solution)/shard_map/ppermute | solution.py:528
  85.5 41.3 %collective-permute-start.15 = (bf16[128,1792]{1,0:T(8,128)(2,1)}, bf16[128,1792]{1,0:T(8,128)(2,1)}, u32[]{:S(2)}, u32[]{:S(2)}) collective-permute-start(bf16[128,1792]{1,0:T(8,128)(2,1)} %combine_far.1), channel_id=1, source_target_pairs={{0,16},{2,18},{4,20},{6,22},{8,24},{10,26},{12,28},{14,30},{16,0},... | collective-permute-start | bytes 1376264 | tf_op jit(solution)/shard_map/ppermute | solution.py:480
  89.2 37.6 %collective-permute-start.12 = (bf16[2,32,1792]{2,1,0:T(8,128)(2,1)}, bf16[2,32,1792]{2,1,0:T(8,128)(2,1)}, u32[]{:S(2)}, u32[]{:S(2)}) collective-permute-start(bf16[2,32,1792]{2,1,0:T(8,128)(2,1)} %get-tuple-element.60), channel_id=1, source_target_pairs={{0,4},{2,6},{4,0},{6,2},{8,12},{10,14},{12,8},{14,10},{16,20},{18,... | collective-permute-start | bytes 688136 | tf_op jit(solution)/shard_map/ppermute | solution.py:528
  90.6 36.1 %collective-permute-start.13 = (bf16[2,32,1792]{2,1,0:T(8,128)(2,1)}, bf16[2,32,1792]{2,1,0:T(8,128)(2,1)}, u32[]{:S(2)}, u32[]{:S(2)}) collective-permute-start(bf16[2,32,1792]{2,1,0:T(8,128)(2,1)} %get-tuple-element.61), channel_id=1, source_target_pairs={{0,8},{2,10},{4,12},{6,14},{8,0},{10,2},{12,4},{14,6},{16,24},{18,... | collective-permute-start | bytes 688136 | tf_op jit(solution)/shard_map/ppermute | solution.py:528
  92.0 34.8 %collective-permute-start.14 = (bf16[2,32,1792]{2,1,0:T(8,128)(2,1)}, bf16[2,32,1792]{2,1,0:T(8,128)(2,1)}, u32[]{:S(2)}, u32[]{:S(2)}) collective-permute-start(bf16[2,32,1792]{2,1,0:T(8,128)(2,1)} %get-tuple-element.62), channel_id=1, source_target_pairs={{0,12},{2,14},{4,8},{6,10},{8,4},{10,6},{12,0},{14,2},{16,28},{18,... | collective-permute-start | bytes 688136 | tf_op jit(solution)/shard_map/ppermute | solution.py:528
  113.2 8.5 %copy-start.10 = (bf16[272,128]{1,0:T(8,128)(2,1)S(1)}, bf16[272,128]{1,0:T(8,128)(2,1)}, u32[]{:S(2)}) copy-start(bf16[272,128]{1,0:T(8,128)(2,1)} %copy-done.9) | copy-start | bytes 208900
  113.2 32.7 %all-to-all-start.3 = ((bf16[32,16,896]{2,1,0:T(8,128)(2,1)}), bf16[32,16,896]{2,1,0:T(8,128)(2,1)}, u32[]{:S(2)}, u32[]{:S(2)}) async-start(bf16[32,16,896]{2,1,0:T(8,128)(2,1)} %route_steps.1), calls=%async_computation.3 | async-start | bytes 1835008 | tf_op jit(solution)/shard_map/all_to_all | solution.py:575
  122.2 7.2 %copy-start.6 = (bf16[128,512]{1,0:T(8,128)(2,1)S(1)}, bf16[128,512]{1,0:T(8,128)(2,1)}, u32[]{:S(2)}) copy-start(bf16[128,512]{1,0:T(8,128)(2,1)} %copy-done.5) | copy-start | bytes 393220
  122.2 7.2 %collective-permute-start.16 = (bf16[256,128]{1,0:T(8,128)(2,1)S(1)}, bf16[256,128]{1,0:T(8,128)(2,1)S(1)}, u32[]{:S(2)}, u32[]{:S(2)}) collective-permute-start(bf16[256,128]{1,0:T(8,128)(2,1)S(1)} %get-tuple-element.69), channel_id=1, source_target_pairs={{0,1},{1,0},{2,3},{3,2},{4,5},{5,4},{6,7},{7,6},{8,9},{9,8},{10,11... | collective-permute-start | bytes 196616 | tf_op jit(solution)/shard_map/ppermute | solution.py:483
  (3 other events, 2.8 us)

commit v3 on v2

--- a/solution.py
+++ b/solution.py
@@ -206,11 +206,11 @@
     far_ref[2 * tok : 2 * tok + 16, :] = jnp.concatenate(pieces + [blank], axis=0).astype(bf16)
 
 
-def split_body(*refs):
-    out_ref = refs[-1]
+def split_body(ref, keep_ref, other_ref):
     side = lax.axis_index("hidden")
-    for k, ref in enumerate(refs[:-1]):
-        out_ref[k] = columns_at(ref, 1 - side, ref.shape[1] // 2)
+    wide = ref.shape[1] // 2
+    keep_ref[0] = columns_at(ref, side, wide)
+    other_ref[0] = columns_at(ref, 1 - side, wide)
 
 
 def read_meta(ref):
@@ -267,24 +267,44 @@
     return lax.rem(lax.axis_index("expert"), half)
 
 
-def forward_body(half, block, recv_ref, weight_ref, beside_ref, *out_refs):
-    cap, wide = out_refs[0].shape[-2:]
-    units = weight_ref.shape[0]
+def output_rows(half, recv_ref, weight_ref, beside_ref, cap):
+    units, wide = weight_ref.shape[1:]
     me = place_in_half(half)
     acts = jnp.concatenate([recv_ref[me ^ r, :, wide:] for r in range(half)], axis=0)
-    total = jnp.dot(
-        acts[:, :units],
-        columns_at(weight_ref, lax.axis_index("hidden"), wide),
-        preferred_element_type=f32,
-    )
+    total = jnp.dot(acts[:, :units], weight_ref[0], preferred_element_type=f32)
     total = total + jnp.dot(acts[:, units:], beside_ref[0], preferred_element_type=f32)
-    total = total.astype(bf16).reshape(half // 2, 2, cap, wide)
-    if block == 1:
-        for distance, ref in enumerate(out_refs):
-            ref[...] = total[distance]
-    else:
-        for core, ref in enumerate(out_refs):
-            ref[...] = total[:, core]
+    return total.astype(bf16).reshape(half // 2, 2, cap, wide)
+
+
+def forward_far_body(half, recv_ref, weight_ref, beside_ref, *out_refs):
+    total = output_rows(half, recv_ref, weight_ref, beside_ref, out_refs[0].shape[1])
+    for distance, ref in enumerate(out_refs):
+        ref[...] = total[distance]
+
+
+def forward_own_body(half, recv_ref, weight_ref, beside_ref, grads_ref, mirror_ref, *out_refs):
+    total = output_rows(half, recv_ref, weight_ref, beside_ref, out_refs[0].shape[1])
+    wide = total.shape[3]
+    units = grads_ref.shape[2]
+    me = place_in_half(half)
+    for core, out_ref in enumerate(out_refs):
+        out_ref[:, :, 0:wide] = total[:, core]
+        for distance in range(half // 2):
+            source = me ^ (2 * distance + core)
+            out_ref[distance, :, wide : wide + units] = grads_ref[source]
+            out_ref[distance, :, wide + units :] = mirror_ref[source]
+
+
+def grad_rows_body(recv_ref, weight_ref, beside_ref, out_ref):
+    units, wide = weight_ref.shape[1:]
+    scaled = rows_of(recv_ref, 0, wide)
+    for part, weight in enumerate((weight_ref[0], beside_ref[0])):
+        rows = lax.dot_general(
+            scaled, weight, (((1,), (1,)), ((), ())), preferred_element_type=f32
+        )
+        out_ref[:, :, part * units : (part + 1) * units] = rows.astype(bf16).reshape(
+            out_ref.shape[:2] + (units,)
+        )
 
 
 def join_cores_body(keep_ref, got_ref, *out_refs):
@@ -300,41 +320,25 @@
 
 
 def update_body(
-    half,
-    recv_ref,
-    far_ref,
-    weight_ref,
-    first_ref,
-    second_ref,
-    weight_beside,
-    first_beside,
-    second_beside,
-    out_ref,
+    recv_ref, far_ref, first_ref, second_ref, first_beside, second_beside, out_ref
 ):
     _, units, wide = first_beside.shape
-    level, here = level_and_side(half)
     groups = out_ref.shape[0]
     narrow = wide // 2
     each = units // groups
-    acts = jnp.concatenate([rows_of(ref, wide, 2 * units) for ref in (recv_ref, far_ref)], axis=0)
-    scaled = jnp.concatenate([rows_of(ref, 0, wide) for ref in (recv_ref, far_ref)], axis=0)
     for part in range(2):
-        grads = lax.dot_general(
-            acts,
-            scaled[:, part * narrow : (part + 1) * narrow],
-            (((0,), (0,)), ((), ())),
-            preferred_element_type=f32,
-        )
+        grads = None
+        for ref in (recv_ref, far_ref):
+            more = lax.dot_general(
+                rows_of(ref, wide, 2 * units),
+                rows_of(ref, part * narrow, narrow),
+                (((0,), (0,)), ((), ())),
+                preferred_element_type=f32,
+            )
+            grads = more if grads is None else grads + more
         for side in range(2):
-            if side == 0:
-                moments = [
-                    columns_at(ref, 2 * here + part, narrow) for ref in (first_ref, second_ref)
-                ]
-            else:
-                moments = [
-                    ref[0, :, part * narrow : (part + 1) * narrow]
-                    for ref in (first_beside, second_beside)
-                ]
+            own = (first_ref, second_ref) if side == 0 else (first_beside, second_beside)
+            moments = [ref[0, :, part * narrow : (part + 1) * narrow] for ref in own]
             grad = grads[side * units : (side + 1) * units]
             first = first_decay * moments[0].astype(f32) + (1.0 - first_decay) * grad
             second = second_decay * moments[1].astype(f32)
@@ -344,17 +348,6 @@
             out_ref[:, part, side * each : (side + 1) * each, 0:narrow] = step.reshape(
                 groups, each, narrow
             )
-    own = columns_at(weight_ref, here, wide)
-    for part, weight in enumerate((own, weight_beside[0])):
-        rows = lax.dot_general(
-            scaled, weight, (((1,), (1,)), ((), ())), preferred_element_type=f32
-        ).astype(bf16)
-        rows = rows.reshape(2, half // 2, 2, -1, units)
-        at = narrow + part * units
-        for block, place in enumerate((level, 1 - level)):
-            lines = pl.ds(place * (half // 2), half // 2)
-            for odd in range(2):
-                out_ref[lines, odd, :, at : at + units] = rows[block, :, odd]
 
 
 def combine_far_body(half, acts_ref, *refs):
@@ -365,23 +358,30 @@
     out_ref[...] = combined(half, acts_ref, pieces, out_ref.shape[0]).astype(bf16)
 
 
-def combine_own_body(half, acts_ref, far_ref, *refs):
+def combine_own_body(half, acts_ref, chosen_ref, far_ref, *refs):
     out_ref = refs[-1]
-    pieces = [ref[core] for ref in refs[:-1] for core in range(2)]
-    total = combined(half, acts_ref, pieces, out_ref.shape[0])
+    tok, wide = out_ref.shape
+    pieces = [ref[core, :, 0:wide] for ref in refs[:-1] for core in range(2)]
+    _, weights = read_meta(acts_ref)
+    total = weighted_sum(chosen_ref[...], weights, jnp.concatenate(pieces, axis=0), tok)
     out_ref[...] = (total + far_ref[...].astype(f32)).astype(bf16)
 
 
-def combined(half, acts_ref, pieces, tok):
-    cap = pieces[0].shape[0]
+def choose_body(half, acts_ref, chosen_ref):
+    ids, _ = read_meta(acts_ref)
+    chosen_ref[...] = returned_choice(half, ids, chosen_ref.shape[0] // half)
+
+
+def returned_choice(half, ids, cap):
     level, _ = level_and_side(half)
-    diagonal = same_index(tok)
-    ids, weights = read_meta(acts_ref)
     ids = ids.astype(jnp.int32) - half * level
     inside = (ids >= 0) & (ids < half)
     bin_of = jnp.where(inside, ids ^ place_in_half(half), -1).astype(f32)
-    chosen = slot_choice(bin_of, half, cap).astype(f32).astype(bf16)
-    rows = jnp.concatenate(pieces, axis=0)
+    return slot_choice(bin_of, half, cap).astype(f32).astype(bf16)
+
+
+def weighted_sum(chosen, weights, rows, tok):
+    diagonal = same_index(tok)
     total = None
     for choice in range(2):
         picked = lax.dot_general(
@@ -396,16 +396,33 @@
     return total
 
 
-def pick_grads_body(meta_ref, recv_ref, own_ref, send_ref):
-    places, rows, total_wide = recv_ref.shape
+def combined(half, acts_ref, pieces, tok):
+    ids, weights = read_meta(acts_ref)
+    chosen = returned_choice(half, ids, pieces[0].shape[0])
+    return weighted_sum(chosen, weights, jnp.concatenate(pieces, axis=0), tok)
+
+
+def pick_grads_body(half, meta_ref, *refs):
+    near_refs, own_ref, send_ref = refs[:-2], refs[-2], refs[-1]
     units = own_ref.shape[1]
+    _, cap, total_wide = near_refs[0].shape
+    wide = total_wide - 4 * units
+    level, _ = level_and_side(half)
     ids, _ = read_meta(meta_ref)
-    chosen = slot_choice(ids, places, rows).astype(f32).astype(bf16)
+    upper = (ids >= half).astype(jnp.int32)
+    place = (ids.astype(jnp.int32) - half * upper) ^ place_in_half(half)
+    bin_of = (2 * place + (upper ^ level)).astype(f32)
+    chosen = slot_choice(bin_of, 2 * half, cap).astype(f32).astype(bf16)
     for part, out_ref in enumerate((own_ref, send_ref)):
-        at = total_wide - (2 - part) * units
+        pieces = []
+        for ref in near_refs:
+            for core in range(2):
+                for expert in range(2):
+                    at = wide + (2 * expert + part) * units
+                    pieces.append(ref[core, :, at : at + units])
         picked = lax.dot_general(
             chosen,
-            recv_ref[:, :, at : at + units].reshape(places * rows, units),
+            jnp.concatenate(pieces, axis=0),
             (((0,), (0,)), ((), ())),
             preferred_element_type=f32,
         )
@@ -499,11 +516,13 @@
     hidden_beside = neighbour(hidden)
     hidden_diagonal = lax.ppermute(hidden, ("expert", "hidden"), diagonal)
 
-    state = (down_weight[0], first_moment[0], second_moment[0])
-    split = whole_call(split_body, shaped(1, units, wide), "split_state")
-    weight_beside = neighbour(split(state[0]))
-    first_beside = neighbour(split(after(state[1], hidden)))
-    second_beside = neighbour(split(after(state[2], hidden)))
+    split = whole_call(split_body, (shaped(1, units, wide),) * 2, "split_state")
+    weight, weight_other = split(down_weight[0])
+    first, first_other = split(after(first_moment[0], hidden))
+    second, second_other = split(after(second_moment[0], hidden))
+    weight_beside = neighbour(weight_other)
+    first_beside = neighbour(first_other)
+    second_beside = neighbour(second_other)
 
     row = wide + 2 * units
     pack = functools.partial(
@@ -517,12 +536,11 @@
         (recv, packed_far, weight_beside, first_beside)
     )
     recv_far = exchange(packed_far)
-    recv_far, second_beside = lax.optimization_barrier((recv_far, second_beside))
-
-    def forward(rows, block, shape, name):
-        return whole_call(functools.partial(forward_body, half, block), shape, name)(
-            rows, state[0], weight_beside
-        )
+    grad_rows = whole_call(grad_rows_body, shaped(half, cap, 2 * units), "grad_rows")
+    rows_own = grad_rows(recv, weight, weight_beside)
+    recv_far, second_beside, rows_own = lax.optimization_barrier(
+        (recv_far, second_beside, rows_own)
+    )
 
     def at_distance(x, distance):
         return lax.ppermute(x, "expert", [(k, k ^ distance) for k in range(places)])
@@ -531,16 +549,18 @@
         return [outputs[0]] + [at_distance(outputs[k], 2 * k) for k in range(1, half // 2)]
 
     pairs = (shaped(2, cap, wide),) * (half // 2)
-    cores = (shaped(half // 2, cap, wide),) * 2
-
-    outputs_far = forward(recv_far, 1, pairs, "forward_far")
-    steps = whole_call(
-        functools.partial(update_body, half),
-        shaped(half, 2, 2 * each, narrow + 2 * units),
-        "update",
-    )(recv, after(recv_far, outputs_far), *state, weight_beside, first_beside, second_beside)
+    extended = wide + 4 * units
+    outputs_far = whole_call(functools.partial(forward_far_body, half), pairs, "forward_far")(
+        recv_far, weight, weight_beside
+    )
+
+    rows_send = grad_rows(recv_far, weight, weight_beside)
+    rows_mirror = mirror(rows_send)
+    steps = whole_call(update_body, shaped(half, 2, 2 * each, narrow), "update")(
+        recv, after(recv_far, outputs_far, rows_send), first, second, first_beside, second_beside
+    )
     spread = lax.all_to_all(
-        steps.reshape(places, 2 * each, narrow + 2 * units),
+        steps.reshape(places, 2 * each, narrow),
         "expert",
         split_axis=0,
         concat_axis=0,
@@ -548,14 +568,20 @@
     )
 
     near_far = by_chip(outputs_far)
-    near_far, steps = lax.optimization_barrier((near_far, steps))
-    crossing = whole_call(other_core_body, cores[0], "other_core_far")(*near_far)
+    near_far, rows_mirror = lax.optimization_barrier((near_far, rows_mirror, steps))[:2]
+    crossing = whole_call(
+        other_core_body, shaped(half // 2, cap, wide), "other_core_far"
+    )(*near_far)
     combined_send = whole_call(
-        functools.partial(combine_far_body, half), shaped(tok, wide), "combine_far", 105_000_000
+        functools.partial(combine_far_body, half), shaped(tok, wide), "combine_far", 55_000_000
     )(noted_far, *near_far, at_distance(crossing, 1))
     combined_far = mirror(combined_send)
-    keep_core, send_core = forward(after(recv, combined_send), 0, cores, "forward_own")
-    joined = whole_call(join_cores_body, pairs, "join_cores")(
+    keep_core, send_core = whole_call(
+        functools.partial(forward_own_body, half),
+        (shaped(half // 2, cap, extended),) * 2,
+        "forward_own",
+    )(after(recv, combined_send), weight, weight_beside, rows_own, rows_mirror)
+    joined = whole_call(join_cores_body, (shaped(2, cap, extended),) * (half // 2), "join_cores")(
         keep_core, at_distance(send_core, 1)
     )
     near = by_chip(joined)
@@ -576,20 +602,21 @@
         after(routed, combined_send), ("expert", "hidden"), split_axis=0, concat_axis=0, tiled=True
     )
 
-    rows_own, rows_send = whole_call(
-        pick_grads_body,
+    chosen = whole_call(
+        functools.partial(choose_body, half), shaped(half * cap, top * tok), "choose", HEAVY
+    )(after(noted, spread))
+    near, combined_far, chosen = lax.optimization_barrier((near, combined_far, chosen))
+    grads_own, grads_send = whole_call(
+        functools.partial(pick_grads_body, half),
         (shaped(top * tok, units, dtype=f32), shaped(top * tok, units)),
         "pick_grads",
-        HEAVY,
-    )(noted, spread)
+    )(noted, *near)
     grad_gate_up = whole_call(gate_grads_body, shaped(tok, 4 * units), "gate_grads")(
-        acts, rows_own, neighbour(rows_send)
+        acts, grads_own, neighbour(grads_send)
     ).reshape(gate_up.shape)
-
-    near, combined_far = lax.optimization_barrier((near, combined_far, rows_own))[:2]
     combined = whole_call(
         functools.partial(combine_own_body, half), shaped(tok, wide), "combine_own"
-    )(noted, combined_far, *near)
+    )(noted, chosen, combined_far, *near)
     adam_step = whole_call(place_steps_body, shaped(units, 2 * wide), "place_steps")(
         placed.reshape(half, 2, 2, each, narrow)
     )

time: 149 us -> 145 us (0.973)
  waiting for transfers between devices: 70 us -> 54.5 us
  starting transfers between devices: 46 us -> 53.8 us
  Pallas kernels: 24.9 us -> 28.9 us
    all_to_all x1, waiting for transfers between devices: 19 us -> 5.24 us  [mirrored_local(): lax.all_to_all(steps.reshape(places, 2 * each, narrow), 'expert', split_a...]
    all_to_all x1, starting transfers between devices: 8.51 us -> 16 us  [mirrored_local(): lax.all_to_all(after(routed, combined_send), ('expert', 'hidden'), split_...]
    pallas_call x9 -> x12, Pallas kernels: 13.4 us -> 17.3 us  [the longest x1 3.6 us: mirrored_local(): whole_call(update_body, shaped(half, 2, 2 * each, narrow), 'update')]
    all_to_all x1, waiting for transfers between devices: 15.7 us -> 12 us  [mirrored_local(): lax.all_to_all(after(routed, combined_send), ('expert', 'hidden'), split_...]
    ppermute x5, waiting for transfers between devices: 13.9 us -> 11.6 us  [neighbour(): return lax.ppermute(x, 'hidden', beside)]
    ppermute x3 -> x4, waiting for transfers between devices: 2.71 us -> 4.87 us  [mirror(): return lax.ppermute(x, 'expert', across)]
    ppermute x3 -> x4, starting transfers between devices: 7.02 us -> 9 us  [mirror(): return lax.ppermute(x, 'expert', across)]
    unnamed x28 -> x32, local copies, waits for them, and re-layouts: 2.88 us -> 3.85 us
  transfers between devices with their start and end apart: 21 -> 22, of which waited for: 10 -> 11; matrix products, arithmetic and copies ran while one was open for 2% -> 1% of each run, Pallas kernels for 14% -> 17%
where the time goes in v3:
time: 145 us; the launch traced here: 144 us
  waiting for transfers between devices  54.5 us (38%)
  starting transfers between devices  53.8 us (37%)
  Pallas kernels  28.9 us (20%)
  local copies, waits for them, and re-layouts  5.86 us (4%)
    all_to_all x1, starting transfers between devices, mirrored_local(): lax.all_to_all(after(routed, combined_send), ('expert', 'hidden'), split_...  16 us
    all_to_all x1, waiting for transfers between devices, mirrored_local(): lax.all_to_all(after(routed, combined_send), ('expert', 'hidden'), split_...  12 us
    ppermute x5, waiting for transfers between devices, neighbour(): return lax.ppermute(x, 'hidden', beside)  11.6 us
    ppermute x1, waiting for transfers between devices, mirrored_local(): hidden_diagonal = lax.ppermute(hidden, ('expert', 'hidden'), diagonal)  10.2 us
    ppermute x4, starting transfers between devices, mirror(): return lax.ppermute(x, 'expert', across)  9 us
    all_to_all x2, waiting for transfers between devices, exchange(): lax.all_to_all(x, 'expert', split_axis=0, concat_axis=0, tiled=True, axis...  7.89 us
    all_to_all x2, starting transfers between devices, exchange(): lax.all_to_all(x, 'expert', split_axis=0, concat_axis=0, tiled=True, axis...  7.81 us
    ppermute x5, starting transfers between devices, neighbour(): return lax.ppermute(x, 'hidden', beside)  7.4 us
  transfers between devices with their start and end apart: 22, of which 11 were waited for; matrix products, arithmetic and copies ran while one was open for 1% of the time, Pallas kernels for 17%

profile of v3, /device:TPU:0, one launch (start us, length us, event | category | flops | bytes accessed | tf_op | source)
XLA Modules:
  0.0 144.1 jit_solution(11390393601583298526)
XLA Ops:
  0.6 4.1 %collective-permute-start.3 = (bf16[128,1792]{1,0:T(8,128)(2,1)}, bf16[128,1792]{1,0:T(8,128)(2,1)S(1)}, u32[]{:S(2)}, u32[]{:S(2)}) collective-permute-start(bf16[128,1792]{1,0:T(8,128)(2,1)} %refs_0_.1), channel_id=1, source_target_pairs={{0,16},{2,18},{4,20},{6,22},{8,24},{10,26},{12,28},{14,30},{16,0},... | collective-permute-start | bytes 1376264 | tf_op jit(solution)/shard_map/ppermute | solution.py:497
  6.9 1.8 %collective-permute-start = (bf16[256,128]{1,0:T(8,128)(2,1)S(1)}, bf16[256,128]{1,0:T(8,128)(2,1)S(1)}, u32[]{:S(2)}, u32[]{:S(2)}) collective-permute-start(bf16[256,128]{1,0:T(8,128)(2,1)S(1)} %get-tuple-element.48), channel_id=1, source_target_pairs={{0,1},{1,0},{2,3},{3,2},{4,5},{5,4},{6,7},{7,6},{8,9},{9,8},{10,11... | collective-permute-start | bytes 196616 | tf_op jit(solution)/shard_map/ppermute | solution.py:500
  8.7 2.5 %collective-permute-start.2 = (bf16[256,128]{1,0:T(8,128)(2,1)S(1)}, bf16[256,128]{1,0:T(8,128)(2,1)S(1)}, u32[]{:S(2)}, u32[]{:S(2)}) collective-permute-start(bf16[256,128]{1,0:T(8,128)(2,1)S(1)} %get-tuple-element.48), channel_id=1, source_target_pairs={{0,17},{1,16},{2,19},{3,18},{4,21},{5,20},{6,23},{7,22},{8,25},{9,... | collective-permute-start | bytes 196616 | tf_op jit(solution)/shard_map/ppermute | solution.py:517
  13.3 1.5 %collective-permute-start.5 = (bf16[1,128,1792]{2,1,0:T(8,128)(2,1)}, bf16[1,128,1792]{2,1,0:T(8,128)(2,1)}, u32[]{:S(2)}, u32[]{:S(2)}) collective-permute-start(bf16[1,128,1792]{2,1,0:T(8,128)(2,1)} %get-tuple-element.51), channel_id=1, source_target_pairs={{0,1},{1,0},{2,3},{3,2},{4,5},{5,4},{6,7},{7,6},{8,9},{9,8},{10,11... | collective-permute-start | bytes 1376264 | tf_op jit(solution)/shard_map/ppermute | solution.py:500
  16.2 1.7 %pack_own.1 = bf16[8,32,2048]{2,1,0:T(8,128)(2,1)} custom-call(bf16[272,128]{1,0:T(8,128)(2,1)S(1)} %get-tuple-element.81.acts_ref.meta_ref, bf16[256,128]{1,0:T(8,128)(2,1)S(1)} %collective-permute-done.beside_ref, bf16[128,1792]{1,0:T(8,128)(2,1)S(1)} %copy-done.7), custom_call_target="tpu_custom_call" | custom-call | tf_op jit(solution)/shard_map/pack_own/pallas_call | solution.py:531
  17.8 4.3 %all-to-all-start = ((bf16[8,32,2048]{2,1,0:T(8,128)(2,1)}), bf16[8,32,2048]{2,1,0:T(8,128)(2,1)}, u32[]{:S(2)}, u32[]{:S(2)}) async-start(bf16[8,32,2048]{2,1,0:T(8,128)(2,1)} %pack_own.1), calls=%async_computation | async-start | bytes 2097152 | tf_op jit(solution)/shard_map/all_to_all | solution.py:503
  22.1 10.2 %collective-permute-done.2.beside_ref = bf16[256,128]{1,0:T(8,128)(2,1)S(1)} collective-permute-done((bf16[256,128]{1,0:T(8,128)(2,1)S(1)}, bf16[256,128]{1,0:T(8,128)(2,1)S(1)}, u32[]{:S(2)}, u32[]{:S(2)}) %collective-permute-start.2) | collective-permute-done | bytes 65568 | tf_op jit(solution)/shard_map/ppermute | solution.py:517
  32.3 1.6 %pack_far.1 = bf16[8,32,2048]{2,1,0:T(8,128)(2,1)} custom-call(bf16[272,128]{1,0:T(8,128)(2,1)S(1)} %collective-permute-done.1.acts_ref, bf16[256,128]{1,0:T(8,128)(2,1)S(1)} %collective-permute-done.2.beside_ref, bf16[128,1792]{1,0:T(8,128)(2,1)S(1)} %collective-permute-done.3.refs_0_), custom_call_target="tpu_custom_call" | custom-call | flops 999999995904 | bytes 10000000000 | tf_op jit(solution)/shard_map/pack_far/pallas_call | solution.py:534
  34.0 2.0 %collective-permute-done.4.beside_ref = bf16[1,128,1792]{2,1,0:T(8,128)(2,1)} collective-permute-done((bf16[1,128,1792]{2,1,0:T(8,128)(2,1)}, bf16[1,128,1792]{2,1,0:T(8,128)(2,1)}, u32[]{:S(2)}, u32[]{:S(2)}) %collective-permute-start.4) | collective-permute-done | bytes 458784 | tf_op jit(solution)/shard_map/ppermute | solution.py:500
  36.0 6.5 %all-to-all-done.recv_ref = bf16[8,32,2048]{2,1,0:T(8,128)(2,1)} async-done(((bf16[8,32,2048]{2,1,0:T(8,128)(2,1)}), bf16[8,32,2048]{2,1,0:T(8,128)(2,1)}, u32[]{:S(2)}, u32[]{:S(2)}) %all-to-all-start) | async-done | bytes 1048608 | tf_op jit(solution)/shard_map/all_to_all | solution.py:503
  42.4 3.6 %all-to-all-start.1 = ((bf16[8,32,2048]{2,1,0:T(8,128)(2,1)}), bf16[8,32,2048]{2,1,0:T(8,128)(2,1)S(1)}, u32[]{:S(2)}, u32[]{:S(2)}) async-start(bf16[8,32,2048]{2,1,0:T(8,128)(2,1)} %pack_far.1), calls=%async_computation.1 | async-start | bytes 2097152 | tf_op jit(solution)/shard_map/all_to_all | solution.py:503
  46.1 1.7 %collective-permute-start.6 = (bf16[1,128,1792]{2,1,0:T(8,128)(2,1)S(1)}, bf16[1,128,1792]{2,1,0:T(8,128)(2,1)S(1)}, u32[]{:S(2)}, u32[]{:S(2)}) collective-permute-start(bf16[1,128,1792]{2,1,0:T(8,128)(2,1)S(1)} %get-tuple-element.55), channel_id=1, source_target_pairs={{0,1},{1,0},{2,3},{3,2},{4,5},{5,4},{6,7},{7,6},{8,9},{9,8},{10,11... | collective-permute-start | bytes 1376264 | tf_op jit(solution)/shard_map/ppermute | solution.py:500
  47.7 2.0 %grad_rows.2.grads_ref = bf16[8,32,256]{2,1,0:T(8,128)(2,1)S(1)} custom-call(bf16[8,32,2048]{2,1,0:T(8,128)(2,1)} %all-to-all-done.recv_ref, bf16[1,128,1792]{2,1,0:T(8,128)(2,1)S(1)} %get-tuple-element.56.weight_ref, bf16[1,128,1792]{2,1,0:T(8,128)(2,1)} %collective-permute-done.4.beside_ref), custom_call_target="tpu_custom_call" | custom-call | tf_op jit(solution)/shard_map/grad_rows/pallas_call | solution.py:540
  49.7 9.2 %collective-permute-done.6.second_beside = bf16[1,128,1792]{2,1,0:T(8,128)(2,1)S(1)} collective-permute-done((bf16[1,128,1792]{2,1,0:T(8,128)(2,1)S(1)}, bf16[1,128,1792]{2,1,0:T(8,128)(2,1)S(1)}, u32[]{:S(2)}, u32[]{:S(2)}) %collective-permute-start.6) | collective-permute-done | bytes 458784 | tf_op jit(solution)/shard_map/ppermute | solution.py:500
  60.4 2.4 %forward_far.1 = (bf16[2,32,1792]{2,1,0:T(8,128)(2,1)S(1)}, bf16[2,32,1792]{2,1,0:T(8,128)(2,1)}, bf16[2,32,1792]{2,1,0:T(8,128)(2,1)}, bf16[2,32,1792]{2,1,0:T(8,128)(2,1)S(1)}) custom-call(bf16[8,32,2048]{2,1,0:T(8,128)(2,1)S(1)} %all-to-all-done.1.recv_ref.far_ref, bf16[1,128,1792]{2,1,0:T(8,128)(2,1)S(1)} %get-tuple-element.56.weight_ref, ...), custom_call_target="tpu_custom_call" | custom-call | tf_op jit(solution)/shard_map/forward_far/pallas_call | solution.py:553
  66.9 1.6 %grad_rows.3 = bf16[8,32,256]{2,1,0:T(8,128)(2,1)S(1)} custom-call(bf16[8,32,2048]{2,1,0:T(8,128)(2,1)S(1)} %all-to-all-done.1.recv_ref.far_ref, bf16[1,128,1792]{2,1,0:T(8,128)(2,1)S(1)} %get-tuple-element.56.weight_ref, bf16[1,128,1792]{2,1,0:T(8,128)(2,1)} %collective-permute-done.4.beside_ref), custom_call_target="tpu_custom_call" | custom-call | tf_op jit(solution)/shard_map/grad_rows/pallas_call | solution.py:557
  68.6 2.9 %collective-permute-start.10 = (bf16[8,32,256]{2,1,0:T(8,128)(2,1)S(1)}, bf16[8,32,256]{2,1,0:T(8,128)(2,1)S(1)}, u32[]{:S(2)}, u32[]{:S(2)}) collective-permute-start(bf16[8,32,256]{2,1,0:T(8,128)(2,1)S(1)} %grad_rows.3), channel_id=1, source_target_pairs={{0,16},{2,18},{4,20},{6,22},{8,24},{10,26},{12,28},{14,30},{16,0},... | collective-permute-start | bytes 393224 | tf_op jit(solution)/shard_map/ppermute | solution.py:497
  71.5 3.6 %update.1 = bf16[8,2,32,896]{3,2,1,0:T(8,128)(2,1)} custom-call(bf16[8,32,2048]{2,1,0:T(8,128)(2,1)} %all-to-all-done.recv_ref, bf16[8,32,2048]{2,1,0:T(8,128)(2,1)S(1)} %all-to-all-done.1.recv_ref.far_ref, bf16[1,128,1792]{2,1,0:T(8,128)(2,1)S(1)} %get-tuple-element.64.first_ref, bf16[1,128,1792]{2,1,0:T(8,128)(2,1)S(1)} %get-tuple-element.65.second_ref, ...), custom_call_target="tpu_custom_call" | custom-call | tf_op jit(solution)/shard_map/update/pallas_call | solution.py:559
  75.1 3.8 %all-to-all-start.2 = ((bf16[16,32,896]{2,1,0:T(8,128)(2,1)}), bf16[16,32,896]{2,1,0:T(8,128)(2,1)S(1)}, u32[]{:S(2)}, u32[]{:S(2)}) async-start(bf16[16,32,896]{2,1,0:T(8,128)(2,1)} %bitcast.3), calls=%async_computation.2 | async-start | bytes 1835008 | tf_op jit(solution)/shard_map/all_to_all | solution.py:562
  81.1 1.8 %collective-permute-done.11.refs_4_ = bf16[4,32,1792]{2,1,0:T(8,128)(2,1)S(1)} collective-permute-done((bf16[4,32,1792]{2,1,0:T(8,128)(2,1)S(1)}, bf16[4,32,1792]{2,1,0:T(8,128)(2,1)S(1)}, u32[]{:S(2)}, u32[]{:S(2)}) %collective-permute-start.11) | collective-permute-done | bytes 458784 | tf_op jit(solution)/shard_map/ppermute | solution.py:546
  82.9 1.8 %combine_far.1 = bf16[128,1792]{1,0:T(8,128)(2,1)S(1)} custom-call(bf16[272,128]{1,0:T(8,128)(2,1)S(1)} %copy-done.12, bf16[2,32,1792]{2,1,0:T(8,128)(2,1)S(1)} %copy-done.9, bf16[2,32,1792]{2,1,0:T(8,128)(2,1)} %collective-permute-done.7.refs_1_, bf16[2,32,1792]{2,1,0:T(8,128)(2,1)} %collective-permute-done.8.refs_2_, ...), custom_call_target="tpu_custom_call" | custom-call | flops 5500000256 | bytes 55000000 | tf_op jit(solution)/shard_map/combine_far/pallas_call | solution.py:575
  85.4 1.9 %forward_own.1 = (bf16[4,32,2304]{2,1,0:T(8,128)(2,1)S(1)}, bf16[4,32,2304]{2,1,0:T(8,128)(2,1)S(1)}) custom-call(bf16[8,32,2048]{2,1,0:T(8,128)(2,1)} %all-to-all-done.recv_ref, bf16[1,128,1792]{2,1,0:T(8,128)(2,1)S(1)} %get-tuple-element.56.weight_ref, bf16[1,128,1792]{2,1,0:T(8,128)(2,1)} %collective-permute-done.4.beside_ref, ...), custom_call_target="tpu_custom_call" | custom-call | tf_op jit(solution)/shard_map/forward_own/pallas_call | solution.py:579
  88.4 1.9 %collective-permute-start.16 = (bf16[128,1792]{1,0:T(8,128)(2,1)}, bf16[128,1792]{1,0:T(8,128)(2,1)}, u32[]{:S(2)}, u32[]{:S(2)}) collective-permute-start(bf16[128,1792]{1,0:T(8,128)(2,1)} %copy-done.10), channel_id=1, source_target_pairs={{0,16},{2,18},{4,20},{6,22},{8,24},{10,26},{12,28},{14,30},{16,0},... | collective-permute-start | bytes 1376264 | tf_op jit(solution)/shard_map/ppermute | solution.py:497
  94.9 5.2 %all-to-all-done.2.recv_ref = bf16[16,32,896]{2,1,0:T(8,128)(2,1)S(1)} async-done(((bf16[16,32,896]{2,1,0:T(8,128)(2,1)}), bf16[16,32,896]{2,1,0:T(8,128)(2,1)S(1)}, u32[]{:S(2)}, u32[]{:S(2)}) %all-to-all-start.2) | async-done | bytes 917536 | tf_op jit(solution)/shard_map/all_to_all | solution.py:562
  100.1 1.6 %route_steps.1 = bf16[32,16,896]{2,1,0:T(8,128)(2,1)} custom-call(s32[32]{0:T(128)S(1)} %reshape.26.source_ref, s32[32]{0:T(128)S(1)} %xor.10.line_ref, bf16[16,32,896]{2,1,0:T(8,128)(2,1)S(1)} %all-to-all-done.2.recv_ref), custom_call_target="tpu_custom_call" | custom-call | tf_op jit(solution)/shard_map/route_steps/pallas_call | solution.py:593
  101.7 16.0 %all-to-all-start.3 = ((bf16[32,16,896]{2,1,0:T(8,128)(2,1)}), bf16[32,16,896]{2,1,0:T(8,128)(2,1)}, u32[]{:S(2)}, u32[]{:S(2)}) async-start(bf16[32,16,896]{2,1,0:T(8,128)(2,1)} %route_steps.1), calls=%async_computation.3 | async-start | bytes 1835008 | tf_op jit(solution)/shard_map/all_to_all | solution.py:601
  117.9 4.9 %collective-permute-done.16.far_ref = bf16[128,1792]{1,0:T(8,128)(2,1)} collective-permute-done((bf16[128,1792]{1,0:T(8,128)(2,1)}, bf16[128,1792]{1,0:T(8,128)(2,1)}, u32[]{:S(2)}, u32[]{:S(2)}) %collective-permute-start.16) | collective-permute-done | bytes 458784 | tf_op jit(solution)/shard_map/ppermute | solution.py:497
  122.8 1.6 %pick_grads.1 = (f32[256,128]{1,0:T(8,128)S(1)}, bf16[256,128]{1,0:T(8,128)(2,1)S(1)}) custom-call(bf16[272,128]{1,0:T(8,128)(2,1)S(1)} %copy-done.6, bf16[2,32,2304]{2,1,0:T(8,128)(2,1)S(1)} %get-tuple-element.84.refs_0_, bf16[2,32,2304]{2,1,0:T(8,128)(2,1)} %collective-permute-done.13.refs_1_, bf16[2,32,2304]{2,1,0:T(8,128)(2,1)} %collective-permute-done.14.refs_2_, ...), custom_call_target="tpu_custom_call" | custom-call | tf_op jit(solution)/shard_map/pick_grads/pallas_call | solution.py:609
  124.4 1.9 %collective-permute-start.17 = (bf16[256,128]{1,0:T(8,128)(2,1)S(1)}, bf16[256,128]{1,0:T(8,128)(2,1)S(1)}, u32[]{:S(2)}, u32[]{:S(2)}) collective-permute-start(bf16[256,128]{1,0:T(8,128)(2,1)S(1)} %get-tuple-element.89), channel_id=1, source_target_pairs={{0,1},{1,0},{2,3},{3,2},{4,5},{5,4},{6,7},{7,6},{8,9},{9,8},{10,11... | collective-permute-start | bytes 196616 | tf_op jit(solution)/shard_map/ppermute | solution.py:500
  126.3 2.5 %combine_own.1 = bf16[128,1792]{1,0:T(8,128)(2,1)} custom-call(bf16[272,128]{1,0:T(8,128)(2,1)S(1)} %copy-done.6, bf16[256,256]{1,0:T(8,128)(2,1)S(1)} %choose.1.chosen_ref, bf16[128,1792]{1,0:T(8,128)(2,1)} %collective-permute-done.16.far_ref, bf16[2,32,2304]{2,1,0:T(8,128)(2,1)S(1)} %get-tuple-element.84.refs_0_, ...), custom_call_target="tpu_custom_call" | custom-call | tf_op jit(solution)/shard_map/combine_own/pallas_call | solution.py:617
  130.0 12.0 %all-to-all-done.3 = bf16[32,16,896]{2,1,0:T(8,128)(2,1)} async-done(((bf16[32,16,896]{2,1,0:T(8,128)(2,1)}), bf16[32,16,896]{2,1,0:T(8,128)(2,1)}, u32[]{:S(2)}, u32[]{:S(2)}) %all-to-all-start.3) | async-done | bytes 917536 | tf_op jit(solution)/shard_map/all_to_all | solution.py:601
  141.9 2.2 %place_steps.1 = bf16[128,3584]{1,0:T(8,128)(2,1)} custom-call(bf16[8,2,2,16,896]{4,3,2,1,0:T(8,128)(2,1)} %bitcast.6.recv_ref), custom_call_target="tpu_custom_call" | custom-call | tf_op jit(solution)/shard_map/place_steps/pallas_call | solution.py:620
  (76 shorter events, 20.9 us)
Async XLA Ops:
  0.6 5.1 %copy-start.13 = (s32[128,2]{0,1:T(2,128)S(1)}, s32[128,2]{0,1:T(2,128)}, u32[]{:S(2)}) copy-start(s32[128,2]{0,1:T(2,128)} %param.9) | copy-start | bytes 3076
  0.6 31.7 %collective-permute-start.3 = (bf16[128,1792]{1,0:T(8,128)(2,1)}, bf16[128,1792]{1,0:T(8,128)(2,1)S(1)}, u32[]{:S(2)}, u32[]{:S(2)}) collective-permute-start(bf16[128,1792]{1,0:T(8,128)(2,1)} %refs_0_.1), channel_id=1, source_target_pairs={{0,16},{2,18},{4,20},{6,22},{8,24},{10,26},{12,28},{14,30},{16,0},... | collective-permute-start | bytes 1376264 | tf_op jit(solution)/shard_map/ppermute | solution.py:497
  6.8 9.3 %copy-start.5 = (bf16[272,128]{1,0:T(8,128)(2,1)}, bf16[272,128]{1,0:T(8,128)(2,1)S(1)}, u32[]{:S(2)}) copy-start(bf16[272,128]{1,0:T(8,128)(2,1)S(1)} %get-tuple-element.81.acts_ref.meta_ref) | copy-start | bytes 208900
  6.8 25.5 %collective-permute-start.1 = (bf16[272,128]{1,0:T(8,128)(2,1)S(1)}, bf16[272,128]{1,0:T(8,128)(2,1)S(1)}, u32[]{:S(2)}, u32[]{:S(2)}) collective-permute-start(bf16[272,128]{1,0:T(8,128)(2,1)S(1)} %get-tuple-element.81.acts_ref.meta_ref), channel_id=1, source_target_pairs={{0,16},{2,18},{4,20},{6,22},{8,24},{10,26},{12,28},{14,30},{16,0},... | collective-permute-start | bytes 208904 | tf_op jit(solution)/shard_map/ppermute | solution.py:497
  6.9 8.7 %collective-permute-start = (bf16[256,128]{1,0:T(8,128)(2,1)S(1)}, bf16[256,128]{1,0:T(8,128)(2,1)S(1)}, u32[]{:S(2)}, u32[]{:S(2)}) collective-permute-start(bf16[256,128]{1,0:T(8,128)(2,1)S(1)} %get-tuple-element.48), channel_id=1, source_target_pairs={{0,1},{1,0},{2,3},{3,2},{4,5},{5,4},{6,7},{7,6},{8,9},{9,8},{10,11... | collective-permute-start | bytes 196616 | tf_op jit(solution)/shard_map/ppermute | solution.py:500
  8.7 23.6 %collective-permute-start.2 = (bf16[256,128]{1,0:T(8,128)(2,1)S(1)}, bf16[256,128]{1,0:T(8,128)(2,1)S(1)}, u32[]{:S(2)}, u32[]{:S(2)}) collective-permute-start(bf16[256,128]{1,0:T(8,128)(2,1)S(1)} %get-tuple-element.48), channel_id=1, source_target_pairs={{0,17},{1,16},{2,19},{3,18},{4,21},{5,20},{6,23},{7,22},{8,25},{9,... | collective-permute-start | bytes 196616 | tf_op jit(solution)/shard_map/ppermute | solution.py:517
  12.4 2.4 %copy-start.3 = (bf16[1,128,3584]{2,1,0:T(8,128)(2,1)S(1)}, bf16[1,128,3584]{2,1,0:T(8,128)(2,1)}, u32[]{:S(2)}) copy-start(bf16[1,128,3584]{2,1,0:T(8,128)(2,1)} %param.13) | copy-start | bytes 2752516
  13.3 20.7 %collective-permute-start.5 = (bf16[1,128,1792]{2,1,0:T(8,128)(2,1)}, bf16[1,128,1792]{2,1,0:T(8,128)(2,1)}, u32[]{:S(2)}, u32[]{:S(2)}) collective-permute-start(bf16[1,128,1792]{2,1,0:T(8,128)(2,1)} %get-tuple-element.51), channel_id=1, source_target_pairs={{0,1},{1,0},{2,3},{3,2},{4,5},{5,4},{6,7},{7,6},{8,9},{9,8},{10,11... | collective-permute-start | bytes 1376264 | tf_op jit(solution)/shard_map/ppermute | solution.py:500
  14.8 1.4 copy-start.7
  15.6 20.3 %collective-permute-start.4 = (bf16[1,128,1792]{2,1,0:T(8,128)(2,1)}, bf16[1,128,1792]{2,1,0:T(8,128)(2,1)}, u32[]{:S(2)}, u32[]{:S(2)}) collective-permute-start(bf16[1,128,1792]{2,1,0:T(8,128)(2,1)} %get-tuple-element.49), channel_id=1, source_target_pairs={{0,1},{1,0},{2,3},{3,2},{4,5},{5,4},{6,7},{7,6},{8,9},{9,8},{10,11... | collective-permute-start | bytes 1376264 | tf_op jit(solution)/shard_map/ppermute | solution.py:500
  17.8 24.6 %all-to-all-start = ((bf16[8,32,2048]{2,1,0:T(8,128)(2,1)}), bf16[8,32,2048]{2,1,0:T(8,128)(2,1)}, u32[]{:S(2)}, u32[]{:S(2)}) async-start(bf16[8,32,2048]{2,1,0:T(8,128)(2,1)} %pack_own.1), calls=%async_computation | async-start | bytes 2097152 | tf_op jit(solution)/shard_map/all_to_all | solution.py:503
  32.3 1.6 %copy-start.11 = (bf16[272,128]{1,0:T(8,128)(2,1)}, bf16[272,128]{1,0:T(8,128)(2,1)S(1)}, u32[]{:S(2)}) copy-start(bf16[272,128]{1,0:T(8,128)(2,1)S(1)} %collective-permute-done.1.acts_ref) | copy-start | bytes 208900
  33.9 12.1 %copy-start.4 = (bf16[1,128,3584]{2,1,0:T(8,128)(2,1)S(1)}, bf16[1,128,3584]{2,1,0:T(8,128)(2,1)}, u32[]{:S(2)}) copy-start(bf16[1,128,3584]{2,1,0:T(8,128)(2,1)} %param.15) | copy-start | bytes 2752516
  42.4 17.9 %all-to-all-start.1 = ((bf16[8,32,2048]{2,1,0:T(8,128)(2,1)}), bf16[8,32,2048]{2,1,0:T(8,128)(2,1)S(1)}, u32[]{:S(2)}, u32[]{:S(2)}) async-start(bf16[8,32,2048]{2,1,0:T(8,128)(2,1)} %pack_far.1), calls=%async_computation.1 | async-start | bytes 2097152 | tf_op jit(solution)/shard_map/all_to_all | solution.py:503
  46.1 12.9 %collective-permute-start.6 = (bf16[1,128,1792]{2,1,0:T(8,128)(2,1)S(1)}, bf16[1,128,1792]{2,1,0:T(8,128)(2,1)S(1)}, u32[]{:S(2)}, u32[]{:S(2)}) collective-permute-start(bf16[1,128,1792]{2,1,0:T(8,128)(2,1)S(1)} %get-tuple-element.55), channel_id=1, source_target_pairs={{0,1},{1,0},{2,3},{3,2},{4,5},{5,4},{6,7},{7,6},{8,9},{9,8},{10,11... | collective-permute-start | bytes 1376264 | tf_op jit(solution)/shard_map/ppermute | solution.py:500
  63.4 15.4 %collective-permute-start.7 = (bf16[2,32,1792]{2,1,0:T(8,128)(2,1)}, bf16[2,32,1792]{2,1,0:T(8,128)(2,1)}, u32[]{:S(2)}, u32[]{:S(2)}) collective-permute-start(bf16[2,32,1792]{2,1,0:T(8,128)(2,1)} %get-tuple-element.60), channel_id=1, source_target_pairs={{0,4},{2,6},{4,0},{6,2},{8,12},{10,14},{12,8},{14,10},{16,20},{18,... | collective-permute-start | bytes 688136 | tf_op jit(solution)/shard_map/ppermute | solution.py:546
  64.9 14.0 %collective-permute-start.8 = (bf16[2,32,1792]{2,1,0:T(8,128)(2,1)}, bf16[2,32,1792]{2,1,0:T(8,128)(2,1)}, u32[]{:S(2)}, u32[]{:S(2)}) collective-permute-start(bf16[2,32,1792]{2,1,0:T(8,128)(2,1)} %get-tuple-element.61), channel_id=1, source_target_pairs={{0,8},{2,10},{4,12},{6,14},{8,0},{10,2},{12,4},{14,6},{16,24},{18,... | collective-permute-start | bytes 688136 | tf_op jit(solution)/shard_map/ppermute | solution.py:546
  65.5 14.3 %collective-permute-start.9 = (bf16[2,32,1792]{2,1,0:T(8,128)(2,1)S(1)}, bf16[2,32,1792]{2,1,0:T(8,128)(2,1)}, u32[]{:S(2)}, u32[]{:S(2)}) collective-permute-start(bf16[2,32,1792]{2,1,0:T(8,128)(2,1)S(1)} %get-tuple-element.62), channel_id=1, source_target_pairs={{0,12},{2,14},{4,8},{6,10},{8,4},{10,6},{12,0},{14,2},{16,28},{18,... | collective-permute-start | bytes 688136 | tf_op jit(solution)/shard_map/ppermute | solution.py:546
  68.6 10.3 %collective-permute-start.10 = (bf16[8,32,256]{2,1,0:T(8,128)(2,1)S(1)}, bf16[8,32,256]{2,1,0:T(8,128)(2,1)S(1)}, u32[]{:S(2)}, u32[]{:S(2)}) collective-permute-start(bf16[8,32,256]{2,1,0:T(8,128)(2,1)S(1)} %grad_rows.3), channel_id=1, source_target_pairs={{0,16},{2,18},{4,20},{6,22},{8,24},{10,26},{12,28},{14,30},{16,0},... | collective-permute-start | bytes 393224 | tf_op jit(solution)/shard_map/ppermute | solution.py:497
  75.1 4.7 %copy-start.9 = (bf16[2,32,1792]{2,1,0:T(8,128)(2,1)S(1)}, bf16[2,32,1792]{2,1,0:T(8,128)(2,1)}, u32[]{:S(2)}) copy-start(bf16[2,32,1792]{2,1,0:T(8,128)(2,1)} %copy-done.8) | copy-start | bytes 688132
  75.1 25.0 %all-to-all-start.2 = ((bf16[16,32,896]{2,1,0:T(8,128)(2,1)}), bf16[16,32,896]{2,1,0:T(8,128)(2,1)S(1)}, u32[]{:S(2)}, u32[]{:S(2)}) async-start(bf16[16,32,896]{2,1,0:T(8,128)(2,1)} %bitcast.3), calls=%async_computation.2 | async-start | bytes 1835008 | tf_op jit(solution)/shard_map/all_to_all | solution.py:562
  78.9 4.0 %copy-start.12 = (bf16[272,128]{1,0:T(8,128)(2,1)S(1)}, bf16[272,128]{1,0:T(8,128)(2,1)}, u32[]{:S(2)}) copy-start(bf16[272,128]{1,0:T(8,128)(2,1)} %copy-done.11) | copy-start | bytes 208900
  81.0 1.9 %collective-permute-start.11 = (bf16[4,32,1792]{2,1,0:T(8,128)(2,1)S(1)}, bf16[4,32,1792]{2,1,0:T(8,128)(2,1)S(1)}, u32[]{:S(2)}, u32[]{:S(2)}) collective-permute-start(bf16[4,32,1792]{2,1,0:T(8,128)(2,1)S(1)} %other_core_far.1), channel_id=1, source_target_pairs={{0,2},{2,0},{4,6},{6,4},{8,10},{10,8},{12,14},{14,12},{16,18},{18,... | collective-permute-start | bytes 1376264 | tf_op jit(solution)/shard_map/ppermute | solution.py:546
  87.4 3.0 %collective-permute-start.12 = (bf16[4,32,2304]{2,1,0:T(8,128)(2,1)S(1)}, bf16[4,32,2304]{2,1,0:T(8,128)(2,1)S(1)}, u32[]{:S(2)}, u32[]{:S(2)}) collective-permute-start(bf16[4,32,2304]{2,1,0:T(8,128)(2,1)S(1)} %get-tuple-element.76), channel_id=1, source_target_pairs={{0,2},{2,0},{4,6},{6,4},{8,10},{10,8},{12,14},{14,12},{16,18},{18,... | collective-permute-start | bytes 1769480 | tf_op jit(solution)/shard_map/ppermute | solution.py:546
  88.4 34.3 %collective-permute-start.16 = (bf16[128,1792]{1,0:T(8,128)(2,1)}, bf16[128,1792]{1,0:T(8,128)(2,1)}, u32[]{:S(2)}, u32[]{:S(2)}) collective-permute-start(bf16[128,1792]{1,0:T(8,128)(2,1)} %copy-done.10), channel_id=1, source_target_pairs={{0,16},{2,18},{4,20},{6,22},{8,24},{10,26},{12,28},{14,30},{16,0},... | collective-permute-start | bytes 1376264 | tf_op jit(solution)/shard_map/ppermute | solution.py:497
  91.4 31.4 %collective-permute-start.13 = (bf16[2,32,2304]{2,1,0:T(8,128)(2,1)}, bf16[2,32,2304]{2,1,0:T(8,128)(2,1)}, u32[]{:S(2)}, u32[]{:S(2)}) collective-permute-start(bf16[2,32,2304]{2,1,0:T(8,128)(2,1)} %get-tuple-element.78), channel_id=1, source_target_pairs={{0,4},{2,6},{4,0},{6,2},{8,12},{10,14},{12,8},{14,10},{16,20},{18,... | collective-permute-start | bytes 884744 | tf_op jit(solution)/shard_map/ppermute | solution.py:546
  92.9 29.9 %collective-permute-start.14 = (bf16[2,32,2304]{2,1,0:T(8,128)(2,1)}, bf16[2,32,2304]{2,1,0:T(8,128)(2,1)}, u32[]{:S(2)}, u32[]{:S(2)}) collective-permute-start(bf16[2,32,2304]{2,1,0:T(8,128)(2,1)} %get-tuple-element.79), channel_id=1, source_target_pairs={{0,8},{2,10},{4,12},{6,14},{8,0},{10,2},{12,4},{14,6},{16,24},{18,... | collective-permute-start | bytes 884744 | tf_op jit(solution)/shard_map/ppermute | solution.py:546
  94.4 28.4 %collective-permute-start.15 = (bf16[2,32,2304]{2,1,0:T(8,128)(2,1)}, bf16[2,32,2304]{2,1,0:T(8,128)(2,1)}, u32[]{:S(2)}, u32[]{:S(2)}) collective-permute-start(bf16[2,32,2304]{2,1,0:T(8,128)(2,1)} %get-tuple-element.80), channel_id=1, source_target_pairs={{0,12},{2,14},{4,8},{6,10},{8,4},{10,6},{12,0},{14,2},{16,28},{18,... | collective-permute-start | bytes 884744 | tf_op jit(solution)/shard_map/ppermute | solution.py:546
  101.7 16.0 %copy-start.6 = (bf16[272,128]{1,0:T(8,128)(2,1)S(1)}, bf16[272,128]{1,0:T(8,128)(2,1)}, u32[]{:S(2)}) copy-start(bf16[272,128]{1,0:T(8,128)(2,1)} %copy-done.5) | copy-start | bytes 208900
  101.7 40.3 %all-to-all-start.3 = ((bf16[32,16,896]{2,1,0:T(8,128)(2,1)}), bf16[32,16,896]{2,1,0:T(8,128)(2,1)}, u32[]{:S(2)}, u32[]{:S(2)}) async-start(bf16[32,16,896]{2,1,0:T(8,128)(2,1)} %route_steps.1), calls=%async_computation.3 | async-start | bytes 1835008 | tf_op jit(solution)/shard_map/all_to_all | solution.py:601
  124.4 4.8 %copy-start.1 = (bf16[128,512]{1,0:T(8,128)(2,1)S(1)}, bf16[128,512]{1,0:T(8,128)(2,1)}, u32[]{:S(2)}) copy-start(bf16[128,512]{1,0:T(8,128)(2,1)} %copy-done) | copy-start | bytes 393220
  124.4 4.7 %collective-permute-start.17 = (bf16[256,128]{1,0:T(8,128)(2,1)S(1)}, bf16[256,128]{1,0:T(8,128)(2,1)S(1)}, u32[]{:S(2)}, u32[]{:S(2)}) collective-permute-start(bf16[256,128]{1,0:T(8,128)(2,1)S(1)} %get-tuple-element.89), channel_id=1, source_target_pairs={{0,1},{1,0},{2,3},{3,2},{4,5},{5,4},{6,7},{7,6},{8,9},{9,8},{10,11... | collective-permute-start | bytes 196616 | tf_op jit(solution)/shard_map/ppermute | solution.py:500
  (6 other events, 5.1 us)

commit v4 on v3

--- a/solution.py
+++ b/solution.py
@@ -276,7 +276,9 @@
     return total.astype(bf16).reshape(half // 2, 2, cap, wide)
 
 
-def forward_far_body(half, recv_ref, weight_ref, beside_ref, *out_refs):
+def forward_far_body(half, recv_ref, weight_ref, beside_ref, *refs):
+    out_refs, grads_ref = refs[:-1], refs[-1]
+    grad_rows_body(recv_ref, weight_ref, beside_ref, grads_ref)
     total = output_rows(half, recv_ref, weight_ref, beside_ref, out_refs[0].shape[1])
     for distance, ref in enumerate(out_refs):
         ref[...] = total[distance]
@@ -550,14 +552,15 @@
 
     pairs = (shaped(2, cap, wide),) * (half // 2)
     extended = wide + 4 * units
-    outputs_far = whole_call(functools.partial(forward_far_body, half), pairs, "forward_far")(
-        recv_far, weight, weight_beside
-    )
-
-    rows_send = grad_rows(recv_far, weight, weight_beside)
+    *outputs_far, rows_send = whole_call(
+        functools.partial(forward_far_body, half),
+        pairs + (shaped(half, cap, 2 * units),),
+        "forward_far",
+    )(recv_far, weight, weight_beside)
+
     rows_mirror = mirror(rows_send)
     steps = whole_call(update_body, shaped(half, 2, 2 * each, narrow), "update")(
-        recv, after(recv_far, outputs_far, rows_send), first, second, first_beside, second_beside
+        recv, after(recv_far, rows_send), first, second, first_beside, second_beside
     )
     spread = lax.all_to_all(
         steps.reshape(places, 2 * each, narrow),

time: 145 us -> 145 us (level)
  waiting for transfers between devices: 54.5 us -> 64.6 us
  starting transfers between devices: 53.8 us -> 44.6 us
    all_to_all x1, starting transfers between devices: 16 us -> 7.14 us  [mirrored_local(): lax.all_to_all(after(routed, combined_send), ('expert', 'hidden'), split_...]
    all_to_all x1, waiting for transfers between devices: 5.24 us -> 13.1 us  [mirrored_local(): lax.all_to_all(steps.reshape(places, 2 * each, narrow), 'expert', split_a...]
    ppermute x8, waiting for transfers between devices: 2.73 us -> 4.29 us  [at_distance(): return lax.ppermute(x, 'expert', [(k, k ^ distance) for k in range(places)])]
    pallas_call x2 -> x1, Pallas kernels: 4.02 us -> 2.86 us  [mirrored_local(): whole_call(functools.partial(forward_far_body, half), pairs + (shaped(hal...]
  transfers between devices with their start and end apart: 22 -> 22, of which waited for: 11 -> 13; matrix products, arithmetic and copies ran while one was open for 1% -> 1% of each run, Pallas kernels for 17% -> 16%
where the time goes in v4:
time: 145 us; the launch traced here: 144 us
  waiting for transfers between devices  64.6 us (45%)
  starting transfers between devices  44.6 us (31%)
  Pallas kernels  27.8 us (19%)
  local copies, waits for them, and re-layouts  5.87 us (4%)
    all_to_all x1, waiting for transfers between devices, mirrored_local(): lax.all_to_all(steps.reshape(places, 2 * each, narrow), 'expert', split_a...  13.1 us
    ppermute x5, waiting for transfers between devices, neighbour(): return lax.ppermute(x, 'hidden', beside)  12.3 us
    all_to_all x1, waiting for transfers between devices, mirrored_local(): lax.all_to_all(after(routed, combined_send), ('expert', 'hidden'), split_...  11.4 us
    ppermute x1, waiting for transfers between devices, mirrored_local(): hidden_diagonal = lax.ppermute(hidden, ('expert', 'hidden'), diagonal)  10.2 us
    ppermute x4, starting transfers between devices, mirror(): return lax.ppermute(x, 'expert', across)  8.48 us
    all_to_all x2, waiting for transfers between devices, exchange(): lax.all_to_all(x, 'expert', split_axis=0, concat_axis=0, tiled=True, axis...  7.89 us
    all_to_all x2, starting transfers between devices, exchange(): lax.all_to_all(x, 'expert', split_axis=0, concat_axis=0, tiled=True, axis...  7.81 us
    ppermute x8, starting transfers between devices, at_distance(): return lax.ppermute(x, 'expert', [(k, k ^ distance) for k in range(places)])  7.61 us
  transfers between devices with their start and end apart: 22, of which 13 were waited for; matrix products, arithmetic and copies ran while one was open for 1% of the time, Pallas kernels for 16%

profile of v4, /device:TPU:0, one launch (start us, length us, event | category | flops | bytes accessed | tf_op | source)
XLA Modules:
  0.0 143.9 jit_solution(4363839439730620331)
XLA Ops:
  0.6 4.1 %collective-permute-start.3 = (bf16[128,1792]{1,0:T(8,128)(2,1)}, bf16[128,1792]{1,0:T(8,128)(2,1)S(1)}, u32[]{:S(2)}, u32[]{:S(2)}) collective-permute-start(bf16[128,1792]{1,0:T(8,128)(2,1)} %refs_0_.1), channel_id=1, source_target_pairs={{0,16},{2,18},{4,20},{6,22},{8,24},{10,26},{12,28},{14,30},{16,0},... | collective-permute-start | bytes 1376264 | tf_op jit(solution)/shard_map/ppermute | solution.py:499
  6.9 1.8 %collective-permute-start = (bf16[256,128]{1,0:T(8,128)(2,1)S(1)}, bf16[256,128]{1,0:T(8,128)(2,1)S(1)}, u32[]{:S(2)}, u32[]{:S(2)}) collective-permute-start(bf16[256,128]{1,0:T(8,128)(2,1)S(1)} %get-tuple-element.49), channel_id=1, source_target_pairs={{0,1},{1,0},{2,3},{3,2},{4,5},{5,4},{6,7},{7,6},{8,9},{9,8},{10,11... | collective-permute-start | bytes 196616 | tf_op jit(solution)/shard_map/ppermute | solution.py:502
  8.7 2.5 %collective-permute-start.2 = (bf16[256,128]{1,0:T(8,128)(2,1)S(1)}, bf16[256,128]{1,0:T(8,128)(2,1)S(1)}, u32[]{:S(2)}, u32[]{:S(2)}) collective-permute-start(bf16[256,128]{1,0:T(8,128)(2,1)S(1)} %get-tuple-element.49), channel_id=1, source_target_pairs={{0,17},{1,16},{2,19},{3,18},{4,21},{5,20},{6,23},{7,22},{8,25},{9,... | collective-permute-start | bytes 196616 | tf_op jit(solution)/shard_map/ppermute | solution.py:519
  13.3 1.5 %collective-permute-start.4 = (bf16[1,128,1792]{2,1,0:T(8,128)(2,1)}, bf16[1,128,1792]{2,1,0:T(8,128)(2,1)}, u32[]{:S(2)}, u32[]{:S(2)}) collective-permute-start(bf16[1,128,1792]{2,1,0:T(8,128)(2,1)} %get-tuple-element.50), channel_id=1, source_target_pairs={{0,1},{1,0},{2,3},{3,2},{4,5},{5,4},{6,7},{7,6},{8,9},{9,8},{10,11... | collective-permute-start | bytes 1376264 | tf_op jit(solution)/shard_map/ppermute | solution.py:502
  16.2 1.7 %pack_own.1 = bf16[8,32,2048]{2,1,0:T(8,128)(2,1)} custom-call(bf16[272,128]{1,0:T(8,128)(2,1)S(1)} %get-tuple-element.83.acts_ref.meta_ref, bf16[256,128]{1,0:T(8,128)(2,1)S(1)} %collective-permute-done.beside_ref, bf16[128,1792]{1,0:T(8,128)(2,1)S(1)} %copy-done.7), custom_call_target="tpu_custom_call" | custom-call | tf_op jit(solution)/shard_map/pack_own/pallas_call | solution.py:533
  17.8 4.3 %all-to-all-start = ((bf16[8,32,2048]{2,1,0:T(8,128)(2,1)}), bf16[8,32,2048]{2,1,0:T(8,128)(2,1)}, u32[]{:S(2)}, u32[]{:S(2)}) async-start(bf16[8,32,2048]{2,1,0:T(8,128)(2,1)} %pack_own.1), calls=%async_computation | async-start | bytes 2097152 | tf_op jit(solution)/shard_map/all_to_all | solution.py:505
  22.1 10.2 %collective-permute-done.2.beside_ref = bf16[256,128]{1,0:T(8,128)(2,1)S(1)} collective-permute-done((bf16[256,128]{1,0:T(8,128)(2,1)S(1)}, bf16[256,128]{1,0:T(8,128)(2,1)S(1)}, u32[]{:S(2)}, u32[]{:S(2)}) %collective-permute-start.2) | collective-permute-done | bytes 65568 | tf_op jit(solution)/shard_map/ppermute | solution.py:519
  32.3 1.6 %pack_far.1 = bf16[8,32,2048]{2,1,0:T(8,128)(2,1)} custom-call(bf16[272,128]{1,0:T(8,128)(2,1)S(1)} %collective-permute-done.1.acts_ref, bf16[256,128]{1,0:T(8,128)(2,1)S(1)} %collective-permute-done.2.beside_ref, bf16[128,1792]{1,0:T(8,128)(2,1)S(1)} %collective-permute-done.3.refs_0_), custom_call_target="tpu_custom_call" | custom-call | flops 999999995904 | bytes 10000000000 | tf_op jit(solution)/shard_map/pack_far/pallas_call | solution.py:536
  34.0 2.0 %collective-permute-done.5.first_beside = bf16[1,128,1792]{2,1,0:T(8,128)(2,1)} collective-permute-done((bf16[1,128,1792]{2,1,0:T(8,128)(2,1)}, bf16[1,128,1792]{2,1,0:T(8,128)(2,1)}, u32[]{:S(2)}, u32[]{:S(2)}) %collective-permute-start.5) | collective-permute-done | bytes 458784 | tf_op jit(solution)/shard_map/ppermute | solution.py:502
  36.0 6.5 %all-to-all-done.recv_ref = bf16[8,32,2048]{2,1,0:T(8,128)(2,1)} async-done(((bf16[8,32,2048]{2,1,0:T(8,128)(2,1)}), bf16[8,32,2048]{2,1,0:T(8,128)(2,1)}, u32[]{:S(2)}, u32[]{:S(2)}) %all-to-all-start) | async-done | bytes 1048608 | tf_op jit(solution)/shard_map/all_to_all | solution.py:505
  42.4 3.6 %all-to-all-start.1 = ((bf16[8,32,2048]{2,1,0:T(8,128)(2,1)}), bf16[8,32,2048]{2,1,0:T(8,128)(2,1)S(1)}, u32[]{:S(2)}, u32[]{:S(2)}) async-start(bf16[8,32,2048]{2,1,0:T(8,128)(2,1)} %pack_far.1), calls=%async_computation.1 | async-start | bytes 2097152 | tf_op jit(solution)/shard_map/all_to_all | solution.py:505
  46.1 1.7 %collective-permute-start.6 = (bf16[1,128,1792]{2,1,0:T(8,128)(2,1)S(1)}, bf16[1,128,1792]{2,1,0:T(8,128)(2,1)S(1)}, u32[]{:S(2)}, u32[]{:S(2)}) collective-permute-start(bf16[1,128,1792]{2,1,0:T(8,128)(2,1)S(1)} %get-tuple-element.56), channel_id=1, source_target_pairs={{0,1},{1,0},{2,3},{3,2},{4,5},{5,4},{6,7},{7,6},{8,9},{9,8},{10,11... | collective-permute-start | bytes 1376264 | tf_op jit(solution)/shard_map/ppermute | solution.py:502
  47.7 2.0 %grad_rows.1.grads_ref = bf16[8,32,256]{2,1,0:T(8,128)(2,1)S(1)} custom-call(bf16[8,32,2048]{2,1,0:T(8,128)(2,1)} %all-to-all-done.recv_ref, bf16[1,128,1792]{2,1,0:T(8,128)(2,1)S(1)} %get-tuple-element.57.weight_ref, bf16[1,128,1792]{2,1,0:T(8,128)(2,1)} %collective-permute-done.4.beside_ref), custom_call_target="tpu_custom_call" | custom-call | tf_op jit(solution)/shard_map/grad_rows/pallas_call | solution.py:542
  49.7 9.2 %collective-permute-done.6.second_beside = bf16[1,128,1792]{2,1,0:T(8,128)(2,1)S(1)} collective-permute-done((bf16[1,128,1792]{2,1,0:T(8,128)(2,1)S(1)}, bf16[1,128,1792]{2,1,0:T(8,128)(2,1)S(1)}, u32[]{:S(2)}, u32[]{:S(2)}) %collective-permute-start.6) | collective-permute-done | bytes 458784 | tf_op jit(solution)/shard_map/ppermute | solution.py:502
  60.4 2.9 %forward_far.1 = (bf16[2,32,1792]{2,1,0:T(8,128)(2,1)S(1)}, bf16[2,32,1792]{2,1,0:T(8,128)(2,1)}, bf16[2,32,1792]{2,1,0:T(8,128)(2,1)}, bf16[2,32,1792]{2,1,0:T(8,128)(2,1)S(1)}, bf16[8,32,256]{2,1,0:T(8,128)(2,1)S(1)}) custom-call(bf16[8,32,2048]{2,1,0:T(8,128)(2,1)S(1)} %all-to-all-done.1.recv_ref.far_ref, ...), custom_call_target="tpu_custom_call" | custom-call | tf_op jit(solution)/shard_map/forward_far/pallas_call | solution.py:555
  67.4 2.8 %collective-permute-start.10 = (bf16[8,32,256]{2,1,0:T(8,128)(2,1)S(1)}, bf16[8,32,256]{2,1,0:T(8,128)(2,1)S(1)}, u32[]{:S(2)}, u32[]{:S(2)}) collective-permute-start(bf16[8,32,256]{2,1,0:T(8,128)(2,1)S(1)} %get-tuple-element.64), channel_id=1, source_target_pairs={{0,16},{2,18},{4,20},{6,22},{8,24},{10,26},{12,28},{14,30},{16,0},... | collective-permute-start | bytes 393224 | tf_op jit(solution)/shard_map/ppermute | solution.py:499
  70.2 3.6 %update.1 = bf16[8,2,32,896]{3,2,1,0:T(8,128)(2,1)} custom-call(bf16[8,32,2048]{2,1,0:T(8,128)(2,1)} %all-to-all-done.recv_ref, bf16[8,32,2048]{2,1,0:T(8,128)(2,1)S(1)} %all-to-all-done.1.recv_ref.far_ref, bf16[1,128,1792]{2,1,0:T(8,128)(2,1)S(1)} %get-tuple-element.66.first_ref, bf16[1,128,1792]{2,1,0:T(8,128)(2,1)S(1)} %get-tuple-element.67.second_ref, ...), custom_call_target="tpu_custom_call" | custom-call | tf_op jit(solution)/shard_map/update/pallas_call | solution.py:562
  73.8 3.8 %all-to-all-start.2 = ((bf16[16,32,896]{2,1,0:T(8,128)(2,1)}), bf16[16,32,896]{2,1,0:T(8,128)(2,1)S(1)}, u32[]{:S(2)}, u32[]{:S(2)}) async-start(bf16[16,32,896]{2,1,0:T(8,128)(2,1)} %bitcast.3), calls=%async_computation.2 | async-start | bytes 1835008 | tf_op jit(solution)/shard_map/all_to_all | solution.py:565
  78.3 2.0 %collective-permute-done.9.refs_3_ = bf16[2,32,1792]{2,1,0:T(8,128)(2,1)} collective-permute-done((bf16[2,32,1792]{2,1,0:T(8,128)(2,1)S(1)}, bf16[2,32,1792]{2,1,0:T(8,128)(2,1)}, u32[]{:S(2)}, u32[]{:S(2)}) %collective-permute-start.9) | collective-permute-done | bytes 229408 | tf_op jit(solution)/shard_map/ppermute | solution.py:548
  81.6 1.8 %collective-permute-done.11.refs_4_ = bf16[4,32,1792]{2,1,0:T(8,128)(2,1)S(1)} collective-permute-done((bf16[4,32,1792]{2,1,0:T(8,128)(2,1)S(1)}, bf16[4,32,1792]{2,1,0:T(8,128)(2,1)S(1)}, u32[]{:S(2)}, u32[]{:S(2)}) %collective-permute-start.11) | collective-permute-done | bytes 458784 | tf_op jit(solution)/shard_map/ppermute | solution.py:548
  83.4 1.8 %combine_far.1 = bf16[128,1792]{1,0:T(8,128)(2,1)S(1)} custom-call(bf16[272,128]{1,0:T(8,128)(2,1)S(1)} %copy-done.12, bf16[2,32,1792]{2,1,0:T(8,128)(2,1)S(1)} %copy-done.9, bf16[2,32,1792]{2,1,0:T(8,128)(2,1)} %collective-permute-done.7.refs_1_, bf16[2,32,1792]{2,1,0:T(8,128)(2,1)} %collective-permute-done.8.refs_2_, ...), custom_call_target="tpu_custom_call" | custom-call | flops 5500000256 | bytes 55000000 | tf_op jit(solution)/shard_map/combine_far/pallas_call | solution.py:578
  86.0 2.0 %forward_own.1 = (bf16[4,32,2304]{2,1,0:T(8,128)(2,1)S(1)}, bf16[4,32,2304]{2,1,0:T(8,128)(2,1)S(1)}) custom-call(bf16[8,32,2048]{2,1,0:T(8,128)(2,1)} %all-to-all-done.recv_ref, bf16[1,128,1792]{2,1,0:T(8,128)(2,1)S(1)} %get-tuple-element.57.weight_ref, bf16[1,128,1792]{2,1,0:T(8,128)(2,1)} %collective-permute-done.4.beside_ref, ...), custom_call_target="tpu_custom_call" | custom-call | tf_op jit(solution)/shard_map/forward_own/pallas_call | solution.py:582
  92.9 2.0 %collective-permute-start.14 = (bf16[2,32,2304]{2,1,0:T(8,128)(2,1)}, bf16[2,32,2304]{2,1,0:T(8,128)(2,1)}, u32[]{:S(2)}, u32[]{:S(2)}) collective-permute-start(bf16[2,32,2304]{2,1,0:T(8,128)(2,1)} %get-tuple-element.81), channel_id=1, source_target_pairs={{0,8},{2,10},{4,12},{6,14},{8,0},{10,2},{12,4},{14,6},{16,24},{18,... | collective-permute-start | bytes 884744 | tf_op jit(solution)/shard_map/ppermute | solution.py:548
  95.3 13.1 %all-to-all-done.2.recv_ref = bf16[16,32,896]{2,1,0:T(8,128)(2,1)S(1)} async-done(((bf16[16,32,896]{2,1,0:T(8,128)(2,1)}), bf16[16,32,896]{2,1,0:T(8,128)(2,1)S(1)}, u32[]{:S(2)}, u32[]{:S(2)}) %all-to-all-start.2) | async-done | bytes 917536 | tf_op jit(solution)/shard_map/all_to_all | solution.py:565
  108.4 1.6 %route_steps.1 = bf16[32,16,896]{2,1,0:T(8,128)(2,1)} custom-call(s32[32]{0:T(128)S(1)} %reshape.26.source_ref, s32[32]{0:T(128)S(1)} %xor.10.line_ref, bf16[16,32,896]{2,1,0:T(8,128)(2,1)S(1)} %all-to-all-done.2.recv_ref), custom_call_target="tpu_custom_call" | custom-call | tf_op jit(solution)/shard_map/route_steps/pallas_call | solution.py:596
  110.0 7.1 %all-to-all-start.3 = ((bf16[32,16,896]{2,1,0:T(8,128)(2,1)}), bf16[32,16,896]{2,1,0:T(8,128)(2,1)}, u32[]{:S(2)}, u32[]{:S(2)}) async-start(bf16[32,16,896]{2,1,0:T(8,128)(2,1)} %route_steps.1), calls=%async_computation.3 | async-start | bytes 1835008 | tf_op jit(solution)/shard_map/all_to_all | solution.py:604
  117.3 4.8 %collective-permute-done.16.far_ref = bf16[128,1792]{1,0:T(8,128)(2,1)} collective-permute-done((bf16[128,1792]{1,0:T(8,128)(2,1)}, bf16[128,1792]{1,0:T(8,128)(2,1)}, u32[]{:S(2)}, u32[]{:S(2)}) %collective-permute-start.16) | collective-permute-done | bytes 458784 | tf_op jit(solution)/shard_map/ppermute | solution.py:499
  122.6 1.6 %pick_grads.1 = (f32[256,128]{1,0:T(8,128)S(1)}, bf16[256,128]{1,0:T(8,128)(2,1)S(1)}) custom-call(bf16[272,128]{1,0:T(8,128)(2,1)S(1)} %copy-done.6, bf16[2,32,2304]{2,1,0:T(8,128)(2,1)S(1)} %get-tuple-element.86.refs_0_, bf16[2,32,2304]{2,1,0:T(8,128)(2,1)} %collective-permute-done.13.refs_1_, bf16[2,32,2304]{2,1,0:T(8,128)(2,1)} %collective-permute-done.14.refs_2_, ...), custom_call_target="tpu_custom_call" | custom-call | tf_op jit(solution)/shard_map/pick_grads/pallas_call | solution.py:612
  124.2 1.8 %collective-permute-start.17 = (bf16[256,128]{1,0:T(8,128)(2,1)S(1)}, bf16[256,128]{1,0:T(8,128)(2,1)S(1)}, u32[]{:S(2)}, u32[]{:S(2)}) collective-permute-start(bf16[256,128]{1,0:T(8,128)(2,1)S(1)} %get-tuple-element.91), channel_id=1, source_target_pairs={{0,1},{1,0},{2,3},{3,2},{4,5},{5,4},{6,7},{7,6},{8,9},{9,8},{10,11... | collective-permute-start | bytes 196616 | tf_op jit(solution)/shard_map/ppermute | solution.py:502
  126.0 2.5 %combine_own.1 = bf16[128,1792]{1,0:T(8,128)(2,1)} custom-call(bf16[272,128]{1,0:T(8,128)(2,1)S(1)} %copy-done.6, bf16[256,256]{1,0:T(8,128)(2,1)S(1)} %choose.1.chosen_ref, bf16[128,1792]{1,0:T(8,128)(2,1)} %collective-permute-done.16.far_ref, bf16[2,32,2304]{2,1,0:T(8,128)(2,1)S(1)} %get-tuple-element.86.refs_0_, ...), custom_call_target="tpu_custom_call" | custom-call | tf_op jit(solution)/shard_map/combine_own/pallas_call | solution.py:620
  130.3 11.4 %all-to-all-done.3 = bf16[32,16,896]{2,1,0:T(8,128)(2,1)} async-done(((bf16[32,16,896]{2,1,0:T(8,128)(2,1)}), bf16[32,16,896]{2,1,0:T(8,128)(2,1)}, u32[]{:S(2)}, u32[]{:S(2)}) %all-to-all-start.3) | async-done | bytes 917536 | tf_op jit(solution)/shard_map/all_to_all | solution.py:604
  141.7 2.2 %place_steps.1 = bf16[128,3584]{1,0:T(8,128)(2,1)} custom-call(bf16[8,2,2,16,896]{4,3,2,1,0:T(8,128)(2,1)} %bitcast.6.recv_ref), custom_call_target="tpu_custom_call" | custom-call | tf_op jit(solution)/shard_map/place_steps/pallas_call | solution.py:623
  (75 shorter events, 21.7 us)
Async XLA Ops:
  0.6 5.1 %copy-start.13 = (s32[128,2]{0,1:T(2,128)S(1)}, s32[128,2]{0,1:T(2,128)}, u32[]{:S(2)}) copy-start(s32[128,2]{0,1:T(2,128)} %param.9) | copy-start | bytes 3076
  0.6 31.7 %collective-permute-start.3 = (bf16[128,1792]{1,0:T(8,128)(2,1)}, bf16[128,1792]{1,0:T(8,128)(2,1)S(1)}, u32[]{:S(2)}, u32[]{:S(2)}) collective-permute-start(bf16[128,1792]{1,0:T(8,128)(2,1)} %refs_0_.1), channel_id=1, source_target_pairs={{0,16},{2,18},{4,20},{6,22},{8,24},{10,26},{12,28},{14,30},{16,0},... | collective-permute-start | bytes 1376264 | tf_op jit(solution)/shard_map/ppermute | solution.py:499
  6.8 9.3 %copy-start.5 = (bf16[272,128]{1,0:T(8,128)(2,1)}, bf16[272,128]{1,0:T(8,128)(2,1)S(1)}, u32[]{:S(2)}) copy-start(bf16[272,128]{1,0:T(8,128)(2,1)S(1)} %get-tuple-element.83.acts_ref.meta_ref) | copy-start | bytes 208900
  6.8 25.5 %collective-permute-start.1 = (bf16[272,128]{1,0:T(8,128)(2,1)S(1)}, bf16[272,128]{1,0:T(8,128)(2,1)S(1)}, u32[]{:S(2)}, u32[]{:S(2)}) collective-permute-start(bf16[272,128]{1,0:T(8,128)(2,1)S(1)} %get-tuple-element.83.acts_ref.meta_ref), channel_id=1, source_target_pairs={{0,16},{2,18},{4,20},{6,22},{8,24},{10,26},{12,28},{14,30},{16,0},... | collective-permute-start | bytes 208904 | tf_op jit(solution)/shard_map/ppermute | solution.py:499
  6.9 8.7 %collective-permute-start = (bf16[256,128]{1,0:T(8,128)(2,1)S(1)}, bf16[256,128]{1,0:T(8,128)(2,1)S(1)}, u32[]{:S(2)}, u32[]{:S(2)}) collective-permute-start(bf16[256,128]{1,0:T(8,128)(2,1)S(1)} %get-tuple-element.49), channel_id=1, source_target_pairs={{0,1},{1,0},{2,3},{3,2},{4,5},{5,4},{6,7},{7,6},{8,9},{9,8},{10,11... | collective-permute-start | bytes 196616 | tf_op jit(solution)/shard_map/ppermute | solution.py:502
  8.7 23.6 %collective-permute-start.2 = (bf16[256,128]{1,0:T(8,128)(2,1)S(1)}, bf16[256,128]{1,0:T(8,128)(2,1)S(1)}, u32[]{:S(2)}, u32[]{:S(2)}) collective-permute-start(bf16[256,128]{1,0:T(8,128)(2,1)S(1)} %get-tuple-element.49), channel_id=1, source_target_pairs={{0,17},{1,16},{2,19},{3,18},{4,21},{5,20},{6,23},{7,22},{8,25},{9,... | collective-permute-start | bytes 196616 | tf_op jit(solution)/shard_map/ppermute | solution.py:519
  12.4 2.4 %copy-start.3 = (bf16[1,128,3584]{2,1,0:T(8,128)(2,1)S(1)}, bf16[1,128,3584]{2,1,0:T(8,128)(2,1)}, u32[]{:S(2)}) copy-start(bf16[1,128,3584]{2,1,0:T(8,128)(2,1)} %param.14) | copy-start | bytes 2752516
  13.3 20.7 %collective-permute-start.4 = (bf16[1,128,1792]{2,1,0:T(8,128)(2,1)}, bf16[1,128,1792]{2,1,0:T(8,128)(2,1)}, u32[]{:S(2)}, u32[]{:S(2)}) collective-permute-start(bf16[1,128,1792]{2,1,0:T(8,128)(2,1)} %get-tuple-element.50), channel_id=1, source_target_pairs={{0,1},{1,0},{2,3},{3,2},{4,5},{5,4},{6,7},{7,6},{8,9},{9,8},{10,11... | collective-permute-start | bytes 1376264 | tf_op jit(solution)/shard_map/ppermute | solution.py:502
  14.8 1.4 copy-start.7
  15.6 20.3 %collective-permute-start.5 = (bf16[1,128,1792]{2,1,0:T(8,128)(2,1)}, bf16[1,128,1792]{2,1,0:T(8,128)(2,1)}, u32[]{:S(2)}, u32[]{:S(2)}) collective-permute-start(bf16[1,128,1792]{2,1,0:T(8,128)(2,1)} %get-tuple-element.52), channel_id=1, source_target_pairs={{0,1},{1,0},{2,3},{3,2},{4,5},{5,4},{6,7},{7,6},{8,9},{9,8},{10,11... | collective-permute-start | bytes 1376264 | tf_op jit(solution)/shard_map/ppermute | solution.py:502
  17.8 24.6 %all-to-all-start = ((bf16[8,32,2048]{2,1,0:T(8,128)(2,1)}), bf16[8,32,2048]{2,1,0:T(8,128)(2,1)}, u32[]{:S(2)}, u32[]{:S(2)}) async-start(bf16[8,32,2048]{2,1,0:T(8,128)(2,1)} %pack_own.1), calls=%async_computation | async-start | bytes 2097152 | tf_op jit(solution)/shard_map/all_to_all | solution.py:505
  32.3 1.6 %copy-start.11 = (bf16[272,128]{1,0:T(8,128)(2,1)}, bf16[272,128]{1,0:T(8,128)(2,1)S(1)}, u32[]{:S(2)}) copy-start(bf16[272,128]{1,0:T(8,128)(2,1)S(1)} %collective-permute-done.1.acts_ref) | copy-start | bytes 208900
  33.9 12.1 %copy-start.4 = (bf16[1,128,3584]{2,1,0:T(8,128)(2,1)S(1)}, bf16[1,128,3584]{2,1,0:T(8,128)(2,1)}, u32[]{:S(2)}) copy-start(bf16[1,128,3584]{2,1,0:T(8,128)(2,1)} %param.15) | copy-start | bytes 2752516
  42.4 17.9 %all-to-all-start.1 = ((bf16[8,32,2048]{2,1,0:T(8,128)(2,1)}), bf16[8,32,2048]{2,1,0:T(8,128)(2,1)S(1)}, u32[]{:S(2)}, u32[]{:S(2)}) async-start(bf16[8,32,2048]{2,1,0:T(8,128)(2,1)} %pack_far.1), calls=%async_computation.1 | async-start | bytes 2097152 | tf_op jit(solution)/shard_map/all_to_all | solution.py:505
  46.1 12.9 %collective-permute-start.6 = (bf16[1,128,1792]{2,1,0:T(8,128)(2,1)S(1)}, bf16[1,128,1792]{2,1,0:T(8,128)(2,1)S(1)}, u32[]{:S(2)}, u32[]{:S(2)}) collective-permute-start(bf16[1,128,1792]{2,1,0:T(8,128)(2,1)S(1)} %get-tuple-element.56), channel_id=1, source_target_pairs={{0,1},{1,0},{2,3},{3,2},{4,5},{5,4},{6,7},{7,6},{8,9},{9,8},{10,11... | collective-permute-start | bytes 1376264 | tf_op jit(solution)/shard_map/ppermute | solution.py:502
  63.9 14.3 %collective-permute-start.7 = (bf16[2,32,1792]{2,1,0:T(8,128)(2,1)}, bf16[2,32,1792]{2,1,0:T(8,128)(2,1)}, u32[]{:S(2)}, u32[]{:S(2)}) collective-permute-start(bf16[2,32,1792]{2,1,0:T(8,128)(2,1)} %get-tuple-element.61), channel_id=1, source_target_pairs={{0,4},{2,6},{4,0},{6,2},{8,12},{10,14},{12,8},{14,10},{16,20},{18,... | collective-permute-start | bytes 688136 | tf_op jit(solution)/shard_map/ppermute | solution.py:548
  65.4 12.9 %collective-permute-start.8 = (bf16[2,32,1792]{2,1,0:T(8,128)(2,1)}, bf16[2,32,1792]{2,1,0:T(8,128)(2,1)}, u32[]{:S(2)}, u32[]{:S(2)}) collective-permute-start(bf16[2,32,1792]{2,1,0:T(8,128)(2,1)} %get-tuple-element.62), channel_id=1, source_target_pairs={{0,8},{2,10},{4,12},{6,14},{8,0},{10,2},{12,4},{14,6},{16,24},{18,... | collective-permute-start | bytes 688136 | tf_op jit(solution)/shard_map/ppermute | solution.py:548
  66.0 14.3 %collective-permute-start.9 = (bf16[2,32,1792]{2,1,0:T(8,128)(2,1)S(1)}, bf16[2,32,1792]{2,1,0:T(8,128)(2,1)}, u32[]{:S(2)}, u32[]{:S(2)}) collective-permute-start(bf16[2,32,1792]{2,1,0:T(8,128)(2,1)S(1)} %get-tuple-element.63), channel_id=1, source_target_pairs={{0,12},{2,14},{4,8},{6,10},{8,4},{10,6},{12,0},{14,2},{16,28},{18,... | collective-permute-start | bytes 688136 | tf_op jit(solution)/shard_map/ppermute | solution.py:548
  67.4 10.8 %collective-permute-start.10 = (bf16[8,32,256]{2,1,0:T(8,128)(2,1)S(1)}, bf16[8,32,256]{2,1,0:T(8,128)(2,1)S(1)}, u32[]{:S(2)}, u32[]{:S(2)}) collective-permute-start(bf16[8,32,256]{2,1,0:T(8,128)(2,1)S(1)} %get-tuple-element.64), channel_id=1, source_target_pairs={{0,16},{2,18},{4,20},{6,22},{8,24},{10,26},{12,28},{14,30},{16,0},... | collective-permute-start | bytes 393224 | tf_op jit(solution)/shard_map/ppermute | solution.py:499
  73.8 6.5 %copy-start.9 = (bf16[2,32,1792]{2,1,0:T(8,128)(2,1)S(1)}, bf16[2,32,1792]{2,1,0:T(8,128)(2,1)}, u32[]{:S(2)}) copy-start(bf16[2,32,1792]{2,1,0:T(8,128)(2,1)} %copy-done.8) | copy-start | bytes 688132
  73.8 34.6 %all-to-all-start.2 = ((bf16[16,32,896]{2,1,0:T(8,128)(2,1)}), bf16[16,32,896]{2,1,0:T(8,128)(2,1)S(1)}, u32[]{:S(2)}, u32[]{:S(2)}) async-start(bf16[16,32,896]{2,1,0:T(8,128)(2,1)} %bitcast.3), calls=%async_computation.2 | async-start | bytes 1835008 | tf_op jit(solution)/shard_map/all_to_all | solution.py:565
  80.3 3.1 %copy-start.12 = (bf16[272,128]{1,0:T(8,128)(2,1)S(1)}, bf16[272,128]{1,0:T(8,128)(2,1)}, u32[]{:S(2)}) copy-start(bf16[272,128]{1,0:T(8,128)(2,1)} %copy-done.11) | copy-start | bytes 208900
  81.5 1.9 %collective-permute-start.11 = (bf16[4,32,1792]{2,1,0:T(8,128)(2,1)S(1)}, bf16[4,32,1792]{2,1,0:T(8,128)(2,1)S(1)}, u32[]{:S(2)}, u32[]{:S(2)}) collective-permute-start(bf16[4,32,1792]{2,1,0:T(8,128)(2,1)S(1)} %other_core_far.1), channel_id=1, source_target_pairs={{0,2},{2,0},{4,6},{6,4},{8,10},{10,8},{12,14},{14,12},{16,18},{18,... | collective-permute-start | bytes 1376264 | tf_op jit(solution)/shard_map/ppermute | solution.py:548
  87.9 2.5 %collective-permute-start.12 = (bf16[4,32,2304]{2,1,0:T(8,128)(2,1)S(1)}, bf16[4,32,2304]{2,1,0:T(8,128)(2,1)S(1)}, u32[]{:S(2)}, u32[]{:S(2)}) collective-permute-start(bf16[4,32,2304]{2,1,0:T(8,128)(2,1)S(1)} %get-tuple-element.78), channel_id=1, source_target_pairs={{0,2},{2,0},{4,6},{6,4},{8,10},{10,8},{12,14},{14,12},{16,18},{18,... | collective-permute-start | bytes 1769480 | tf_op jit(solution)/shard_map/ppermute | solution.py:548
  89.0 33.1 %collective-permute-start.16 = (bf16[128,1792]{1,0:T(8,128)(2,1)}, bf16[128,1792]{1,0:T(8,128)(2,1)}, u32[]{:S(2)}, u32[]{:S(2)}) collective-permute-start(bf16[128,1792]{1,0:T(8,128)(2,1)} %copy-done.10), channel_id=1, source_target_pairs={{0,16},{2,18},{4,20},{6,22},{8,24},{10,26},{12,28},{14,30},{16,0},... | collective-permute-start | bytes 1376264 | tf_op jit(solution)/shard_map/ppermute | solution.py:499
  91.5 30.6 %collective-permute-start.13 = (bf16[2,32,2304]{2,1,0:T(8,128)(2,1)}, bf16[2,32,2304]{2,1,0:T(8,128)(2,1)}, u32[]{:S(2)}, u32[]{:S(2)}) collective-permute-start(bf16[2,32,2304]{2,1,0:T(8,128)(2,1)} %get-tuple-element.80), channel_id=1, source_target_pairs={{0,4},{2,6},{4,0},{6,2},{8,12},{10,14},{12,8},{14,10},{16,20},{18,... | collective-permute-start | bytes 884744 | tf_op jit(solution)/shard_map/ppermute | solution.py:548
  92.9 29.2 %collective-permute-start.14 = (bf16[2,32,2304]{2,1,0:T(8,128)(2,1)}, bf16[2,32,2304]{2,1,0:T(8,128)(2,1)}, u32[]{:S(2)}, u32[]{:S(2)}) collective-permute-start(bf16[2,32,2304]{2,1,0:T(8,128)(2,1)} %get-tuple-element.81), channel_id=1, source_target_pairs={{0,8},{2,10},{4,12},{6,14},{8,0},{10,2},{12,4},{14,6},{16,24},{18,... | collective-permute-start | bytes 884744 | tf_op jit(solution)/shard_map/ppermute | solution.py:548
  94.9 27.7 %collective-permute-start.15 = (bf16[2,32,2304]{2,1,0:T(8,128)(2,1)}, bf16[2,32,2304]{2,1,0:T(8,128)(2,1)}, u32[]{:S(2)}, u32[]{:S(2)}) collective-permute-start(bf16[2,32,2304]{2,1,0:T(8,128)(2,1)} %get-tuple-element.82), channel_id=1, source_target_pairs={{0,12},{2,14},{4,8},{6,10},{8,4},{10,6},{12,0},{14,2},{16,28},{18,... | collective-permute-start | bytes 884744 | tf_op jit(solution)/shard_map/ppermute | solution.py:548
  110.0 7.2 %copy-start.6 = (bf16[272,128]{1,0:T(8,128)(2,1)S(1)}, bf16[272,128]{1,0:T(8,128)(2,1)}, u32[]{:S(2)}) copy-start(bf16[272,128]{1,0:T(8,128)(2,1)} %copy-done.5) | copy-start | bytes 208900
  110.0 31.8 %all-to-all-start.3 = ((bf16[32,16,896]{2,1,0:T(8,128)(2,1)}), bf16[32,16,896]{2,1,0:T(8,128)(2,1)}, u32[]{:S(2)}, u32[]{:S(2)}) async-start(bf16[32,16,896]{2,1,0:T(8,128)(2,1)} %route_steps.1), calls=%async_computation.3 | async-start | bytes 1835008 | tf_op jit(solution)/shard_map/all_to_all | solution.py:604
  124.2 5.3 %copy-start.1 = (bf16[128,512]{1,0:T(8,128)(2,1)S(1)}, bf16[128,512]{1,0:T(8,128)(2,1)}, u32[]{:S(2)}) copy-start(bf16[128,512]{1,0:T(8,128)(2,1)} %copy-done) | copy-start | bytes 393220
  124.2 5.3 %collective-permute-start.17 = (bf16[256,128]{1,0:T(8,128)(2,1)S(1)}, bf16[256,128]{1,0:T(8,128)(2,1)S(1)}, u32[]{:S(2)}, u32[]{:S(2)}) collective-permute-start(bf16[256,128]{1,0:T(8,128)(2,1)S(1)} %get-tuple-element.91), channel_id=1, source_target_pairs={{0,1},{1,0},{2,3},{3,2},{4,5},{5,4},{6,7},{7,6},{8,9},{9,8},{10,11... | collective-permute-start | bytes 196616 | tf_op jit(solution)/shard_map/ppermute | solution.py:502
  (6 other events, 5.1 us)

commit v5 on v4

--- a/solution.py
+++ b/solution.py
@@ -250,7 +250,8 @@
     by_token = (one_hot[:, :tok] + one_hot[:, tok:]).astype(bf16)
     rows = jnp.dot(by_token, grads, preferred_element_type=f32)
     out_ref[:, :, 0:wide] = (rows * factor).astype(bf16).reshape(bins, cap, wide)
-    for side, ref in enumerate((acts_ref, beside_ref)):
+    for side in range((out_ref.shape[2] - wide) // units):
+        ref = (acts_ref, beside_ref)[side]
         at = wide + side * units
         acts = jnp.dot(
             one_hot.astype(bf16), ref[0 : 2 * tok, :], preferred_element_type=f32
@@ -267,25 +268,29 @@
     return lax.rem(lax.axis_index("expert"), half)
 
 
-def output_rows(half, recv_ref, weight_ref, beside_ref, cap):
+def output_rows(half, recv_refs, weight_ref, beside_ref, cap):
     units, wide = weight_ref.shape[1:]
     me = place_in_half(half)
-    acts = jnp.concatenate([recv_ref[me ^ r, :, wide:] for r in range(half)], axis=0)
-    total = jnp.dot(acts[:, :units], weight_ref[0], preferred_element_type=f32)
-    total = total + jnp.dot(acts[:, units:], beside_ref[0], preferred_element_type=f32)
+    total = None
+    for ref, at, weight in zip(recv_refs, (wide, recv_refs[1].shape[2] - units), (weight_ref, beside_ref)):
+        acts = jnp.concatenate([ref[me ^ r, :, at : at + units] for r in range(half)], axis=0)
+        part = jnp.dot(acts, weight[0], preferred_element_type=f32)
+        total = part if total is None else total + part
     return total.astype(bf16).reshape(half // 2, 2, cap, wide)
 
 
 def forward_far_body(half, recv_ref, weight_ref, beside_ref, *refs):
     out_refs, grads_ref = refs[:-1], refs[-1]
     grad_rows_body(recv_ref, weight_ref, beside_ref, grads_ref)
-    total = output_rows(half, recv_ref, weight_ref, beside_ref, out_refs[0].shape[1])
+    total = output_rows(half, (recv_ref,) * 2, weight_ref, beside_ref, out_refs[0].shape[1])
     for distance, ref in enumerate(out_refs):
         ref[...] = total[distance]
 
 
-def forward_own_body(half, recv_ref, weight_ref, beside_ref, grads_ref, mirror_ref, *out_refs):
-    total = output_rows(half, recv_ref, weight_ref, beside_ref, out_refs[0].shape[1])
+def forward_own_body(half, recv_ref, acts_ref, weight_ref, beside_ref, grads_ref, mirror_ref, *out_refs):
+    total = output_rows(
+        half, (recv_ref, acts_ref), weight_ref, beside_ref, out_refs[0].shape[1]
+    )
     wide = total.shape[3]
     units = grads_ref.shape[2]
     me = place_in_half(half)
@@ -322,7 +327,7 @@
 
 
 def update_body(
-    recv_ref, far_ref, first_ref, second_ref, first_beside, second_beside, out_ref
+    recv_ref, acts_ref, far_ref, first_ref, second_ref, first_beside, second_beside, out_ref
 ):
     _, units, wide = first_beside.shape
     groups = out_ref.shape[0]
@@ -330,9 +335,10 @@
     each = units // groups
     for part in range(2):
         grads = None
-        for ref in (recv_ref, far_ref):
+        own = jnp.concatenate([rows_of(recv_ref, wide, units), rows_of(acts_ref, 0, units)], axis=1)
+        for ref, acts in ((recv_ref, own), (far_ref, rows_of(far_ref, wide, 2 * units))):
             more = lax.dot_general(
-                rows_of(ref, wide, 2 * units),
+                acts,
                 rows_of(ref, part * narrow, narrow),
                 (((0,), (0,)), ((), ())),
                 preferred_element_type=f32,
@@ -515,7 +521,6 @@
         prepare_body, (shaped(top * tok, units), shaped(top * tok + 16, units)), "prepare"
     )(acts, jnp.concatenate([expert_ids.astype(f32), route_weights], axis=1))
     noted_far = mirror(noted)
-    hidden_beside = neighbour(hidden)
     hidden_diagonal = lax.ppermute(hidden, ("expert", "hidden"), diagonal)
 
     split = whole_call(split_body, (shaped(1, units, wide),) * 2, "split_state")
@@ -527,21 +532,22 @@
     second_beside = neighbour(second_other)
 
     row = wide + 2 * units
-    pack = functools.partial(
-        whole_call, functools.partial(pack_body, half), shaped(half, cap, row)
-    )
-    packed = pack("pack_own")(noted, hidden_beside, grad_out)
+    pack = functools.partial(whole_call, functools.partial(pack_body, half))
+    packed = pack(shaped(half, cap, wide + units), "pack_own")(
+        after(noted, weight_other, first_other), hidden, grad_out
+    )
     recv = exchange(packed)
-
-    packed_far = pack("pack_far", moved=HEAVY)(noted_far, hidden_diagonal, *grads_far)
+    acts_beside = neighbour(recv[:, :, wide:])
+
+    packed_far = pack(shaped(half, cap, row), "pack_far", moved=HEAVY)(noted_far, hidden_diagonal, *grads_far)
     recv, packed_far, weight_beside, first_beside = lax.optimization_barrier(
         (recv, packed_far, weight_beside, first_beside)
     )
     recv_far = exchange(packed_far)
     grad_rows = whole_call(grad_rows_body, shaped(half, cap, 2 * units), "grad_rows")
     rows_own = grad_rows(recv, weight, weight_beside)
-    recv_far, second_beside, rows_own = lax.optimization_barrier(
-        (recv_far, second_beside, rows_own)
+    recv_far, second_beside, rows_own, acts_beside = lax.optimization_barrier(
+        (recv_far, second_beside, rows_own, acts_beside)
     )
 
     def at_distance(x, distance):
@@ -560,7 +566,7 @@
 
     rows_mirror = mirror(rows_send)
     steps = whole_call(update_body, shaped(half, 2, 2 * each, narrow), "update")(
-        recv, after(recv_far, rows_send), first, second, first_beside, second_beside
+        recv, acts_beside, after(recv_far, rows_send), first, second, first_beside, second_beside
     )
     spread = lax.all_to_all(
         steps.reshape(places, 2 * each, narrow),
@@ -583,7 +589,7 @@
         functools.partial(forward_own_body, half),
         (shaped(half // 2, cap, extended),) * 2,
         "forward_own",
-    )(after(recv, combined_send), weight, weight_beside, rows_own, rows_mirror)
+    )(after(recv, combined_send), acts_beside, weight, weight_beside, rows_own, rows_mirror)
     joined = whole_call(join_cores_body, (shaped(2, cap, extended),) * (half // 2), "join_cores")(
         keep_core, at_distance(send_core, 1)
     )

time: 145 us -> 144 us (level)
  waiting for transfers between devices: 64.6 us -> 62 us
    all_to_all x2, waiting for transfers between devices: 7.89 us -> 6.01 us  [exchange(): lax.all_to_all(x, 'expert', split_axis=0, concat_axis=0, tiled=True, axis...]
    unnamed x32 -> x28, local copies, waits for them, and re-layouts: 3.86 us -> 3.84 us
  transfers between devices with their start and end apart: 22 -> 22, of which waited for: 13 -> 12; matrix products, arithmetic and copies ran while one was open for 1% -> 2% of each run, Pallas kernels for 16% -> 16%
where the time goes in v5:
time: 144 us; the launch traced here: 143 us
  waiting for transfers between devices  62 us (43%)
  starting transfers between devices  45.9 us (32%)
  Pallas kernels  27.7 us (19%)
  local copies, waits for them, and re-layouts  6.7 us (5%)
    all_to_all x1, waiting for transfers between devices, mirrored_local(): lax.all_to_all(steps.reshape(places, 2 * each, narrow), 'expert', split_a...  12.4 us
    all_to_all x1, waiting for transfers between devices, mirrored_local(): lax.all_to_all(after(routed, combined_send), ('expert', 'hidden'), split_...  11.7 us
    ppermute x5, waiting for transfers between devices, neighbour(): return lax.ppermute(x, 'hidden', beside)  11.3 us
    ppermute x1, waiting for transfers between devices, mirrored_local(): hidden_diagonal = lax.ppermute(hidden, ('expert', 'hidden'), diagonal)  10.9 us
    ppermute x4, starting transfers between devices, mirror(): return lax.ppermute(x, 'expert', across)  9.42 us
    all_to_all x2, starting transfers between devices, exchange(): lax.all_to_all(x, 'expert', split_axis=0, concat_axis=0, tiled=True, axis...  7.78 us
    ppermute x8, starting transfers between devices, at_distance(): return lax.ppermute(x, 'expert', [(k, k ^ distance) for k in range(places)])  7.46 us
    all_to_all x1, starting transfers between devices, mirrored_local(): lax.all_to_all(after(routed, combined_send), ('expert', 'hidden'), split_...  6.81 us
  transfers between devices with their start and end apart: 22, of which 12 were waited for; matrix products, arithmetic and copies ran while one was open for 2% of the time, Pallas kernels for 16%

profile of v5, /device:TPU:0, one launch (start us, length us, event | category | flops | bytes accessed | tf_op | source)
XLA Modules:
  0.0 143.3 jit_solution(17659860077529003585)
XLA Ops:
  0.6 4.1 %collective-permute-start.2 = (bf16[128,1792]{1,0:T(8,128)(2,1)}, bf16[128,1792]{1,0:T(8,128)(2,1)S(1)}, u32[]{:S(2)}, u32[]{:S(2)}) collective-permute-start(bf16[128,1792]{1,0:T(8,128)(2,1)} %refs_0_.1), channel_id=1, source_target_pairs={{0,16},{2,18},{4,20},{6,22},{8,24},{10,26},{12,28},{14,30},{16,0},... | collective-permute-start | bytes 1376264 | tf_op jit(solution)/shard_map/ppermute | solution.py:505
  6.9 3.9 %collective-permute-start.1 = (bf16[256,128]{1,0:T(8,128)(2,1)S(1)}, bf16[256,128]{1,0:T(8,128)(2,1)S(1)}, u32[]{:S(2)}, u32[]{:S(2)}) collective-permute-start(bf16[256,128]{1,0:T(8,128)(2,1)S(1)} %get-tuple-element.52.beside_ref), channel_id=1, source_target_pairs={{0,17},{1,16},{2,19},{3,18},{4,21},{5,20},{6,23},{7,22},{8,25},{9,... | collective-permute-start | bytes 196616 | tf_op jit(solution)/shard_map/ppermute | solution.py:524
  14.1 1.5 %collective-permute-start.4 = (bf16[1,128,1792]{2,1,0:T(8,128)(2,1)}, bf16[1,128,1792]{2,1,0:T(8,128)(2,1)}, u32[]{:S(2)}, u32[]{:S(2)}) collective-permute-start(bf16[1,128,1792]{2,1,0:T(8,128)(2,1)} %get-tuple-element.54), channel_id=1, source_target_pairs={{0,1},{1,0},{2,3},{3,2},{4,5},{5,4},{6,7},{7,6},{8,9},{9,8},{10,11... | collective-permute-start | bytes 1376264 | tf_op jit(solution)/shard_map/ppermute | solution.py:508
  15.6 1.6 %pack_own.1 = bf16[8,32,1920]{2,1,0:T(8,128)(2,1)} custom-call(bf16[272,128]{1,0:T(8,128)(2,1)S(1)} %get-tuple-element.87.acts_ref.meta_ref, bf16[256,128]{1,0:T(8,128)(2,1)S(1)} %get-tuple-element.52.beside_ref, bf16[128,1792]{1,0:T(8,128)(2,1)S(1)} %copy-done.7), custom_call_target="tpu_custom_call" | custom-call | tf_op jit(solution)/shard_map/pack_own/pallas_call | solution.py:536
  17.2 4.2 %all-to-all-start = ((bf16[8,32,1920]{2,1,0:T(8,128)(2,1)}), bf16[8,32,1920]{2,1,0:T(8,128)(2,1)}, u32[]{:S(2)}, u32[]{:S(2)}) async-start(bf16[8,32,1920]{2,1,0:T(8,128)(2,1)} %pack_own.1), calls=%async_computation | async-start | bytes 1966080 | tf_op jit(solution)/shard_map/all_to_all | solution.py:511
  21.4 10.9 %collective-permute-done.1.beside_ref = bf16[256,128]{1,0:T(8,128)(2,1)S(1)} collective-permute-done((bf16[256,128]{1,0:T(8,128)(2,1)S(1)}, bf16[256,128]{1,0:T(8,128)(2,1)S(1)}, u32[]{:S(2)}, u32[]{:S(2)}) %collective-permute-start.1) | collective-permute-done | bytes 65568 | tf_op jit(solution)/shard_map/ppermute | solution.py:524
  32.3 1.7 %pack_far.1 = bf16[8,32,2048]{2,1,0:T(8,128)(2,1)} custom-call(bf16[272,128]{1,0:T(8,128)(2,1)S(1)} %collective-permute-done.acts_ref, bf16[256,128]{1,0:T(8,128)(2,1)S(1)} %collective-permute-done.1.beside_ref, bf16[128,1792]{1,0:T(8,128)(2,1)S(1)} %collective-permute-done.2.refs_0_), custom_call_target="tpu_custom_call" | custom-call | flops 999999995904 | bytes 10000000000 | tf_op jit(solution)/shard_map/pack_far/pallas_call | solution.py:542
  34.0 1.8 %collective-permute-done.4.first_beside = bf16[1,128,1792]{2,1,0:T(8,128)(2,1)} collective-permute-done((bf16[1,128,1792]{2,1,0:T(8,128)(2,1)}, bf16[1,128,1792]{2,1,0:T(8,128)(2,1)}, u32[]{:S(2)}, u32[]{:S(2)}) %collective-permute-start.4) | collective-permute-done | bytes 458784 | tf_op jit(solution)/shard_map/ppermute | solution.py:508
  35.7 6.0 %all-to-all-done.recv_ref = bf16[8,32,1920]{2,1,0:T(8,128)(2,1)} async-done(((bf16[8,32,1920]{2,1,0:T(8,128)(2,1)}), bf16[8,32,1920]{2,1,0:T(8,128)(2,1)}, u32[]{:S(2)}, u32[]{:S(2)}) %all-to-all-start) | async-done | bytes 983072 | tf_op jit(solution)/shard_map/all_to_all | solution.py:511
  41.7 3.6 %all-to-all-start.1 = ((bf16[8,32,2048]{2,1,0:T(8,128)(2,1)}), bf16[8,32,2048]{2,1,0:T(8,128)(2,1)S(1)}, u32[]{:S(2)}, u32[]{:S(2)}) async-start(bf16[8,32,2048]{2,1,0:T(8,128)(2,1)} %pack_far.1), calls=%async_computation.1 | async-start | bytes 2097152 | tf_op jit(solution)/shard_map/all_to_all | solution.py:511
  45.4 1.7 %collective-permute-start.5 = (bf16[1,128,1792]{2,1,0:T(8,128)(2,1)S(1)}, bf16[1,128,1792]{2,1,0:T(8,128)(2,1)S(1)}, u32[]{:S(2)}, u32[]{:S(2)}) collective-permute-start(bf16[1,128,1792]{2,1,0:T(8,128)(2,1)S(1)} %get-tuple-element.59), channel_id=1, source_target_pairs={{0,1},{1,0},{2,3},{3,2},{4,5},{5,4},{6,7},{7,6},{8,9},{9,8},{10,11... | collective-permute-start | bytes 1376264 | tf_op jit(solution)/shard_map/ppermute | solution.py:508
  48.3 1.9 %grad_rows.1.grads_ref = bf16[8,32,256]{2,1,0:T(8,128)(2,1)S(1)} custom-call(bf16[8,32,1920]{2,1,0:T(8,128)(2,1)} %all-to-all-done.recv_ref, bf16[1,128,1792]{2,1,0:T(8,128)(2,1)S(1)} %get-tuple-element.60.weight_ref, bf16[1,128,1792]{2,1,0:T(8,128)(2,1)} %collective-permute-done.3.beside_ref), custom_call_target="tpu_custom_call" | custom-call | tf_op jit(solution)/shard_map/grad_rows/pallas_call | solution.py:548
  50.3 8.5 %collective-permute-done.5.second_beside = bf16[1,128,1792]{2,1,0:T(8,128)(2,1)S(1)} collective-permute-done((bf16[1,128,1792]{2,1,0:T(8,128)(2,1)S(1)}, bf16[1,128,1792]{2,1,0:T(8,128)(2,1)S(1)}, u32[]{:S(2)}, u32[]{:S(2)}) %collective-permute-start.5) | collective-permute-done | bytes 458784 | tf_op jit(solution)/shard_map/ppermute | solution.py:508
  59.7 3.0 %forward_far.1 = (bf16[2,32,1792]{2,1,0:T(8,128)(2,1)S(1)}, bf16[2,32,1792]{2,1,0:T(8,128)(2,1)}, bf16[2,32,1792]{2,1,0:T(8,128)(2,1)}, bf16[2,32,1792]{2,1,0:T(8,128)(2,1)}, bf16[8,32,256]{2,1,0:T(8,128)(2,1)S(1)}) custom-call(bf16[8,32,2048]{2,1,0:T(8,128)(2,1)S(1)} %all-to-all-done.1.recv_ref.far_ref, ...), custom_call_target="tpu_custom_call" | custom-call | tf_op jit(solution)/shard_map/forward_far/pallas_call | solution.py:561
  63.3 1.7 %collective-permute-start.7 = (bf16[2,32,1792]{2,1,0:T(8,128)(2,1)}, bf16[2,32,1792]{2,1,0:T(8,128)(2,1)}, u32[]{:S(2)}, u32[]{:S(2)}) collective-permute-start(bf16[2,32,1792]{2,1,0:T(8,128)(2,1)} %get-tuple-element.64), channel_id=1, source_target_pairs={{0,4},{2,6},{4,0},{6,2},{8,12},{10,14},{12,8},{14,10},{16,20},{18,... | collective-permute-start | bytes 688136 | tf_op jit(solution)/shard_map/ppermute | solution.py:554
  66.8 2.8 %collective-permute-start.10 = (bf16[8,32,256]{2,1,0:T(8,128)(2,1)S(1)}, bf16[8,32,256]{2,1,0:T(8,128)(2,1)S(1)}, u32[]{:S(2)}, u32[]{:S(2)}) collective-permute-start(bf16[8,32,256]{2,1,0:T(8,128)(2,1)S(1)} %get-tuple-element.67), channel_id=1, source_target_pairs={{0,16},{2,18},{4,20},{6,22},{8,24},{10,26},{12,28},{14,30},{16,0},... | collective-permute-start | bytes 393224 | tf_op jit(solution)/shard_map/ppermute | solution.py:505
  69.7 3.5 %update.1 = bf16[8,2,32,896]{3,2,1,0:T(8,128)(2,1)} custom-call(bf16[8,32,1920]{2,1,0:T(8,128)(2,1)} %all-to-all-done.recv_ref, bf16[8,32,128]{2,1,0:T(8,128)(2,1)S(1)} %collective-permute-done.6.acts_ref, bf16[8,32,2048]{2,1,0:T(8,128)(2,1)S(1)} %all-to-all-done.1.recv_ref.far_ref, bf16[1,128,1792]{2,1,0:T(8,128)(2,1)S(1)} %get-tuple-element.70.first_ref, ...), custom_call_target="tpu_custom_call" | custom-call | tf_op jit(solution)/shard_map/update/pallas_call | solution.py:568
  73.2 4.1 %all-to-all-start.2 = ((bf16[16,32,896]{2,1,0:T(8,128)(2,1)}), bf16[16,32,896]{2,1,0:T(8,128)(2,1)S(1)}, u32[]{:S(2)}, u32[]{:S(2)}) async-start(bf16[16,32,896]{2,1,0:T(8,128)(2,1)} %bitcast.3), calls=%async_computation.2 | async-start | bytes 1835008 | tf_op jit(solution)/shard_map/all_to_all | solution.py:571
  81.0 1.8 %collective-permute-done.11.refs_4_ = bf16[4,32,1792]{2,1,0:T(8,128)(2,1)S(1)} collective-permute-done((bf16[4,32,1792]{2,1,0:T(8,128)(2,1)S(1)}, bf16[4,32,1792]{2,1,0:T(8,128)(2,1)S(1)}, u32[]{:S(2)}, u32[]{:S(2)}) %collective-permute-start.11) | collective-permute-done | bytes 458784 | tf_op jit(solution)/shard_map/ppermute | solution.py:554
  82.8 1.8 %combine_far.1 = bf16[128,1792]{1,0:T(8,128)(2,1)S(1)} custom-call(bf16[272,128]{1,0:T(8,128)(2,1)S(1)} %collective-permute-done.acts_ref, bf16[2,32,1792]{2,1,0:T(8,128)(2,1)S(1)} %copy-done.9, bf16[2,32,1792]{2,1,0:T(8,128)(2,1)} %collective-permute-done.7.refs_1_, bf16[2,32,1792]{2,1,0:T(8,128)(2,1)} %collective-permute-done.8.refs_2_, ...), custom_call_target="tpu_custom_call" | custom-call | flops 5500000256 | bytes 55000000 | tf_op jit(solution)/shard_map/combine_far/pallas_call | solution.py:584
  85.3 1.9 %forward_own.1 = (bf16[4,32,2304]{2,1,0:T(8,128)(2,1)S(1)}, bf16[4,32,2304]{2,1,0:T(8,128)(2,1)S(1)}) custom-call(bf16[8,32,1920]{2,1,0:T(8,128)(2,1)} %all-to-all-done.recv_ref, bf16[8,32,128]{2,1,0:T(8,128)(2,1)S(1)} %collective-permute-done.6.acts_ref, bf16[1,128,1792]{2,1,0:T(8,128)(2,1)S(1)} %get-tuple-element.60.weight_ref, ...), custom_call_target="tpu_custom_call" | custom-call | tf_op jit(solution)/shard_map/forward_own/pallas_call | solution.py:588
  88.3 2.4 %collective-permute-start.16 = (bf16[128,1792]{1,0:T(8,128)(2,1)}, bf16[128,1792]{1,0:T(8,128)(2,1)}, u32[]{:S(2)}, u32[]{:S(2)}) collective-permute-start(bf16[128,1792]{1,0:T(8,128)(2,1)} %copy-done.10), channel_id=1, source_target_pairs={{0,16},{2,18},{4,20},{6,22},{8,24},{10,26},{12,28},{14,30},{16,0},... | collective-permute-start | bytes 1376264 | tf_op jit(solution)/shard_map/ppermute | solution.py:505
  92.3 3.1 %collective-permute-start.14 = (bf16[2,32,2304]{2,1,0:T(8,128)(2,1)}, bf16[2,32,2304]{2,1,0:T(8,128)(2,1)}, u32[]{:S(2)}, u32[]{:S(2)}) collective-permute-start(bf16[2,32,2304]{2,1,0:T(8,128)(2,1)} %get-tuple-element.85), channel_id=1, source_target_pairs={{0,8},{2,10},{4,12},{6,14},{8,0},{10,2},{12,4},{14,6},{16,24},{18,... | collective-permute-start | bytes 884744 | tf_op jit(solution)/shard_map/ppermute | solution.py:554
  95.4 12.4 %all-to-all-done.2.recv_ref = bf16[16,32,896]{2,1,0:T(8,128)(2,1)S(1)} async-done(((bf16[16,32,896]{2,1,0:T(8,128)(2,1)}), bf16[16,32,896]{2,1,0:T(8,128)(2,1)S(1)}, u32[]{:S(2)}, u32[]{:S(2)}) %all-to-all-start.2) | async-done | bytes 917536 | tf_op jit(solution)/shard_map/all_to_all | solution.py:571
  107.8 1.6 %route_steps.1 = bf16[32,16,896]{2,1,0:T(8,128)(2,1)} custom-call(s32[32]{0:T(128)S(1)} %reshape.26.source_ref, s32[32]{0:T(128)S(1)} %xor.10.line_ref, bf16[16,32,896]{2,1,0:T(8,128)(2,1)S(1)} %all-to-all-done.2.recv_ref), custom_call_target="tpu_custom_call" | custom-call | tf_op jit(solution)/shard_map/route_steps/pallas_call | solution.py:602
  109.4 6.8 %all-to-all-start.3 = ((bf16[32,16,896]{2,1,0:T(8,128)(2,1)}), bf16[32,16,896]{2,1,0:T(8,128)(2,1)}, u32[]{:S(2)}, u32[]{:S(2)}) async-start(bf16[32,16,896]{2,1,0:T(8,128)(2,1)} %route_steps.1), calls=%async_computation.3 | async-start | bytes 1835008 | tf_op jit(solution)/shard_map/all_to_all | solution.py:610
  116.4 5.4 %collective-permute-done.16.far_ref = bf16[128,1792]{1,0:T(8,128)(2,1)} collective-permute-done((bf16[128,1792]{1,0:T(8,128)(2,1)}, bf16[128,1792]{1,0:T(8,128)(2,1)}, u32[]{:S(2)}, u32[]{:S(2)}) %collective-permute-start.16) | collective-permute-done | bytes 458784 | tf_op jit(solution)/shard_map/ppermute | solution.py:505
  121.8 1.6 %pick_grads.1 = (f32[256,128]{1,0:T(8,128)S(1)}, bf16[256,128]{1,0:T(8,128)(2,1)S(1)}) custom-call(bf16[272,128]{1,0:T(8,128)(2,1)S(1)} %copy-done.6, bf16[2,32,2304]{2,1,0:T(8,128)(2,1)S(1)} %get-tuple-element.90.refs_0_, bf16[2,32,2304]{2,1,0:T(8,128)(2,1)} %collective-permute-done.13.refs_1_, bf16[2,32,2304]{2,1,0:T(8,128)(2,1)} %collective-permute-done.14.refs_2_, ...), custom_call_target="tpu_custom_call" | custom-call | tf_op jit(solution)/shard_map/pick_grads/pallas_call | solution.py:618
  123.5 2.4 %collective-permute-start.17 = (bf16[256,128]{1,0:T(8,128)(2,1)S(1)}, bf16[256,128]{1,0:T(8,128)(2,1)S(1)}, u32[]{:S(2)}, u32[]{:S(2)}) collective-permute-start(bf16[256,128]{1,0:T(8,128)(2,1)S(1)} %get-tuple-element.95), channel_id=1, source_target_pairs={{0,1},{1,0},{2,3},{3,2},{4,5},{5,4},{6,7},{7,6},{8,9},{9,8},{10,11... | collective-permute-start | bytes 196616 | tf_op jit(solution)/shard_map/ppermute | solution.py:508
  125.9 2.5 %combine_own.1 = bf16[128,1792]{1,0:T(8,128)(2,1)} custom-call(bf16[272,128]{1,0:T(8,128)(2,1)S(1)} %copy-done.6, bf16[256,256]{1,0:T(8,128)(2,1)S(1)} %choose.1.chosen_ref, bf16[128,1792]{1,0:T(8,128)(2,1)} %collective-permute-done.16.far_ref, bf16[2,32,2304]{2,1,0:T(8,128)(2,1)S(1)} %get-tuple-element.90.refs_0_, ...), custom_call_target="tpu_custom_call" | custom-call | tf_op jit(solution)/shard_map/combine_own/pallas_call | solution.py:626
  129.4 11.7 %all-to-all-done.3 = bf16[32,16,896]{2,1,0:T(8,128)(2,1)} async-done(((bf16[32,16,896]{2,1,0:T(8,128)(2,1)}), bf16[32,16,896]{2,1,0:T(8,128)(2,1)}, u32[]{:S(2)}, u32[]{:S(2)}) %all-to-all-start.3) | async-done | bytes 917536 | tf_op jit(solution)/shard_map/all_to_all | solution.py:610
  141.1 2.2 %place_steps.1 = bf16[128,3584]{1,0:T(8,128)(2,1)} custom-call(bf16[8,2,2,16,896]{4,3,2,1,0:T(8,128)(2,1)} %bitcast.6.recv_ref), custom_call_target="tpu_custom_call" | custom-call | tf_op jit(solution)/shard_map/place_steps/pallas_call | solution.py:629
  (72 shorter events, 18.5 us)
Async XLA Ops:
  0.6 5.1 %copy-start.11 = (s32[128,2]{0,1:T(2,128)S(1)}, s32[128,2]{0,1:T(2,128)}, u32[]{:S(2)}) copy-start(s32[128,2]{0,1:T(2,128)} %param.9) | copy-start | bytes 3076
  0.6 31.7 %collective-permute-start.2 = (bf16[128,1792]{1,0:T(8,128)(2,1)}, bf16[128,1792]{1,0:T(8,128)(2,1)S(1)}, u32[]{:S(2)}, u32[]{:S(2)}) collective-permute-start(bf16[128,1792]{1,0:T(8,128)(2,1)} %refs_0_.1), channel_id=1, source_target_pairs={{0,16},{2,18},{4,20},{6,22},{8,24},{10,26},{12,28},{14,30},{16,0},... | collective-permute-start | bytes 1376264 | tf_op jit(solution)/shard_map/ppermute | solution.py:505
  5.7 1.1 copy-start
  6.8 8.8 %copy-start.5 = (bf16[272,128]{1,0:T(8,128)(2,1)}, bf16[272,128]{1,0:T(8,128)(2,1)S(1)}, u32[]{:S(2)}) copy-start(bf16[272,128]{1,0:T(8,128)(2,1)S(1)} %get-tuple-element.87.acts_ref.meta_ref) | copy-start | bytes 208900
  6.8 25.5 %collective-permute-start = (bf16[272,128]{1,0:T(8,128)(2,1)S(1)}, bf16[272,128]{1,0:T(8,128)(2,1)S(1)}, u32[]{:S(2)}, u32[]{:S(2)}) collective-permute-start(bf16[272,128]{1,0:T(8,128)(2,1)S(1)} %get-tuple-element.87.acts_ref.meta_ref), channel_id=1, source_target_pairs={{0,16},{2,18},{4,20},{6,22},{8,24},{10,26},{12,28},{14,30},{16,0},... | collective-permute-start | bytes 208904 | tf_op jit(solution)/shard_map/ppermute | solution.py:505
  6.9 25.4 %collective-permute-start.1 = (bf16[256,128]{1,0:T(8,128)(2,1)S(1)}, bf16[256,128]{1,0:T(8,128)(2,1)S(1)}, u32[]{:S(2)}, u32[]{:S(2)}) collective-permute-start(bf16[256,128]{1,0:T(8,128)(2,1)S(1)} %get-tuple-element.52.beside_ref), channel_id=1, source_target_pairs={{0,17},{1,16},{2,19},{3,18},{4,21},{5,20},{6,23},{7,22},{8,25},{9,... | collective-permute-start | bytes 196616 | tf_op jit(solution)/shard_map/ppermute | solution.py:524
  10.8 1.2 copy-start.2
  11.9 1.3 copy-start.3
  12.8 21.2 %collective-permute-start.3 = (bf16[1,128,1792]{2,1,0:T(8,128)(2,1)}, bf16[1,128,1792]{2,1,0:T(8,128)(2,1)}, u32[]{:S(2)}, u32[]{:S(2)}) collective-permute-start(bf16[1,128,1792]{2,1,0:T(8,128)(2,1)} %get-tuple-element.51), channel_id=1, source_target_pairs={{0,1},{1,0},{2,3},{3,2},{4,5},{5,4},{6,7},{7,6},{8,9},{9,8},{10,11... | collective-permute-start | bytes 1376264 | tf_op jit(solution)/shard_map/ppermute | solution.py:508
  13.3 2.3 %copy-start.7 = (bf16[128,1792]{1,0:T(8,128)(2,1)S(1)}, bf16[128,1792]{1,0:T(8,128)(2,1)}, u32[]{:S(2)}) copy-start(bf16[128,1792]{1,0:T(8,128)(2,1)} %refs_0_.1) | copy-start | bytes 1376260
  14.1 21.6 %collective-permute-start.4 = (bf16[1,128,1792]{2,1,0:T(8,128)(2,1)}, bf16[1,128,1792]{2,1,0:T(8,128)(2,1)}, u32[]{:S(2)}, u32[]{:S(2)}) collective-permute-start(bf16[1,128,1792]{2,1,0:T(8,128)(2,1)} %get-tuple-element.54), channel_id=1, source_target_pairs={{0,1},{1,0},{2,3},{3,2},{4,5},{5,4},{6,7},{7,6},{8,9},{9,8},{10,11... | collective-permute-start | bytes 1376264 | tf_op jit(solution)/shard_map/ppermute | solution.py:508
  17.2 24.5 %all-to-all-start = ((bf16[8,32,1920]{2,1,0:T(8,128)(2,1)}), bf16[8,32,1920]{2,1,0:T(8,128)(2,1)}, u32[]{:S(2)}, u32[]{:S(2)}) async-start(bf16[8,32,1920]{2,1,0:T(8,128)(2,1)} %pack_own.1), calls=%async_computation | async-start | bytes 1966080 | tf_op jit(solution)/shard_map/all_to_all | solution.py:511
  34.0 11.3 %copy-start.4 = (bf16[1,128,3584]{2,1,0:T(8,128)(2,1)S(1)}, bf16[1,128,3584]{2,1,0:T(8,128)(2,1)}, u32[]{:S(2)}) copy-start(bf16[1,128,3584]{2,1,0:T(8,128)(2,1)} %param.15) | copy-start | bytes 2752516
  41.7 17.9 %all-to-all-start.1 = ((bf16[8,32,2048]{2,1,0:T(8,128)(2,1)}), bf16[8,32,2048]{2,1,0:T(8,128)(2,1)S(1)}, u32[]{:S(2)}, u32[]{:S(2)}) async-start(bf16[8,32,2048]{2,1,0:T(8,128)(2,1)} %pack_far.1), calls=%async_computation.1 | async-start | bytes 2097152 | tf_op jit(solution)/shard_map/all_to_all | solution.py:511
  45.4 13.4 %collective-permute-start.5 = (bf16[1,128,1792]{2,1,0:T(8,128)(2,1)S(1)}, bf16[1,128,1792]{2,1,0:T(8,128)(2,1)S(1)}, u32[]{:S(2)}, u32[]{:S(2)}) collective-permute-start(bf16[1,128,1792]{2,1,0:T(8,128)(2,1)S(1)} %get-tuple-element.59), channel_id=1, source_target_pairs={{0,1},{1,0},{2,3},{3,2},{4,5},{5,4},{6,7},{7,6},{8,9},{9,8},{10,11... | collective-permute-start | bytes 1376264 | tf_op jit(solution)/shard_map/ppermute | solution.py:508
  47.9 11.8 %collective-permute-start.6 = (bf16[8,32,128]{2,1,0:T(8,128)(2,1)S(1)}, bf16[8,32,128]{2,1,0:T(8,128)(2,1)S(1)}, u32[]{:S(2)}, u32[]{:S(2)}) collective-permute-start(bf16[8,32,128]{2,1,0:T(8,128)(2,1)S(1)} %slice.12), channel_id=1, source_target_pairs={{0,1},{1,0},{2,3},{3,2},{4,5},{5,4},{6,7},{7,6},{8,9},{9,8},{10,11... | collective-permute-start | bytes 196616 | tf_op jit(solution)/shard_map/ppermute | solution.py:508
  63.3 15.3 %collective-permute-start.7 = (bf16[2,32,1792]{2,1,0:T(8,128)(2,1)}, bf16[2,32,1792]{2,1,0:T(8,128)(2,1)}, u32[]{:S(2)}, u32[]{:S(2)}) collective-permute-start(bf16[2,32,1792]{2,1,0:T(8,128)(2,1)} %get-tuple-element.64), channel_id=1, source_target_pairs={{0,4},{2,6},{4,0},{6,2},{8,12},{10,14},{12,8},{14,10},{16,20},{18,... | collective-permute-start | bytes 688136 | tf_op jit(solution)/shard_map/ppermute | solution.py:554
  65.0 13.7 %collective-permute-start.8 = (bf16[2,32,1792]{2,1,0:T(8,128)(2,1)}, bf16[2,32,1792]{2,1,0:T(8,128)(2,1)}, u32[]{:S(2)}, u32[]{:S(2)}) collective-permute-start(bf16[2,32,1792]{2,1,0:T(8,128)(2,1)} %get-tuple-element.65), channel_id=1, source_target_pairs={{0,8},{2,10},{4,12},{6,14},{8,0},{10,2},{12,4},{14,6},{16,24},{18,... | collective-permute-start | bytes 688136 | tf_op jit(solution)/shard_map/ppermute | solution.py:554
  66.5 13.2 %collective-permute-start.9 = (bf16[2,32,1792]{2,1,0:T(8,128)(2,1)}, bf16[2,32,1792]{2,1,0:T(8,128)(2,1)}, u32[]{:S(2)}, u32[]{:S(2)}) collective-permute-start(bf16[2,32,1792]{2,1,0:T(8,128)(2,1)} %get-tuple-element.66), channel_id=1, source_target_pairs={{0,12},{2,14},{4,8},{6,10},{8,4},{10,6},{12,0},{14,2},{16,28},{18,... | collective-permute-start | bytes 688136 | tf_op jit(solution)/shard_map/ppermute | solution.py:554
  66.8 11.8 %collective-permute-start.10 = (bf16[8,32,256]{2,1,0:T(8,128)(2,1)S(1)}, bf16[8,32,256]{2,1,0:T(8,128)(2,1)S(1)}, u32[]{:S(2)}, u32[]{:S(2)}) collective-permute-start(bf16[8,32,256]{2,1,0:T(8,128)(2,1)S(1)} %get-tuple-element.67), channel_id=1, source_target_pairs={{0,16},{2,18},{4,20},{6,22},{8,24},{10,26},{12,28},{14,30},{16,0},... | collective-permute-start | bytes 393224 | tf_op jit(solution)/shard_map/ppermute | solution.py:505
  73.2 6.5 %copy-start.9 = (bf16[2,32,1792]{2,1,0:T(8,128)(2,1)S(1)}, bf16[2,32,1792]{2,1,0:T(8,128)(2,1)}, u32[]{:S(2)}) copy-start(bf16[2,32,1792]{2,1,0:T(8,128)(2,1)} %copy-done.8) | copy-start | bytes 688132
  73.2 34.6 %all-to-all-start.2 = ((bf16[16,32,896]{2,1,0:T(8,128)(2,1)}), bf16[16,32,896]{2,1,0:T(8,128)(2,1)S(1)}, u32[]{:S(2)}, u32[]{:S(2)}) async-start(bf16[16,32,896]{2,1,0:T(8,128)(2,1)} %bitcast.3), calls=%async_computation.2 | async-start | bytes 1835008 | tf_op jit(solution)/shard_map/all_to_all | solution.py:571
  80.9 1.9 %collective-permute-start.11 = (bf16[4,32,1792]{2,1,0:T(8,128)(2,1)S(1)}, bf16[4,32,1792]{2,1,0:T(8,128)(2,1)S(1)}, u32[]{:S(2)}, u32[]{:S(2)}) collective-permute-start(bf16[4,32,1792]{2,1,0:T(8,128)(2,1)S(1)} %other_core_far.1), channel_id=1, source_target_pairs={{0,2},{2,0},{4,6},{6,4},{8,10},{10,8},{12,14},{14,12},{16,18},{18,... | collective-permute-start | bytes 1376264 | tf_op jit(solution)/shard_map/ppermute | solution.py:554
  87.3 3.4 %collective-permute-start.12 = (bf16[4,32,2304]{2,1,0:T(8,128)(2,1)S(1)}, bf16[4,32,2304]{2,1,0:T(8,128)(2,1)S(1)}, u32[]{:S(2)}, u32[]{:S(2)}) collective-permute-start(bf16[4,32,2304]{2,1,0:T(8,128)(2,1)S(1)} %get-tuple-element.82), channel_id=1, source_target_pairs={{0,2},{2,0},{4,6},{6,4},{8,10},{10,8},{12,14},{14,12},{16,18},{18,... | collective-permute-start | bytes 1769480 | tf_op jit(solution)/shard_map/ppermute | solution.py:554
  88.3 33.5 %collective-permute-start.16 = (bf16[128,1792]{1,0:T(8,128)(2,1)}, bf16[128,1792]{1,0:T(8,128)(2,1)}, u32[]{:S(2)}, u32[]{:S(2)}) collective-permute-start(bf16[128,1792]{1,0:T(8,128)(2,1)} %copy-done.10), channel_id=1, source_target_pairs={{0,16},{2,18},{4,20},{6,22},{8,24},{10,26},{12,28},{14,30},{16,0},... | collective-permute-start | bytes 1376264 | tf_op jit(solution)/shard_map/ppermute | solution.py:505
  91.7 30.1 %collective-permute-start.13 = (bf16[2,32,2304]{2,1,0:T(8,128)(2,1)}, bf16[2,32,2304]{2,1,0:T(8,128)(2,1)}, u32[]{:S(2)}, u32[]{:S(2)}) collective-permute-start(bf16[2,32,2304]{2,1,0:T(8,128)(2,1)} %get-tuple-element.84), channel_id=1, source_target_pairs={{0,4},{2,6},{4,0},{6,2},{8,12},{10,14},{12,8},{14,10},{16,20},{18,... | collective-permute-start | bytes 884744 | tf_op jit(solution)/shard_map/ppermute | solution.py:554
  92.3 29.5 %collective-permute-start.14 = (bf16[2,32,2304]{2,1,0:T(8,128)(2,1)}, bf16[2,32,2304]{2,1,0:T(8,128)(2,1)}, u32[]{:S(2)}, u32[]{:S(2)}) collective-permute-start(bf16[2,32,2304]{2,1,0:T(8,128)(2,1)} %get-tuple-element.85), channel_id=1, source_target_pairs={{0,8},{2,10},{4,12},{6,14},{8,0},{10,2},{12,4},{14,6},{16,24},{18,... | collective-permute-start | bytes 884744 | tf_op jit(solution)/shard_map/ppermute | solution.py:554
  95.4 26.4 %collective-permute-start.15 = (bf16[2,32,2304]{2,1,0:T(8,128)(2,1)}, bf16[2,32,2304]{2,1,0:T(8,128)(2,1)}, u32[]{:S(2)}, u32[]{:S(2)}) collective-permute-start(bf16[2,32,2304]{2,1,0:T(8,128)(2,1)} %get-tuple-element.86), channel_id=1, source_target_pairs={{0,12},{2,14},{4,8},{6,10},{8,4},{10,6},{12,0},{14,2},{16,28},{18,... | collective-permute-start | bytes 884744 | tf_op jit(solution)/shard_map/ppermute | solution.py:554
  109.4 6.8 %copy-start.6 = (bf16[272,128]{1,0:T(8,128)(2,1)S(1)}, bf16[272,128]{1,0:T(8,128)(2,1)}, u32[]{:S(2)}) copy-start(bf16[272,128]{1,0:T(8,128)(2,1)} %copy-done.5) | copy-start | bytes 208900
  109.4 31.8 %all-to-all-start.3 = ((bf16[32,16,896]{2,1,0:T(8,128)(2,1)}), bf16[32,16,896]{2,1,0:T(8,128)(2,1)}, u32[]{:S(2)}, u32[]{:S(2)}) async-start(bf16[32,16,896]{2,1,0:T(8,128)(2,1)} %route_steps.1), calls=%async_computation.3 | async-start | bytes 1835008 | tf_op jit(solution)/shard_map/all_to_all | solution.py:610
  123.5 5.1 %copy-start.1 = (bf16[128,512]{1,0:T(8,128)(2,1)S(1)}, bf16[128,512]{1,0:T(8,128)(2,1)}, u32[]{:S(2)}) copy-start(bf16[128,512]{1,0:T(8,128)(2,1)} %copy-done) | copy-start | bytes 393220
  123.5 5.1 %collective-permute-start.17 = (bf16[256,128]{1,0:T(8,128)(2,1)S(1)}, bf16[256,128]{1,0:T(8,128)(2,1)S(1)}, u32[]{:S(2)}, u32[]{:S(2)}) collective-permute-start(bf16[256,128]{1,0:T(8,128)(2,1)S(1)} %get-tuple-element.95), channel_id=1, source_target_pairs={{0,1},{1,0},{2,3},{3,2},{4,5},{5,4},{6,7},{7,6},{8,9},{9,8},{10,11... | collective-permute-start | bytes 196616 | tf_op jit(solution)/shard_map/ppermute | solution.py:508
  (4 other events, 2.8 us)
